TPU v7x, 32 devices: a whole 2x2x4 slice. The times are simulated.
32 devices in a mesh: beams: 2 (over y), freq: 4 (over z), tm: 2 (over x), sub: 2 (over core).
Axes of the slice: x: 2, y: 2, z: 4, core: 2. Of those that a mesh axis runs over, the one named last changes fastest.
Arguments:
- filterbank: bfloat16 [1024, 4096], P(('beams', 'freq', 'sub'), 'tm'), parts along dimension 0, may hold values from -8 to 8
- delay_shifts: int32 [9, 512], replicated, may hold values from 0 to 256, as said below
- pulse_filters: bfloat16 [6, 256], replicated, may hold values from -0.375 to 0.375
Outputs:
- dedispersed: float32 [1024, 4096], P(('beams', 'freq', 'sub'), 'tm'), parts along dimension 0
There are 2 independent parts, one for each index of `beams`. A program takes and returns all parts, laid end to end along the dimension named above; an argument that names none is the same for every part. Nothing has to cross between parts.
Inputs may be any that keep to these rules, and one draw needn't show every extreme that they name: `delay_shifts`: at level l every shift lies in 0 to 2^l; trial 0 of every subband has shift 0 and its last trial shift 2^l.
All inputs are finite; a program needn't handle non-finite values.
Results may differ from a plain program's by a relative error of at most 0.0035.
Values may be sent and summed in bfloat16 or wider, within the bound.
No kernel may reach another device: no remote copies, remote signals or barrier semaphores. Data moves between devices by JAX's collectives and lax.ppermute only.
A program may use at most 64 MiB of HBM per device.

v0:
```python
import functools
import math

import jax
import jax.numpy as jnp
from jax import lax
from jax.experimental import pallas as pl
from jax.experimental.pallas import tpu as pltpu
from jax.sharding import PartitionSpec as P

LANES = 128
SUBLANES = 8
PACKED = 16
VMEM_LIMIT = 48 * 2**20


def rounded_up(value, unit):
    return -(-value // unit) * unit


def reversed_bits(value, bit_count):
    result = 0
    for bit_num in range(bit_count):
        result = result | (value >> bit_num & 1) << bit_count - 1 - bit_num
    return result


def bits_of(count):
    return count.bit_length() - 1


def from_ahead(value, steps, crossed):
    count, cores = lax.axis_size("tm"), lax.axis_size("sub")
    route = [
        ((block + steps) * cores + core, block * cores + (core ^ crossed))
        for block in range(count - steps)
        for core in range(cores)
    ]
    return lax.ppermute(value, ("tm", "sub"), route)


def from_partner(value, axis, mask):
    count = lax.axis_size(axis)
    return lax.ppermute(value, axis, [(source, source ^ mask) for source in range(count)])


def delayed(source, start, tiles, amount, most):
    whole, part = (0, amount) if most < LANES else (amount >> bits_of(LANES), amount & LANES - 1)
    first = source[pl.ds(start + whole, tiles), :]
    second = source[pl.ds(start + whole + 1, tiles), :]
    lane = lax.broadcasted_iota(jnp.int32, first.shape, 1)
    mixed = jnp.where(lane >= part, first, second)
    return pltpu.roll(mixed, LANES - part & LANES - 1, 1)


def merge(source, target, low, high, out, tiles, amounts, most):
    lower = source[pl.ds(low, tiles), :]
    for amount, place in zip(amounts, out):
        target[pl.ds(place, tiles), :] = lower + delayed(source, high, tiles, amount, most)


def chip_kernel(spans, tile_count, out_tiles, group_count, shifts, *refs):
    pieces = (refs[: len(spans)], refs[len(spans) : 2 * len(spans)])
    blocks = refs[2 * len(spans) : 2 * len(spans) + group_count]
    ping, pong = refs[2 * len(spans) + group_count :]
    chan_rows = pieces[0][0].shape[0]
    step = rounded_up(tile_count, SUBLANES)
    chip = lax.axis_index("freq")
    core = lax.axis_index("sub")
    for side in range(2):
        for first_row in range(0, chan_rows, PACKED):
            tile = 0
            for piece, (column, length) in zip(pieces[side], spans):
                for start in range(column, column + length, LANES):
                    part = piece[first_row : first_row + PACKED, start : start + LANES].astype(jnp.float32)
                    for half in range(0, PACKED, SUBLANES):
                        row = side * chan_rows + first_row + half
                        ping[pl.ds(row * step + tile, SUBLANES, stride=step), :] = part[half : half + SUBLANES]
                    tile += 1
            for later in range(tile, tile_count):
                for half in range(0, PACKED, SUBLANES):
                    row = side * chan_rows + first_row + half
                    ping[pl.ds(row * step + later, SUBLANES, stride=step), :] = jnp.zeros(
                        (SUBLANES, LANES), jnp.float32
                    )
    source, target = ping, pong
    local_count = bits_of(chan_rows)
    place = chip * 2 * chan_rows
    for level in range(local_count):
        width = 2**level
        for side in range(2):
            for subband in range(chan_rows // (2 * width)):
                band = (side * chan_rows) // (2 * width) + subband
                table = place + (core ^ side) * chan_rows + subband * 2 * width + core * width
                for pair in range(max(width // 2, 1)):
                    rows = range(band * width + 2 * pair, band * width + min(2 * pair + 2, width))
                    held = max(width // 2, 1)
                    merge(
                        source,
                        target,
                        (2 * band * held + pair) * step,
                        ((2 * band + 1) * held + pair) * step,
                        [row * step for row in rows],
                        step,
                        [shifts[level, table + row - band * width] for row in rows],
                        width,
                    )
        source, target = target, source
    half_rows = chan_rows // 2
    low = pl.multiple_of(core * half_rows * step, SUBLANES)
    high = pl.multiple_of((1 - core) * half_rows * step, SUBLANES)
    for pair in range(half_rows):
        rows = (2 * pair, 2 * pair + 1)
        merge(
            source,
            target,
            low + pair * step,
            high + pair * step,
            [row * out_tiles for row in rows],
            step,
            [shifts[local_count, place + core * chan_rows + row] for row in rows],
            chan_rows,
        )
    size = chan_rows // group_count * out_tiles
    own = reversed_bits(chip, bits_of(group_count))
    for mask, block in enumerate(blocks):
        start = (own ^ reversed_bits(mask, bits_of(group_count))) * size
        if size % SUBLANES == 0:
            start = pl.multiple_of(start, SUBLANES)
        block[...] = target[pl.ds(start, size), :].astype(jnp.bfloat16)


def toeplitz(filters, target):
    width_count, tap_count = filters.shape
    lane = lax.broadcasted_iota(jnp.int32, (LANES, LANES), 1)
    row = lax.broadcasted_iota(jnp.int32, (LANES, LANES), 0)
    taps = filters[...].astype(jnp.float32)
    zeros = jnp.zeros((LANES, LANES), jnp.float32)
    for width in range(width_count):
        before = zeros
        for start in range(0, tap_count + LANES, LANES):
            if start < tap_count:
                spread = jnp.broadcast_to(taps[width : width + 1, start : start + LANES], (LANES, LANES))
                rolled = pltpu.roll(spread, 0, 1, stride=1, stride_axis=0)
            else:
                rolled = zeros
            part = jnp.where(lane >= row, rolled, before)
            target[width * LANES : (width + 1) * LANES, start : start + LANES] = part.astype(jnp.bfloat16)
            before = rolled


def trial_kernel(plan, group_count, level_count, *refs):
    shifts, filters, refs = refs[0], refs[1], refs[2:]
    parts = []
    for _ in plan.tile_counts:
        parts.append(refs[:group_count])
        refs = refs[group_count:]
    if plan.taken:
        carried, so_far, refs = refs[0], refs[1], refs[2:]
    out, refs = refs[0], refs[1:]
    if plan.given:
        handed, refs = refs[0], refs[1:]
    *stages, ping, pong, last, taps, linear, result, arrived = refs
    width_count, tap_count = filters.shape
    chan_rows = result.shape[0]
    block_rows = chan_rows // group_count
    first_level = level_count - bits_of(group_count)
    chip = lax.axis_index("freq")
    core = lax.axis_index("sub")
    own = reversed_bits(chip * 2 + core, bits_of(group_count) + 1)
    toeplitz(filters, taps)
    for blocks, stage, tiles in zip(parts, stages, plan.tile_counts):
        size = block_rows * tiles
        for mask, block in enumerate(blocks):
            start = (chip ^ mask) * size
            if size % SUBLANES == 0:
                start = pl.multiple_of(start, SUBLANES)
            stage[pl.ds(start, size), :] = block[...].astype(jnp.float32)
    step = plan.step
    if len(stages) == 1 and plan.first == 0:
        source, target, spare, in_step = stages[0], ping, pong, plan.tile_counts[0]
    else:
        for row in range(chan_rows):
            at = row * step
            for index, (stage, tiles) in enumerate(zip(stages, plan.tile_counts)):
                skip = plan.first if index == 0 else 0
                span = rounded_up(tiles - skip, SUBLANES)
                ping[pl.ds(at, span), :] = stage[pl.ds(row * tiles + skip, span), :]
                at += tiles - skip
        source, target, spare, in_step = ping, pong, ping, step
    head = tap_count // LANES if plan.taken else 0
    for section in range(bits_of(group_count)):
        level = first_level + section
        width = block_rows * 2**section
        is_last = section == bits_of(group_count) - 1
        tiles = plan.lengths[section]
        for subband in range(group_count >> section + 1):
            table = subband * 2 ** (level + 1) + own * 2 * width
            for pair in range(width):
                rows = [subband * 2 * width + 2 * pair + odd for odd in range(2)]
                low = subband * 2 * width + pair
                merge(
                    source,
                    last if is_last else target,
                    low * in_step,
                    (low + width) * in_step,
                    [row * plan.last_step + head if is_last else row * step for row in rows],
                    tiles,
                    [shifts[level, table + 2 * pair + odd] for odd in range(2)],
                    2**level,
                )
                if is_last and plan.taken:
                    for row in rows:
                        last[pl.ds(row * plan.last_step, head), :] = carried[pl.ds(row * head, head), :]
        source, target, spare, in_step = target, spare, target, step
    count = plan.out_tiles
    if plan.given:
        kept = tap_count // LANES
        for row in range(chan_rows):
            handed[pl.ds(row * kept, kept), :] = last[pl.ds(row * plan.last_step + count, kept), :]
    scale = 1.0 / math.sqrt(shifts.shape[1])
    rows_now = SUBLANES * plan.last_step
    for first_row in range(0, chan_rows, SUBLANES):
        columns = [
            (last[pl.ds(first_row * plan.last_step + offset, rows_now), :] * scale).astype(jnp.bfloat16)
            for offset in range(tap_count // LANES + 1)
        ]
        response = lax.dot_general(
            jnp.concatenate(columns, axis=1),
            taps[...],
            (((1,), (1,)), ((), ())),
            preferred_element_type=jnp.float32,
        )
        energies = []
        for width in range(width_count):
            one = response[:, width * LANES : (width + 1) * LANES]
            energies.append(0.5 * one * one)
        highest = functools.reduce(jnp.maximum, energies)
        total = functools.reduce(jnp.add, [jnp.exp(energy - highest) for energy in energies])
        linear[pl.ds(first_row * plan.last_step, rows_now), :] = jnp.log(total) + highest
        for tile in range(count):
            result[first_row : first_row + SUBLANES, tile * LANES : (tile + 1) * LANES] = linear[
                pl.ds(first_row * plan.last_step + tile, SUBLANES, stride=plan.last_step), :
            ]
    place = out.at[:, pl.ds(plan.out_first * LANES, count * LANES)]
    copy = pltpu.make_async_copy(result, place, arrived)
    copy.start()
    copy.wait()


class Plan:
    def __init__(self, tile_counts, out_first, out_tiles, taken, given, levels, tap_tiles):
        self.tile_counts = tile_counts
        self.out_first, self.out_tiles = out_first, out_tiles
        self.taken, self.given = taken, given
        reaches = [-(-(2**level) // LANES) for level in levels]
        made = out_tiles if taken else out_tiles + tap_tiles
        self.first = out_first + tap_tiles if taken else 0
        self.lengths = [rounded_up(made + sum(reaches[at + 1 :]), SUBLANES) for at in range(len(levels))]
        self.step = rounded_up(sum(tile_counts) - self.first, SUBLANES)
        self.last_step = out_tiles + tap_tiles


def local(filterbank, delay_shifts, pulse_filters):
    chan_rows, time_len = filterbank.shape
    group_count = lax.axis_size("freq")
    assert lax.axis_size("sub") == 2
    level_count = delay_shifts.shape[0]
    width_count, tap_count = pulse_filters.shape
    tap_tiles = tap_count // LANES
    time_tiles = time_len // LANES
    far_levels = range(level_count - bits_of(group_count), level_count)
    near_reach = 2 ** far_levels[0] - 1
    margin_len = rounded_up(2**level_count - 1 + tap_count, LANES)
    main_tiles = time_tiles - -(-near_reach // LANES)
    whole_tiles = (time_len + rounded_up(2**level_count - 1 - near_reach + tap_count, LANES)) // LANES
    late_tiles = whole_tiles - main_tiles
    late_len = margin_len + time_len - main_tiles * LANES
    hop_count = min(lax.axis_size("tm") - 1, -(-margin_len // time_len))

    in_vmem = pl.BlockSpec(memory_space=pltpu.VMEM)
    in_smem = pl.BlockSpec(memory_space=pltpu.SMEM)
    in_any = pl.BlockSpec(memory_space=pl.ANY)
    params = pltpu.CompilerParams(vmem_limit_bytes=VMEM_LIMIT)
    block_rows = chan_rows // group_count

    def within_chip(own, other, spans, tile_count, out_tiles):
        step = rounded_up(tile_count, SUBLANES)
        state = pltpu.VMEM((2 * chan_rows * step + 2 * SUBLANES, LANES), jnp.float32)
        return pl.pallas_call(
            functools.partial(chip_kernel, spans, tile_count, out_tiles, group_count),
            out_shape=[jax.ShapeDtypeStruct((block_rows * out_tiles, LANES), jnp.bfloat16)] * group_count,
            in_specs=[in_smem] + [in_vmem] * (2 * len(spans)),
            out_specs=[in_vmem] * group_count,
            scratch_shapes=[state, state],
            compiler_params=params,
        )(delay_shifts, *own, *other)

    def exchanged(blocks):
        order = sorted(range(1, group_count), key=lambda mask: -mask)
        received = {mask: from_partner(blocks[mask], "freq", mask) for mask in order}
        return [blocks[0]] + [received[mask] for mask in range(1, group_count)]

    def between_chips(plan, parts, carried=None, so_far=None):
        spare = 2 ** (level_count - 1) // LANES + 2 * SUBLANES
        state = pltpu.VMEM((chan_rows * plan.step + spare, LANES), jnp.float32)
        stages = [
            pltpu.VMEM((chan_rows * tiles + spare + SUBLANES, LANES), jnp.float32) for tiles in plan.tile_counts
        ]
        operands = [delay_shifts, pulse_filters] + [block for blocks in parts for block in blocks]
        in_specs = [in_smem, in_vmem] + [in_vmem] * (len(operands) - 2)
        aliases = {}
        if plan.taken:
            operands += [carried, so_far]
            in_specs += [in_vmem, in_any]
            aliases = {len(operands) - 1: 0}
        out_shape = [jax.ShapeDtypeStruct((chan_rows, time_len), jnp.float32)]
        out_specs = [in_any]
        if plan.given:
            out_shape.append(jax.ShapeDtypeStruct((chan_rows * tap_tiles, LANES), jnp.float32))
            out_specs.append(in_vmem)
        return pl.pallas_call(
            functools.partial(trial_kernel, plan, group_count, level_count),
            out_shape=out_shape,
            in_specs=in_specs,
            out_specs=out_specs,
            scratch_shapes=stages
            + [
                state,
                state,
                pltpu.VMEM((chan_rows * plan.last_step + 4 * SUBLANES + spare, LANES), jnp.float32),
                pltpu.VMEM((width_count * LANES, tap_count + LANES), jnp.bfloat16),
                pltpu.VMEM((chan_rows * plan.last_step, LANES), jnp.float32),
                pltpu.VMEM((chan_rows, plan.out_tiles * LANES), jnp.float32),
                pltpu.SemaphoreType.DMA,
            ],
            input_output_aliases=aliases,
            compiler_params=params,
        )(*operands)

    other_core = from_partner(filterbank, "sub", 1)
    halos, spans = ([], []), [(main_tiles * LANES, time_len - main_tiles * LANES)]
    collected = 0
    for hop in range(1, hop_count + 1):
        take_len = min(time_len, margin_len - collected)
        ahead = filterbank[:, :take_len]
        for crossed in range(2):
            halos[crossed].append(from_ahead(ahead, hop, crossed))
        spans.append((0, take_len))
        collected += take_len
    main = within_chip([filterbank], [other_core], [(0, time_len)], time_tiles, main_tiles)
    main = exchanged(main)
    late = within_chip(
        [filterbank] + halos[0], [other_core] + halos[1], spans, late_len // LANES, late_tiles
    )
    late = exchanged(late)
    lost = sum(-(-(2**level) // LANES) for level in far_levels) + tap_tiles
    early_tiles = main_tiles - lost
    if early_tiles <= 0:
        plan = Plan([main_tiles, late_tiles], 0, time_tiles, False, False, far_levels, tap_tiles)
        return between_chips(plan, [main, late])[0]
    plan = Plan([main_tiles], 0, early_tiles, False, True, far_levels, tap_tiles)
    out, carried = between_chips(plan, [main])
    plan = Plan(
        [main_tiles, late_tiles], early_tiles, time_tiles - early_tiles, True, False, far_levels, tap_tiles
    )
    return between_chips(plan, [main, late], carried, out)[0]


def solution(mesh):
    in_specs = (P(("beams", "freq", "sub"), "tm"), P(), P())
    out_specs = P(("beams", "freq", "sub"), "tm")
    return jax.shard_map(local, mesh=mesh, in_specs=in_specs, out_specs=out_specs, check_vma=False)
```

profile of v0, /device:TPU:0, one launch (start us, length us, event | category | flops | bytes accessed | tf_op | source)
XLA Modules:
  0.0 29.0 jit_solution(13878053419311583100)
XLA Ops:
  0.0 0.5 %collective-permute-start = (bf16[64,2048]{1,0:T(8,128)(2,1)}, bf16[64,2048]{1,0:T(8,128)(2,1)S(1)}, u32[]{:S(2)}, u32[]{:S(2)}) collective-permute-start(bf16[64,2048]{1,0:T(8,128)(2,1)} %refs_0_.5), channel_id=1, source_target_pairs={{0,1},{1,0},{2,3},{3,2},{4,5},{5,4},{6,7},{7,6},{8,9},{9,8},{10,11... | collective-permute-start | bytes 786440 | tf_op jit(solution)/shard_map/ppermute | solution.py:44
  0.5 0.9 %slice.3 = bf16[64,768]{1,0:T(8,128)(2,1)S(1)} slice(bf16[64,2048]{1,0:T(8,128)(2,1)} %refs_0_.5), slice={[0:64], [0:768]} | slice | bytes 196608 | tf_op jit(solution)/shard_map/slice | solution.py:346
  1.4 1.3 %collective-permute-start.5 = (bf16[64,768]{1,0:T(8,128)(2,1)S(1)}, bf16[64,768]{1,0:T(8,128)(2,1)S(1)}, u32[]{:S(2)}, u32[]{:S(2)}) collective-permute-start(bf16[64,768]{1,0:T(8,128)(2,1)S(1)} %slice.3), channel_id=1, source_target_pairs={{2,1},{3,0},{6,5},{7,4},{10,9},{11,8},{14,13},{15,12},{18,17},{19,... | collective-permute-start | bytes 294920 | tf_op jit(solution)/shard_map/ppermute | solution.py:39
  2.6 1.3 %collective-permute-start.4 = (bf16[64,768]{1,0:T(8,128)(2,1)S(1)}, bf16[64,768]{1,0:T(8,128)(2,1)S(1)}, u32[]{:S(2)}, u32[]{:S(2)}) collective-permute-start(bf16[64,768]{1,0:T(8,128)(2,1)S(1)} %slice.3), channel_id=1, source_target_pairs={{2,0},{3,1},{6,4},{7,5},{10,8},{11,9},{14,12},{15,13},{18,16},{19,... | collective-permute-start | bytes 294920 | tf_op jit(solution)/shard_map/ppermute | solution.py:39
  3.9 0.0 collective-permute-done.refs_1_.refs_2_
  4.0 0.0 copy-start
  4.0 0.9 %copy-done = bf16[64,2048]{1,0:T(8,128)(2,1)S(1)} copy-done((bf16[64,2048]{1,0:T(8,128)(2,1)S(1)}, bf16[64,2048]{1,0:T(8,128)(2,1)}, u32[]{:S(2)}) %copy-start) | copy-done | bytes 262168
  4.9 2.6 %shard_map.37 = (bf16[240,128]{1,0:T(8,128)(2,1)S(1)}, bf16[240,128]{1,0:T(8,128)(2,1)S(1)}, bf16[240,128]{1,0:T(8,128)(2,1)S(1)}, bf16[240,128]{1,0:T(8,128)(2,1)S(1)}) custom-call(s32[9,512]{1,0:T(8,128)S(1)} %copy-done.1, bf16[64,2048]{1,0:T(8,128)(2,1)S(1)} %copy-done, bf16[64,2048]{1,0:T(8,128)(2,1)S(1)} %collective-permute-done.refs_1_.refs_2_), custom_call_target="tpu_custom_call" | custom-call | tf_op jit(solution)/shard_map/pallas_call | solution.py:290
  7.5 2.6 %collective-permute-start.1 = (bf16[240,128]{1,0:T(8,128)(2,1)S(1)}, bf16[240,128]{1,0:T(8,128)(2,1)S(1)}, u32[]{:S(2)}, u32[]{:S(2)}) collective-permute-start(bf16[240,128]{1,0:T(8,128)(2,1)S(1)} %get-tuple-element.16), channel_id=1, source_target_pairs={{0,4},{4,0},{8,12},{12,8},{1,5},{5,1},{9,13},{13,9},{2,6},{6,2},{1... | collective-permute-start | bytes 184328 | tf_op jit(solution)/shard_map/ppermute | solution.py:44
  10.1 2.6 %collective-permute-start.2 = (bf16[240,128]{1,0:T(8,128)(2,1)S(1)}, bf16[240,128]{1,0:T(8,128)(2,1)S(1)}, u32[]{:S(2)}, u32[]{:S(2)}) collective-permute-start(bf16[240,128]{1,0:T(8,128)(2,1)S(1)} %get-tuple-element.17), channel_id=1, source_target_pairs={{0,8},{4,12},{8,0},{12,4},{1,9},{5,13},{9,1},{13,5},{2,10},{6,14},... | collective-permute-start | bytes 184328 | tf_op jit(solution)/shard_map/ppermute | solution.py:44
  12.7 0.0 collective-permute-start.3
  12.7 0.0 collective-permute-done.5.refs_3_
  12.7 2.3 %shard_map.38 = (bf16[96,128]{1,0:T(8,128)(2,1)S(1)}, bf16[96,128]{1,0:T(8,128)(2,1)S(1)}, bf16[96,128]{1,0:T(8,128)(2,1)S(1)}, bf16[96,128]{1,0:T(8,128)(2,1)S(1)}) custom-call(s32[9,512]{1,0:T(8,128)S(1)} %copy-done.1, bf16[64,2048]{1,0:T(8,128)(2,1)S(1)} %copy-done, bf16[64,768]{1,0:T(8,128)(2,1)S(1)} %collective-permute-done.4.refs_1_, ...), custom_call_target="tpu_custom_call" | custom-call | tf_op jit(solution)/shard_map/pallas_call | solution.py:290
  15.0 0.0 copy-start.2
  15.1 1.0 %collective-permute-start.6 = (bf16[96,128]{1,0:T(8,128)(2,1)S(1)}, bf16[96,128]{1,0:T(8,128)(2,1)S(1)}, u32[]{:S(2)}, u32[]{:S(2)}) collective-permute-start(bf16[96,128]{1,0:T(8,128)(2,1)S(1)} %get-tuple-element.20), channel_id=1, source_target_pairs={{0,4},{4,0},{8,12},{12,8},{1,5},{5,1},{9,13},{13,9},{2,6},{6,2},{1... | collective-permute-start | bytes 73736 | tf_op jit(solution)/shard_map/ppermute | solution.py:44
  16.0 3.5 %collective-permute-start.7 = (bf16[96,128]{1,0:T(8,128)(2,1)S(1)}, bf16[96,128]{1,0:T(8,128)(2,1)S(1)}, u32[]{:S(2)}, u32[]{:S(2)}) collective-permute-start(bf16[96,128]{1,0:T(8,128)(2,1)S(1)} %get-tuple-element.21), channel_id=1, source_target_pairs={{0,8},{4,12},{8,0},{12,4},{1,9},{5,13},{9,1},{13,5},{2,10},{6,14},... | collective-permute-start | bytes 73736 | tf_op jit(solution)/shard_map/ppermute | solution.py:44
  19.5 0.0 collective-permute-done.1.refs_3_
  19.5 0.0 collective-permute-start.8
  19.5 0.0 collective-permute-done.2.refs_4_
  19.5 0.0 collective-permute-done.3.refs_5_
  19.5 3.9 %shard_map.39 = (f32[64,2048]{1,0:T(8,128)}, f32[128,128]{1,0:T(8,128)S(1)}) custom-call(s32[9,512]{1,0:T(8,128)S(1)} %copy-done.1, bf16[6,256]{1,0:T(8,128)(2,1)S(1)} %copy-done.2, bf16[240,128]{1,0:T(8,128)(2,1)S(1)} %get-tuple-element.15.refs_2_, bf16[240,128]{1,0:T(8,128)(2,1)S(1)} %collective-permute-done.1.refs_3_, ...), custom_call_target="tpu_custom_call" | custom-call | tf_op jit(solution)/shard_map/pallas_call | solution.py:322
  23.5 0.0 collective-permute-done.7.refs_8_
  23.5 1.6 %collective-permute-done.8.refs_9_ = bf16[96,128]{1,0:T(8,128)(2,1)S(1)} collective-permute-done((bf16[96,128]{1,0:T(8,128)(2,1)S(1)}, bf16[96,128]{1,0:T(8,128)(2,1)S(1)}, u32[]{:S(2)}, u32[]{:S(2)}) %collective-permute-start.8) | collective-permute-done | bytes 24608 | tf_op jit(solution)/shard_map/ppermute | solution.py:44
  25.1 3.9 %shard_map.40 = f32[64,2048]{1,0:T(8,128)} custom-call(s32[9,512]{1,0:T(8,128)S(1)} %copy-done.1, bf16[6,256]{1,0:T(8,128)(2,1)S(1)} %copy-done.2, bf16[240,128]{1,0:T(8,128)(2,1)S(1)} %get-tuple-element.15.refs_2_, bf16[240,128]{1,0:T(8,128)(2,1)S(1)} %collective-permute-done.1.refs_3_, ...), custom_call_target="tpu_custom_call", output_to_operand_aliasing={{}: (11, {})} | custom-call | tf_op jit(solution)/shard_map/pallas_call | solution.py:322
  (5 shorter events, 0.0 us)
Async XLA Ops:
  0.0 4.0 %copy-start.1 = (s32[9,512]{1,0:T(8,128)S(1)}, s32[9,512]{1,0:T(8,128)}, u32[]{:S(2)}) copy-start(s32[9,512]{1,0:T(8,128)} %refs_0_.7) | copy-start | bytes 55300
  0.0 3.9 %collective-permute-start = (bf16[64,2048]{1,0:T(8,128)(2,1)}, bf16[64,2048]{1,0:T(8,128)(2,1)S(1)}, u32[]{:S(2)}, u32[]{:S(2)}) collective-permute-start(bf16[64,2048]{1,0:T(8,128)(2,1)} %refs_0_.5), channel_id=1, source_target_pairs={{0,1},{1,0},{2,3},{3,2},{4,5},{5,4},{6,7},{7,6},{8,9},{9,8},{10,11... | collective-permute-start | bytes 786440 | tf_op jit(solution)/shard_map/ppermute | solution.py:44
  1.4 11.4 %collective-permute-start.5 = (bf16[64,768]{1,0:T(8,128)(2,1)S(1)}, bf16[64,768]{1,0:T(8,128)(2,1)S(1)}, u32[]{:S(2)}, u32[]{:S(2)}) collective-permute-start(bf16[64,768]{1,0:T(8,128)(2,1)S(1)} %slice.3), channel_id=1, source_target_pairs={{2,1},{3,0},{6,5},{7,4},{10,9},{11,8},{14,13},{15,12},{18,17},{19,... | collective-permute-start | bytes 294920 | tf_op jit(solution)/shard_map/ppermute | solution.py:39
  2.6 10.1 %collective-permute-start.4 = (bf16[64,768]{1,0:T(8,128)(2,1)S(1)}, bf16[64,768]{1,0:T(8,128)(2,1)S(1)}, u32[]{:S(2)}, u32[]{:S(2)}) collective-permute-start(bf16[64,768]{1,0:T(8,128)(2,1)S(1)} %slice.3), channel_id=1, source_target_pairs={{2,0},{3,1},{6,4},{7,5},{10,8},{11,9},{14,12},{15,13},{18,16},{19,... | collective-permute-start | bytes 294920 | tf_op jit(solution)/shard_map/ppermute | solution.py:39
  4.0 1.0 %copy-start = (bf16[64,2048]{1,0:T(8,128)(2,1)S(1)}, bf16[64,2048]{1,0:T(8,128)(2,1)}, u32[]{:S(2)}) copy-start(bf16[64,2048]{1,0:T(8,128)(2,1)} %refs_0_.5) | copy-start | bytes 786436
  7.5 12.0 %collective-permute-start.1 = (bf16[240,128]{1,0:T(8,128)(2,1)S(1)}, bf16[240,128]{1,0:T(8,128)(2,1)S(1)}, u32[]{:S(2)}, u32[]{:S(2)}) collective-permute-start(bf16[240,128]{1,0:T(8,128)(2,1)S(1)} %get-tuple-element.16), channel_id=1, source_target_pairs={{0,4},{4,0},{8,12},{12,8},{1,5},{5,1},{9,13},{13,9},{2,6},{6,2},{1... | collective-permute-start | bytes 184328 | tf_op jit(solution)/shard_map/ppermute | solution.py:44
  10.1 9.4 %collective-permute-start.2 = (bf16[240,128]{1,0:T(8,128)(2,1)S(1)}, bf16[240,128]{1,0:T(8,128)(2,1)S(1)}, u32[]{:S(2)}, u32[]{:S(2)}) collective-permute-start(bf16[240,128]{1,0:T(8,128)(2,1)S(1)} %get-tuple-element.17), channel_id=1, source_target_pairs={{0,8},{4,12},{8,0},{12,4},{1,9},{5,13},{9,1},{13,5},{2,10},{6,14},... | collective-permute-start | bytes 184328 | tf_op jit(solution)/shard_map/ppermute | solution.py:44
  12.7 6.8 %collective-permute-start.3 = (bf16[240,128]{1,0:T(8,128)(2,1)S(1)}, bf16[240,128]{1,0:T(8,128)(2,1)S(1)}, u32[]{:S(2)}, u32[]{:S(2)}) collective-permute-start(bf16[240,128]{1,0:T(8,128)(2,1)S(1)} %get-tuple-element.18), channel_id=1, source_target_pairs={{0,12},{4,8},{8,4},{12,0},{1,13},{5,9},{9,5},{13,1},{2,14},{6,10},... | collective-permute-start | bytes 184328 | tf_op jit(solution)/shard_map/ppermute | solution.py:44
  15.0 4.5 %copy-start.2 = (bf16[6,256]{1,0:T(8,128)(2,1)S(1)}, bf16[6,256]{1,0:T(8,128)(2,1)}, u32[]{:S(2)}) copy-start(bf16[6,256]{1,0:T(8,128)(2,1)} %refs_1_.3) | copy-start | bytes 9220
  15.1 8.4 %collective-permute-start.6 = (bf16[96,128]{1,0:T(8,128)(2,1)S(1)}, bf16[96,128]{1,0:T(8,128)(2,1)S(1)}, u32[]{:S(2)}, u32[]{:S(2)}) collective-permute-start(bf16[96,128]{1,0:T(8,128)(2,1)S(1)} %get-tuple-element.20), channel_id=1, source_target_pairs={{0,4},{4,0},{8,12},{12,8},{1,5},{5,1},{9,13},{13,9},{2,6},{6,2},{1... | collective-permute-start | bytes 73736 | tf_op jit(solution)/shard_map/ppermute | solution.py:44
  16.0 7.5 %collective-permute-start.7 = (bf16[96,128]{1,0:T(8,128)(2,1)S(1)}, bf16[96,128]{1,0:T(8,128)(2,1)S(1)}, u32[]{:S(2)}, u32[]{:S(2)}) collective-permute-start(bf16[96,128]{1,0:T(8,128)(2,1)S(1)} %get-tuple-element.21), channel_id=1, source_target_pairs={{0,8},{4,12},{8,0},{12,4},{1,9},{5,13},{9,1},{13,5},{2,10},{6,14},... | collective-permute-start | bytes 73736 | tf_op jit(solution)/shard_map/ppermute | solution.py:44
  19.5 5.6 %collective-permute-start.8 = (bf16[96,128]{1,0:T(8,128)(2,1)S(1)}, bf16[96,128]{1,0:T(8,128)(2,1)S(1)}, u32[]{:S(2)}, u32[]{:S(2)}) collective-permute-start(bf16[96,128]{1,0:T(8,128)(2,1)S(1)} %get-tuple-element.22), channel_id=1, source_target_pairs={{0,12},{4,8},{8,4},{12,0},{1,13},{5,9},{9,5},{13,1},{2,14},{6,10},... | collective-permute-start | bytes 73736 | tf_op jit(solution)/shard_map/ppermute | solution.py:44
where the time goes:
time: 29.2 us; the launch traced here: 29 us
  starting transfers between devices  12.7 us (43%)
  Pallas kernels  12.7 us (43%)
  local copies, waits for them, and re-layouts  1.85 us (6%)
  waiting for transfers between devices  1.64 us (6%)
    ppermute x7, starting transfers between devices, from_partner(): lax.ppermute(value, axis, [(source, source ^ mask) for source in range(co...  10.1 us
    pallas_call x2, Pallas kernels, between_chips(): pl.pallas_call(functools.partial(trial_kernel, plan, group_count, level_c...  7.81 us
    pallas_call x2, Pallas kernels, within_chip(): pl.pallas_call(functools.partial(chip_kernel, spans, tile_count, out_tile...  4.86 us
    ppermute x2, starting transfers between devices, from_ahead(): return lax.ppermute(value, ('tm', 'sub'), route)  2.57 us
    ppermute x7, waiting for transfers between devices, from_partner(): lax.ppermute(value, axis, [(source, source ^ mask) for source in range(co...  1.64 us
    unnamed x6, local copies, waits for them, and re-layouts  0.96 us
    slice x1, local copies, waits for them, and re-layouts, local(): ahead = filterbank[:, :take_len]  0.9 us
  transfers between devices with their start and end apart: 9, of which 1 were waited for; matrix products, arithmetic and copies ran while one was open for 3% of the time, Pallas kernels for 30%

commit v1 on v0

v1 whole, which is shorter than its diff:
```python
import functools
import math

import jax
import jax.numpy as jnp
from jax import lax
from jax.experimental import pallas as pl
from jax.experimental.pallas import tpu as pltpu
from jax.sharding import PartitionSpec as P

LANES = 128
SUBLANES = 8
PACKED = 16
LOG2_E = 1.4426950408889634
VMEM_LIMIT = 48 * 2**20


def rounded_up(value, unit):
    return -(-value // unit) * unit


def reversed_bits(value, bit_count):
    result = 0
    for bit_num in range(bit_count):
        result = result | (value >> bit_num & 1) << bit_count - 1 - bit_num
    return result


def bits_of(count):
    return count.bit_length() - 1


def from_ahead(value, steps, crossed):
    count, cores = lax.axis_size("tm"), lax.axis_size("sub")
    route = [
        ((block + steps) % count * cores + core, block * cores + (core ^ crossed))
        for block in range(count)
        for core in range(cores)
    ]
    return lax.ppermute(value, ("tm", "sub"), route)


def from_partner(value, axis, mask):
    count = lax.axis_size(axis)
    return lax.ppermute(value, axis, [(source, source ^ mask) for source in range(count)])


def lanes():
    return lax.broadcasted_iota(jnp.int32, (SUBLANES, LANES), 1)


def gathered(value, index):
    return jnp.take_along_axis(value, index, axis=1, mode="promise_in_bounds")


def transposed_table(rows, table, columns):
    for index, row in enumerate(rows):
        table[index : index + 1, :] = row.astype(jnp.float32)
    columns[...] = table[...].T


def merge(source, target, low, high, outs, tiles, most):
    lane = lanes()
    apart = max(most // LANES, 1)
    chosen = []
    for amount, place in outs:
        part = amount if most < LANES else amount & LANES - 1
        moved = (lane < part).astype(jnp.int32)
        if most >= LANES:
            moved = moved + (amount >> bits_of(LANES))
        masks = [moved == offset for offset in range(1, apart + 1)]
        chosen.append((masks, lane + part & LANES - 1, place))
    upper = [source[offset, high, :] for offset in range(apart)]
    for tile in range(tiles):
        upper.append(source[tile + apart, high, :])
        lower = source[tile, low, :]
        for masks, index, place in chosen:
            mixed = upper[0]
            for mask, other in zip(masks, upper[1:]):
                mixed = jnp.where(mask, other, mixed)
            target[tile, place, :] = lower + gathered(mixed, index)
        upper = upper[1:]


def tree_levels(state, other, columns, first, levels, held, lengths):
    rows = columns.shape[0] // 2
    source, target = state, other
    done = 0
    while done < len(levels):
        narrow = held < SUBLANES
        bits = min(bits_of(SUBLANES // held), len(levels) - done) if narrow else len(levels) - done
        for turn in range(bits):
            level = levels[done + turn]
            inner = turn + 1 < bits

            def rows_in(vector, start, stride):
                return pl.ds(start, SUBLANES, stride=stride) if turn == 0 else pl.ds(vector * SUBLANES, SUBLANES)

            def rows_out(vector, start, stride):
                return pl.ds(vector * SUBLANES, SUBLANES) if inner else pl.ds(start, SUBLANES, stride=stride)

            def amounts(start, stride):
                column = columns[pl.ds(start, SUBLANES, stride=stride), :]
                one = column[:, first + done + turn : first + done + turn + 1]
                return jnp.broadcast_to(one, (SUBLANES, LANES)).astype(jnp.int32)

            if narrow:
                now = held << turn
                for band in range(SUBLANES // (2 * now)):
                    for trial in range(now):
                        low, high = 2 * band * now + trial, (2 * band + 1) * now + trial
                        outs = [band * 2 * now + 2 * trial + odd for odd in range(2)]
                        merge(
                            source,
                            target,
                            rows_in(low, low, SUBLANES),
                            rows_in(high, high, SUBLANES),
                            [(amounts(out, SUBLANES), rows_out(out, out, SUBLANES)) for out in outs],
                            lengths[done + turn],
                            2**level,
                        )
            else:
                groups, split = held // SUBLANES, 2**turn
                for band in range(rows // (2 * held * split)):
                    for group in range(groups):
                        for place in range(split):
                            low, high = [
                                ((2 * band + upper) * groups + group) * split + place for upper in range(2)
                            ]
                            outs = []
                            for odd in range(2):
                                vector = (band * groups + group) * 2 * split + 2 * place + odd
                                start = (band * groups + group) * SUBLANES * 2 * split + 2 * place + odd
                                outs.append((amounts(start, 2 * split), rows_out(vector, start, 2 * split)))
                            merge(
                                source,
                                target,
                                rows_in(low, low * SUBLANES, 1),
                                rows_in(high, high * SUBLANES, 1),
                                outs,
                                lengths[done + turn],
                                2**level,
                            )
            source, target = target, source
        held <<= bits
        done += bits
    return source


def lengths_of(made, levels):
    return [made + -(-sum(2**later for later in levels if later > level) // LANES) for level in levels]


def chip_kernel(spans, out_tiles, group_count, shifts, *refs):
    pieces = (refs[: len(spans)], refs[len(spans) : 2 * len(spans)])
    blocks = refs[2 * len(spans) : 2 * len(spans) + group_count]
    raw, ping, pong, table, columns = refs[2 * len(spans) + group_count :]
    chan_rows = pieces[0][0].shape[0]
    local_count = bits_of(chan_rows)
    chip, core = lax.axis_index("freq"), lax.axis_index("sub")
    chunk = shifts[0:SUBLANES, pl.ds(pl.multiple_of(chip * LANES, LANES), LANES)]
    lane, level = lanes(), lax.broadcasted_iota(jnp.int32, (SUBLANES, LANES), 0)
    kept = lane & (1 << level) - 1
    picked = gathered(chunk, (2 * (lane - kept) + (core << level) + kept) & LANES - 1)
    transposed_table([picked[at : at + 1, :] for at in range(local_count + 1)], table, columns)
    for side in range(2):
        place = pl.multiple_of((core ^ side) * chan_rows, chan_rows)
        tile = 0
        for piece, (column, length, ahead) in zip(pieces[side], spans):
            there = lax.axis_index("tm") + ahead < lax.axis_size("tm")
            for start in range(column, column + length, LANES):
                part = piece[:, start : start + LANES].astype(jnp.float32)
                if ahead:
                    part = jnp.where(there, part, 0.0)
                raw[tile, pl.ds(place, chan_rows), :] = part
                tile += 1
        for later in range(tile, raw.shape[0] - 1):
            raw[later, pl.ds(place, chan_rows), :] = jnp.zeros((chan_rows, LANES), jnp.float32)
    levels = list(range(local_count + 1))
    lengths = lengths_of(out_tiles, levels)
    for vector in range(SUBLANES):
        column = columns[pl.ds(vector, SUBLANES, stride=SUBLANES), :]
        amount = jnp.broadcast_to(column[:, 0:1], (SUBLANES, LANES)).astype(jnp.int32)
        merge(
            raw,
            ping,
            pl.ds(2 * vector, SUBLANES, stride=2 * SUBLANES),
            pl.ds(2 * vector + 1, SUBLANES, stride=2 * SUBLANES),
            [(amount, pl.ds(vector, SUBLANES, stride=SUBLANES))],
            lengths[0],
            1,
        )
    last = tree_levels(ping, pong, columns, 1, levels[1:], 1, lengths[1:])
    size = chan_rows // group_count
    own = reversed_bits(chip, bits_of(group_count))
    for mask, block in enumerate(blocks):
        start = pl.multiple_of((own ^ reversed_bits(mask, bits_of(group_count))) * size, size)
        for tile in range(out_tiles):
            block[tile, :, :] = last[tile, pl.ds(start, size), :].astype(jnp.bfloat16)


def toeplitz(filters, target):
    width_count, tap_count = filters.shape
    lane = lax.broadcasted_iota(jnp.int32, (LANES, LANES), 1)
    row = lax.broadcasted_iota(jnp.int32, (LANES, LANES), 0)
    taps = filters[...].astype(jnp.float32)
    zeros = jnp.zeros((LANES, LANES), jnp.float32)
    for width in range(width_count):
        before = zeros
        for start in range(0, tap_count + LANES, LANES):
            if start < tap_count:
                spread = jnp.broadcast_to(taps[width : width + 1, start : start + LANES], (LANES, LANES))
                rolled = pltpu.roll(spread, 0, 1, stride=1, stride_axis=0)
            else:
                rolled = zeros
            part = jnp.where(lane >= row, rolled, before)
            target[width * LANES : (width + 1) * LANES, start : start + LANES] = part.astype(jnp.bfloat16)
            before = rolled


def trial_kernel(plan, group_count, level_count, *refs):
    shifts, filters, refs = refs[0], refs[1], refs[2:]
    parts = []
    for _ in plan.tile_counts:
        parts.append(refs[:group_count])
        refs = refs[group_count:]
    if plan.taken:
        carried, taps, so_far, refs = refs[0], refs[1], refs[2], refs[3:]
    out, refs = refs[0], refs[1:]
    if plan.given:
        handed, taps, refs = refs[0], refs[1], refs[2:]
    state, other, table, columns, normal, responses, result, arrived = refs[:8]
    if not plan.given and not plan.taken:
        taps = refs[8]
    width_count, tap_count = filters.shape
    chan_rows = result.shape[0]
    block_rows = chan_rows // group_count
    levels = list(range(level_count - bits_of(group_count), level_count))
    chip, core = lax.axis_index("freq"), lax.axis_index("sub")
    own = reversed_bits(chip * 2 + core, bits_of(group_count) + 1)
    lane = lax.broadcasted_iota(jnp.int32, (1, LANES), 1)
    rows = []
    for section, level in enumerate(levels):
        wide = block_rows * 2 ** (section + 1)
        row = jnp.zeros((1, LANES), jnp.int32)
        for subband in range(chan_rows // wide):
            start = subband * 2 ** (level + 1) + own * wide
            tile = pl.multiple_of(start >> bits_of(LANES) << bits_of(LANES), LANES)
            chunk = shifts[level : level + 1, pl.ds(tile, LANES)]
            moved = pltpu.roll(chunk, subband * wide - (start & LANES - 1) & LANES - 1, 1)
            row = jnp.where(lane >= subband * wide, moved, row)
        rows.append(row)
    transposed_table(rows, table, columns)
    if not plan.taken:
        toeplitz(filters, taps)
    at = 0
    for index, (blocks, tiles) in enumerate(zip(parts, plan.tile_counts)):
        skip = plan.first if index == 0 else 0
        for mask, block in enumerate(blocks):
            start = pl.multiple_of((chip ^ mask) * block_rows, block_rows)
            for tile in range(skip, tiles):
                state[at + tile - skip, pl.ds(start, block_rows), :] = block[tile, :, :].astype(jnp.float32)
        at += tiles - skip
    last = tree_levels(state, other, columns, 0, levels, block_rows, plan.lengths)
    scale = 1.0 / math.sqrt(shifts.shape[1])
    kept = tap_count // LANES
    head = kept if plan.taken else 0
    for tile in range(head):
        normal[tile, :, :] = carried[tile, :, :]
    for tile in range(plan.made):
        normal[head + tile, :, :] = (last[tile, :, :] * scale).astype(jnp.bfloat16)
    count = plan.out_tiles
    if plan.given:
        for tile in range(kept):
            handed[tile, :, :] = normal[count + tile, :, :]
    copies = []
    for turn, (first_tile, some) in enumerate(plan.chunks):
        size = some * chan_rows
        windows = [
            normal[first_tile + offset : first_tile + offset + some, :, :].reshape(size, LANES)
            for offset in range(kept + 1)
        ]
        responses[0:size, :] = lax.dot_general(
            jnp.concatenate(windows, axis=1),
            taps[...],
            (((1,), (1,)), ((), ())),
            preferred_element_type=jnp.float32,
        )
        for first_row in range(0, size, PACKED):
            energies = []
            for width in range(width_count):
                one = responses[first_row : first_row + PACKED, width * LANES : (width + 1) * LANES]
                energies.append((0.5 * LOG2_E) * one * one)
            highest = functools.reduce(jnp.maximum, energies)
            total = functools.reduce(jnp.add, [jnp.exp2(energy - highest) for energy in energies])
            tile, row = first_tile + first_row // chan_rows, first_row % chan_rows
            result[row : row + PACKED, tile * LANES : (tile + 1) * LANES] = (
                jnp.log2(total) + highest
            ) * (1.0 / LOG2_E)
        columns_now = pl.ds(first_tile * LANES, some * LANES)
        place = out.at[:, pl.ds((plan.out_first + first_tile) * LANES, some * LANES)]
        copies.append(pltpu.make_async_copy(result.at[:, columns_now], place, arrived.at[turn]))
        copies[-1].start()
    for copy in copies:
        copy.wait()


class Plan:
    def __init__(self, tile_counts, out_first, out_tiles, taken, given, levels, tap_tiles):
        self.tile_counts = tile_counts
        self.out_first, self.out_tiles = out_first, out_tiles
        self.taken, self.given = taken, given
        self.made = out_tiles if taken else out_tiles + tap_tiles
        self.first = out_first + tap_tiles if taken else 0
        self.lengths = lengths_of(self.made, levels)
        turns = -(-out_tiles // 6)
        ends = [out_tiles * turn // turns for turn in range(turns + 1)]
        self.chunks = [(start, end - start) for start, end in zip(ends, ends[1:])]
        self.state_tiles = sum(tile_counts) - self.first + max(2 ** levels[-1] // LANES, 1) + 1


def local(filterbank, delay_shifts, pulse_filters):
    chan_rows, time_len = filterbank.shape
    group_count = lax.axis_size("freq")
    assert lax.axis_size("sub") == 2 and 2 * chan_rows == LANES
    level_count = delay_shifts.shape[0]
    width_count, tap_count = pulse_filters.shape
    tap_tiles = tap_count // LANES
    time_tiles = time_len // LANES
    far_levels = range(level_count - bits_of(group_count), level_count)
    near_reach = 2 ** far_levels[0] - 1
    margin_len = rounded_up(2**level_count - 1 + tap_count, LANES)
    main_tiles = time_tiles - -(-near_reach // LANES)
    whole_tiles = (time_len + rounded_up(2**level_count - 1 - near_reach + tap_count, LANES)) // LANES
    late_tiles = whole_tiles - main_tiles
    late_len = margin_len + time_len - main_tiles * LANES
    hop_count = min(lax.axis_size("tm") - 1, -(-margin_len // time_len))

    in_vmem = pl.BlockSpec(memory_space=pltpu.VMEM)
    in_any = pl.BlockSpec(memory_space=pl.ANY)
    params = pltpu.CompilerParams(vmem_limit_bytes=VMEM_LIMIT)
    block_rows = chan_rows // group_count
    table = pltpu.VMEM((LANES, LANES), jnp.float32)

    def within_chip(own, other, spans, tile_count, out_tiles):
        state = pltpu.VMEM((tile_count + 1, chan_rows, LANES), jnp.float32)
        block = jax.ShapeDtypeStruct((out_tiles, block_rows, LANES), jnp.bfloat16)
        return pl.pallas_call(
            functools.partial(chip_kernel, spans, out_tiles, group_count),
            out_shape=[block] * group_count,
            in_specs=[in_vmem] * (1 + 2 * len(spans)),
            out_specs=[in_vmem] * group_count,
            scratch_shapes=[
                pltpu.VMEM((tile_count + 1, 2 * chan_rows, LANES), jnp.float32),
                state,
                state,
                table,
                table,
            ],
            compiler_params=params,
        )(delay_shifts, *own, *other)

    def exchanged(blocks):
        order = sorted(range(1, group_count), key=lambda mask: -mask)
        received = {mask: from_partner(blocks[mask], "freq", mask) for mask in order}
        return [blocks[0]] + [received[mask] for mask in range(1, group_count)]

    def between_chips(plan, parts, carried=()):
        state = pltpu.VMEM((plan.state_tiles, chan_rows, LANES), jnp.float32)
        taps = ((width_count * LANES, tap_count + LANES), jnp.bfloat16)
        operands = [delay_shifts, pulse_filters] + [block for blocks in parts for block in blocks]
        operands += carried
        in_specs = [in_vmem] * len(operands)
        aliases = {}
        if plan.taken:
            in_specs[-1] = in_any
            aliases = {len(operands) - 1: 0}
        out_shape = [jax.ShapeDtypeStruct((chan_rows, time_len), jnp.float32)]
        out_specs = [in_any]
        scratch = []
        if plan.given:
            out_shape += [
                jax.ShapeDtypeStruct((tap_tiles, chan_rows, LANES), jnp.bfloat16),
                jax.ShapeDtypeStruct(*taps),
            ]
            out_specs += [in_vmem] * 2
        elif not plan.taken:
            scratch = [pltpu.VMEM(*taps)]
        most = max(some for _, some in plan.chunks)
        return pl.pallas_call(
            functools.partial(trial_kernel, plan, group_count, level_count),
            out_shape=out_shape,
            in_specs=in_specs,
            out_specs=out_specs,
            scratch_shapes=[
                state,
                state,
                table,
                table,
                pltpu.VMEM((plan.out_tiles + tap_tiles, chan_rows, LANES), jnp.bfloat16),
                pltpu.VMEM((most * chan_rows, width_count * LANES), jnp.float32),
                pltpu.VMEM((chan_rows, plan.out_tiles * LANES), jnp.float32),
                pltpu.SemaphoreType.DMA((len(plan.chunks),)),
            ]
            + scratch,
            input_output_aliases=aliases,
            compiler_params=params,
        )(*operands)

    other_core = from_partner(filterbank, "sub", 1)
    halos, spans = ([], []), [(main_tiles * LANES, time_len - main_tiles * LANES, 0)]
    collected = 0
    for hop in range(1, hop_count + 1):
        take_len = min(time_len, margin_len - collected)
        ahead = filterbank[:, :take_len]
        for crossed in range(2):
            halos[crossed].append(from_ahead(ahead, hop, crossed))
        spans.append((0, take_len, hop))
        collected += take_len
    main = within_chip([filterbank], [other_core], [(0, time_len, 0)], time_tiles, main_tiles)
    main = exchanged(main)
    late = within_chip(
        [filterbank] + halos[0], [other_core] + halos[1], spans, late_len // LANES, late_tiles
    )
    late = exchanged(late)
    lost = -(-sum(2**level for level in far_levels) // LANES) + tap_tiles
    early_tiles = main_tiles - lost
    if early_tiles <= 0:
        plan = Plan([main_tiles, late_tiles], 0, time_tiles, False, False, far_levels, tap_tiles)
        return between_chips(plan, [main, late])[0]
    plan = Plan([main_tiles], 0, early_tiles, False, True, far_levels, tap_tiles)
    out, *carried = between_chips(plan, [main])
    plan = Plan(
        [main_tiles, late_tiles], early_tiles, time_tiles - early_tiles, True, False, far_levels, tap_tiles
    )
    return between_chips(plan, [main, late], [*carried, out])[0]


def solution(mesh):
    in_specs = (P(("beams", "freq", "sub"), "tm"), P(), P())
    out_specs = P(("beams", "freq", "sub"), "tm")
    return jax.shard_map(local, mesh=mesh, in_specs=in_specs, out_specs=out_specs, check_vma=False)
```

time: 29.2 us -> 27 us (0.925)
  Pallas kernels: 12.7 us -> 9.33 us
  waiting for transfers between devices: 1.64 us -> 3.27 us
  starting transfers between devices: 12.7 us -> 12.3 us
    pallas_call x2, Pallas kernels: 7.81 us -> 4.21 us  [between_chips(): pl.pallas_call(functools.partial(trial_kernel, plan, group_count, level_c...]
    ppermute x7, waiting for transfers between devices: 1.64 us -> 3.26 us  [from_partner(): lax.ppermute(value, axis, [(source, source ^ mask) for source in range(co...]
    ppermute x7, starting transfers between devices: 10.1 us -> 9.65 us  [from_partner(): lax.ppermute(value, axis, [(source, source ^ mask) for source in range(co...]
  transfers between devices with their start and end apart: 9 -> 9, of which waited for: 1 -> 2; matrix products, arithmetic and copies ran while one was open for 3% -> 3% of each run, Pallas kernels for 30% -> 28%
where the time goes in v1:
time: 27 us; the launch traced here: 26.8 us
  starting transfers between devices  12.3 us (46%)
  Pallas kernels  9.33 us (35%)
  waiting for transfers between devices  3.27 us (12%)
  local copies, waits for them, and re-layouts  1.85 us (7%)
    ppermute x7, starting transfers between devices, from_partner(): lax.ppermute(value, axis, [(source, source ^ mask) for source in range(co...  9.65 us
    pallas_call x2, Pallas kernels, within_chip(): pl.pallas_call(functools.partial(chip_kernel, spans, out_tiles, group_cou...  5.12 us
    pallas_call x2, Pallas kernels, between_chips(): pl.pallas_call(functools.partial(trial_kernel, plan, group_count, level_c...  4.21 us
    ppermute x7, waiting for transfers between devices, from_partner(): lax.ppermute(value, axis, [(source, source ^ mask) for source in range(co...  3.26 us
    ppermute x2, starting transfers between devices, from_ahead(): return lax.ppermute(value, ('tm', 'sub'), route)  2.62 us
    unnamed x6, local copies, waits for them, and re-layouts  0.96 us
    slice x1, local copies, waits for them, and re-layouts, local(): ahead = filterbank[:, :take_len]  0.9 us
  transfers between devices with their start and end apart: 9, of which 2 were waited for; matrix products, arithmetic and copies ran while one was open for 3% of the time, Pallas kernels for 28%

profile of v1, /device:TPU:0, one launch (start us, length us, event | category | flops | bytes accessed | tf_op | source)
XLA Modules:
  0.0 26.8 jit_solution(9990495371334552447)
XLA Ops:
  0.0 0.5 %collective-permute-start = (bf16[64,2048]{1,0:T(8,128)(2,1)}, bf16[64,2048]{1,0:T(8,128)(2,1)S(1)}, u32[]{:S(2)}, u32[]{:S(2)}) collective-permute-start(bf16[64,2048]{1,0:T(8,128)(2,1)} %refs_0_.5), channel_id=1, source_target_pairs={{0,1},{1,0},{2,3},{3,2},{4,5},{5,4},{6,7},{7,6},{8,9},{9,8},{10,11... | collective-permute-start | bytes 786440 | tf_op jit(solution)/shard_map/ppermute | solution.py:45
  0.5 0.9 %slice.3 = bf16[64,768]{1,0:T(8,128)(2,1)S(1)} slice(bf16[64,2048]{1,0:T(8,128)(2,1)} %refs_0_.5), slice={[0:64], [0:768]} | slice | bytes 196608 | tf_op jit(solution)/shard_map/slice | solution.py:415
  1.4 2.6 %collective-permute-start.5 = (bf16[64,768]{1,0:T(8,128)(2,1)S(1)}, bf16[64,768]{1,0:T(8,128)(2,1)S(1)}, u32[]{:S(2)}, u32[]{:S(2)}) collective-permute-start(bf16[64,768]{1,0:T(8,128)(2,1)S(1)} %slice.3), channel_id=1, source_target_pairs={{2,1},{3,0},{0,3},{1,2},{6,5},{7,4},{4,7},{5,6},{10,9},{11,8},{8,1... | collective-permute-start | bytes 294920 | tf_op jit(solution)/shard_map/ppermute | solution.py:40
  4.0 0.0 collective-permute-start.4
  4.0 0.0 collective-permute-done.refs_1_.refs_2_
  4.0 0.0 copy-start
  4.0 0.9 %copy-done = bf16[64,2048]{1,0:T(8,128)(2,1)S(1)} copy-done((bf16[64,2048]{1,0:T(8,128)(2,1)S(1)}, bf16[64,2048]{1,0:T(8,128)(2,1)}, u32[]{:S(2)}) %copy-start) | copy-done | bytes 262168
  4.9 3.8 %shard_map.37 = (bf16[15,16,128]{2,1,0:T(8,128)(2,1)S(1)}, bf16[15,16,128]{2,1,0:T(8,128)(2,1)S(1)}, bf16[15,16,128]{2,1,0:T(8,128)(2,1)S(1)}, bf16[15,16,128]{2,1,0:T(8,128)(2,1)S(1)}) custom-call(s32[9,512]{1,0:T(8,128)S(1)} %copy-done.1, bf16[64,2048]{1,0:T(8,128)(2,1)S(1)} %copy-done, bf16[64,2048]{1,0:T(8,128)(2,1)S(1)} %collective-permute-done.refs_1_.refs_2_), custom_call_target="tpu_custom_call" | custom-call | tf_op jit(solution)/shard_map/pallas_call | solution.py:348
  8.8 2.2 %collective-permute-start.1 = (bf16[15,16,128]{2,1,0:T(8,128)(2,1)S(1)}, bf16[15,16,128]{2,1,0:T(8,128)(2,1)S(1)}, u32[]{:S(2)}, u32[]{:S(2)}) collective-permute-start(bf16[15,16,128]{2,1,0:T(8,128)(2,1)S(1)} %get-tuple-element.17), channel_id=1, source_target_pairs={{0,4},{4,0},{8,12},{12,8},{1,5},{5,1},{9,13},{13,9},{2,6},{6,2},{1... | collective-permute-start | bytes 184328 | tf_op jit(solution)/shard_map/ppermute | solution.py:45
  10.9 2.6 %collective-permute-start.2 = (bf16[15,16,128]{2,1,0:T(8,128)(2,1)S(1)}, bf16[15,16,128]{2,1,0:T(8,128)(2,1)S(1)}, u32[]{:S(2)}, u32[]{:S(2)}) collective-permute-start(bf16[15,16,128]{2,1,0:T(8,128)(2,1)S(1)} %get-tuple-element.18), channel_id=1, source_target_pairs={{0,8},{4,12},{8,0},{12,4},{1,9},{5,13},{9,1},{13,5},{2,10},{6,14},... | collective-permute-start | bytes 184328 | tf_op jit(solution)/shard_map/ppermute | solution.py:45
  13.5 0.0 collective-permute-start.3
  13.5 0.0 collective-permute-done.5.refs_3_
  13.5 0.0 collective-permute-done.4.refs_1_
  13.5 1.3 %shard_map.38 = (bf16[6,16,128]{2,1,0:T(8,128)(2,1)S(1)}, bf16[6,16,128]{2,1,0:T(8,128)(2,1)S(1)}, bf16[6,16,128]{2,1,0:T(8,128)(2,1)S(1)}, bf16[6,16,128]{2,1,0:T(8,128)(2,1)S(1)}) custom-call(s32[9,512]{1,0:T(8,128)S(1)} %copy-done.1, bf16[64,2048]{1,0:T(8,128)(2,1)S(1)} %copy-done, bf16[64,768]{1,0:T(8,128)(2,1)S(1)} %collective-permute-done.4.refs_1_, ...), custom_call_target="tpu_custom_call" | custom-call | tf_op jit(solution)/shard_map/pallas_call | solution.py:348
  14.8 0.0 copy-start.2
  14.8 1.0 %collective-permute-start.6 = (bf16[6,16,128]{2,1,0:T(8,128)(2,1)S(1)}, bf16[6,16,128]{2,1,0:T(8,128)(2,1)S(1)}, u32[]{:S(2)}, u32[]{:S(2)}) collective-permute-start(bf16[6,16,128]{2,1,0:T(8,128)(2,1)S(1)} %get-tuple-element.21), channel_id=1, source_target_pairs={{0,4},{4,0},{8,12},{12,8},{1,5},{5,1},{9,13},{13,9},{2,6},{6,2},{1... | collective-permute-start | bytes 73736 | tf_op jit(solution)/shard_map/ppermute | solution.py:45
  15.8 3.5 %collective-permute-start.7 = (bf16[6,16,128]{2,1,0:T(8,128)(2,1)S(1)}, bf16[6,16,128]{2,1,0:T(8,128)(2,1)S(1)}, u32[]{:S(2)}, u32[]{:S(2)}) collective-permute-start(bf16[6,16,128]{2,1,0:T(8,128)(2,1)S(1)} %get-tuple-element.22), channel_id=1, source_target_pairs={{0,8},{4,12},{8,0},{12,4},{1,9},{5,13},{9,1},{13,5},{2,10},{6,14},... | collective-permute-start | bytes 73736 | tf_op jit(solution)/shard_map/ppermute | solution.py:45
  19.3 0.0 collective-permute-start.8
  19.3 0.0 collective-permute-done.2.refs_4_
  19.3 0.5 %collective-permute-done.3.refs_5_ = bf16[15,16,128]{2,1,0:T(8,128)(2,1)S(1)} collective-permute-done((bf16[15,16,128]{2,1,0:T(8,128)(2,1)S(1)}, bf16[15,16,128]{2,1,0:T(8,128)(2,1)S(1)}, u32[]{:S(2)}, u32[]{:S(2)}) %collective-permute-start.3) | collective-permute-done | bytes 61472 | tf_op jit(solution)/shard_map/ppermute | solution.py:45
  19.8 2.3 %shard_map.39 = (f32[64,2048]{1,0:T(8,128)}, bf16[2,64,128]{2,1,0:T(8,128)(2,1)S(1)}, bf16[768,384]{1,0:T(8,128)(2,1)S(1)}) custom-call(s32[9,512]{1,0:T(8,128)S(1)} %copy-done.1, bf16[6,256]{1,0:T(8,128)(2,1)S(1)} %copy-done.2, bf16[15,16,128]{2,1,0:T(8,128)(2,1)S(1)} %get-tuple-element.16.refs_2_, bf16[15,16,128]{2,1,0:T(8,128)(2,1)S(1)} %collective-permute-done.1.refs_3_, ...), custom_call_target="tpu_custom_call" | custom-call | tf_op jit(solution)/shard_map/pallas_call | solution.py:390
  22.1 0.0 collective-permute-done.6.refs_7_
  22.1 2.8 %collective-permute-done.8.refs_9_ = bf16[6,16,128]{2,1,0:T(8,128)(2,1)S(1)} collective-permute-done((bf16[6,16,128]{2,1,0:T(8,128)(2,1)S(1)}, bf16[6,16,128]{2,1,0:T(8,128)(2,1)S(1)}, u32[]{:S(2)}, u32[]{:S(2)}) %collective-permute-start.8) | collective-permute-done | bytes 24608 | tf_op jit(solution)/shard_map/ppermute | solution.py:45
  24.9 1.9 %shard_map.40 = f32[64,2048]{1,0:T(8,128)} custom-call(s32[9,512]{1,0:T(8,128)S(1)} %copy-done.1, bf16[6,256]{1,0:T(8,128)(2,1)S(1)} %copy-done.2, bf16[15,16,128]{2,1,0:T(8,128)(2,1)S(1)} %get-tuple-element.16.refs_2_, bf16[15,16,128]{2,1,0:T(8,128)(2,1)S(1)} %collective-permute-done.1.refs_3_, ...), custom_call_target="tpu_custom_call", output_to_operand_aliasing={{}: (12, {})} | custom-call | tf_op jit(solution)/shard_map/pallas_call | solution.py:390
  (5 shorter events, 0.0 us)
Async XLA Ops:
  0.0 4.0 %copy-start.1 = (s32[9,512]{1,0:T(8,128)S(1)}, s32[9,512]{1,0:T(8,128)}, u32[]{:S(2)}) copy-start(s32[9,512]{1,0:T(8,128)} %refs_0_.7) | copy-start | bytes 55300
  0.0 4.0 %collective-permute-start = (bf16[64,2048]{1,0:T(8,128)(2,1)}, bf16[64,2048]{1,0:T(8,128)(2,1)S(1)}, u32[]{:S(2)}, u32[]{:S(2)}) collective-permute-start(bf16[64,2048]{1,0:T(8,128)(2,1)} %refs_0_.5), channel_id=1, source_target_pairs={{0,1},{1,0},{2,3},{3,2},{4,5},{5,4},{6,7},{7,6},{8,9},{9,8},{10,11... | collective-permute-start | bytes 786440 | tf_op jit(solution)/shard_map/ppermute | solution.py:45
  1.4 12.2 %collective-permute-start.5 = (bf16[64,768]{1,0:T(8,128)(2,1)S(1)}, bf16[64,768]{1,0:T(8,128)(2,1)S(1)}, u32[]{:S(2)}, u32[]{:S(2)}) collective-permute-start(bf16[64,768]{1,0:T(8,128)(2,1)S(1)} %slice.3), channel_id=1, source_target_pairs={{2,1},{3,0},{0,3},{1,2},{6,5},{7,4},{4,7},{5,6},{10,9},{11,8},{8,1... | collective-permute-start | bytes 294920 | tf_op jit(solution)/shard_map/ppermute | solution.py:40
  4.0 9.6 %collective-permute-start.4 = (bf16[64,768]{1,0:T(8,128)(2,1)S(1)}, bf16[64,768]{1,0:T(8,128)(2,1)S(1)}, u32[]{:S(2)}, u32[]{:S(2)}) collective-permute-start(bf16[64,768]{1,0:T(8,128)(2,1)S(1)} %slice.3), channel_id=1, source_target_pairs={{2,0},{3,1},{0,2},{1,3},{6,4},{7,5},{4,6},{5,7},{10,8},{11,9},{8,1... | collective-permute-start | bytes 294920 | tf_op jit(solution)/shard_map/ppermute | solution.py:40
  4.0 1.0 %copy-start = (bf16[64,2048]{1,0:T(8,128)(2,1)S(1)}, bf16[64,2048]{1,0:T(8,128)(2,1)}, u32[]{:S(2)}) copy-start(bf16[64,2048]{1,0:T(8,128)(2,1)} %refs_0_.5) | copy-start | bytes 786436
  8.8 10.5 %collective-permute-start.1 = (bf16[15,16,128]{2,1,0:T(8,128)(2,1)S(1)}, bf16[15,16,128]{2,1,0:T(8,128)(2,1)S(1)}, u32[]{:S(2)}, u32[]{:S(2)}) collective-permute-start(bf16[15,16,128]{2,1,0:T(8,128)(2,1)S(1)} %get-tuple-element.17), channel_id=1, source_target_pairs={{0,4},{4,0},{8,12},{12,8},{1,5},{5,1},{9,13},{13,9},{2,6},{6,2},{1... | collective-permute-start | bytes 184328 | tf_op jit(solution)/shard_map/ppermute | solution.py:45
  10.9 8.4 %collective-permute-start.2 = (bf16[15,16,128]{2,1,0:T(8,128)(2,1)S(1)}, bf16[15,16,128]{2,1,0:T(8,128)(2,1)S(1)}, u32[]{:S(2)}, u32[]{:S(2)}) collective-permute-start(bf16[15,16,128]{2,1,0:T(8,128)(2,1)S(1)} %get-tuple-element.18), channel_id=1, source_target_pairs={{0,8},{4,12},{8,0},{12,4},{1,9},{5,13},{9,1},{13,5},{2,10},{6,14},... | collective-permute-start | bytes 184328 | tf_op jit(solution)/shard_map/ppermute | solution.py:45
  13.5 6.3 %collective-permute-start.3 = (bf16[15,16,128]{2,1,0:T(8,128)(2,1)S(1)}, bf16[15,16,128]{2,1,0:T(8,128)(2,1)S(1)}, u32[]{:S(2)}, u32[]{:S(2)}) collective-permute-start(bf16[15,16,128]{2,1,0:T(8,128)(2,1)S(1)} %get-tuple-element.19), channel_id=1, source_target_pairs={{0,12},{4,8},{8,4},{12,0},{1,13},{5,9},{9,5},{13,1},{2,14},{6,10},... | collective-permute-start | bytes 184328 | tf_op jit(solution)/shard_map/ppermute | solution.py:45
  14.8 5.0 %copy-start.2 = (bf16[6,256]{1,0:T(8,128)(2,1)S(1)}, bf16[6,256]{1,0:T(8,128)(2,1)}, u32[]{:S(2)}) copy-start(bf16[6,256]{1,0:T(8,128)(2,1)} %refs_1_.3) | copy-start | bytes 9220
  14.8 7.3 %collective-permute-start.6 = (bf16[6,16,128]{2,1,0:T(8,128)(2,1)S(1)}, bf16[6,16,128]{2,1,0:T(8,128)(2,1)S(1)}, u32[]{:S(2)}, u32[]{:S(2)}) collective-permute-start(bf16[6,16,128]{2,1,0:T(8,128)(2,1)S(1)} %get-tuple-element.21), channel_id=1, source_target_pairs={{0,4},{4,0},{8,12},{12,8},{1,5},{5,1},{9,13},{13,9},{2,6},{6,2},{1... | collective-permute-start | bytes 73736 | tf_op jit(solution)/shard_map/ppermute | solution.py:45
  15.8 6.3 %collective-permute-start.7 = (bf16[6,16,128]{2,1,0:T(8,128)(2,1)S(1)}, bf16[6,16,128]{2,1,0:T(8,128)(2,1)S(1)}, u32[]{:S(2)}, u32[]{:S(2)}) collective-permute-start(bf16[6,16,128]{2,1,0:T(8,128)(2,1)S(1)} %get-tuple-element.22), channel_id=1, source_target_pairs={{0,8},{4,12},{8,0},{12,4},{1,9},{5,13},{9,1},{13,5},{2,10},{6,14},... | collective-permute-start | bytes 73736 | tf_op jit(solution)/shard_map/ppermute | solution.py:45
  19.3 5.6 %collective-permute-start.8 = (bf16[6,16,128]{2,1,0:T(8,128)(2,1)S(1)}, bf16[6,16,128]{2,1,0:T(8,128)(2,1)S(1)}, u32[]{:S(2)}, u32[]{:S(2)}) collective-permute-start(bf16[6,16,128]{2,1,0:T(8,128)(2,1)S(1)} %get-tuple-element.23), channel_id=1, source_target_pairs={{0,12},{4,8},{8,4},{12,0},{1,13},{5,9},{9,5},{13,1},{2,14},{6,10},... | collective-permute-start | bytes 73736 | tf_op jit(solution)/shard_map/ppermute | solution.py:45

commit v2 on v1

--- a/solution.py
+++ b/solution.py
@@ -43,6 +43,27 @@
 def from_partner(value, axis, mask):
     count = lax.axis_size(axis)
     return lax.ppermute(value, axis, [(source, source ^ mask) for source in range(count)])
+
+
+def mask_orders(group_count):
+    order = list(range(group_count - 1, 0, -1))
+    return order, order[-1:] + order[:-1]
+
+
+def step_masks(group_count, core):
+    orders = mask_orders(group_count)
+    return [0] + [jnp.where(core == 0, first, second) for first, second in zip(*orders)]
+
+
+def exchanged(blocks):
+    count = lax.axis_size("freq")
+    received = [blocks[0]]
+    for block, masks in zip(blocks[1:], zip(*mask_orders(count))):
+        route = [
+            (chip * 2 + core, (chip ^ masks[core]) * 2 + core) for chip in range(count) for core in range(2)
+        ]
+        received.append(lax.ppermute(block, ("freq", "sub"), route))
+    return received
 
 
 def lanes():
@@ -70,16 +91,15 @@
             moved = moved + (amount >> bits_of(LANES))
         masks = [moved == offset for offset in range(1, apart + 1)]
         chosen.append((masks, lane + part & LANES - 1, place))
-    upper = [source[offset, high, :] for offset in range(apart)]
-    for tile in range(tiles):
-        upper.append(source[tile + apart, high, :])
-        lower = source[tile, low, :]
-        for masks, index, place in chosen:
+    for masks, index, place in chosen:
+        upper = [source[offset, high, :] for offset in range(apart)]
+        for tile in range(tiles):
+            upper.append(source[tile + apart, high, :])
             mixed = upper[0]
             for mask, other in zip(masks, upper[1:]):
                 mixed = jnp.where(mask, other, mixed)
-            target[tile, place, :] = lower + gathered(mixed, index)
-        upper = upper[1:]
+            target[tile, place, :] = source[tile, low, :] + gathered(mixed, index)
+            upper = upper[1:]
 
 
 def tree_levels(state, other, columns, first, levels, held, lengths):
@@ -151,6 +171,27 @@
     return [made + -(-sum(2**later for later in levels if later > level) // LANES) for level in levels]
 
 
+def load_kernel(whole, copied, ahead):
+    copied[...] = whole[...]
+    ahead[...] = whole[:, : ahead.shape[1]]
+
+
+def placed(target, blocks, tiles, skip):
+    chip, core = lax.axis_index("freq"), lax.axis_index("sub")
+    rows = blocks[0].shape[1]
+    for mask, block in zip(step_masks(len(blocks), core), blocks):
+        start = pl.multiple_of((chip ^ mask) * rows, rows)
+        for tile in range(skip, tiles):
+            target[tile - skip, pl.ds(start, rows), :] = block[tile, :, :].astype(jnp.float32)
+
+
+def gather_kernel(*refs):
+    *blocks, out, state = refs
+    placed(state, blocks, out.shape[0], 0)
+    for tile in range(out.shape[0]):
+        out[tile, :, :] = state[tile, :, :].astype(jnp.bfloat16)
+
+
 def chip_kernel(spans, out_tiles, group_count, shifts, *refs):
     pieces = (refs[: len(spans)], refs[len(spans) : 2 * len(spans)])
     blocks = refs[2 * len(spans) : 2 * len(spans) + group_count]
@@ -178,22 +219,19 @@
             raw[later, pl.ds(place, chan_rows), :] = jnp.zeros((chan_rows, LANES), jnp.float32)
     levels = list(range(local_count + 1))
     lengths = lengths_of(out_tiles, levels)
+    mask = lanes() >= core
     for vector in range(SUBLANES):
-        column = columns[pl.ds(vector, SUBLANES, stride=SUBLANES), :]
-        amount = jnp.broadcast_to(column[:, 0:1], (SUBLANES, LANES)).astype(jnp.int32)
-        merge(
-            raw,
-            ping,
-            pl.ds(2 * vector, SUBLANES, stride=2 * SUBLANES),
-            pl.ds(2 * vector + 1, SUBLANES, stride=2 * SUBLANES),
-            [(amount, pl.ds(vector, SUBLANES, stride=SUBLANES))],
-            lengths[0],
-            1,
-        )
+        low, high = [pl.ds(2 * vector + odd, SUBLANES, stride=2 * SUBLANES) for odd in range(2)]
+        upper = raw[0, high, :]
+        for tile in range(lengths[0]):
+            later = raw[tile + 1, high, :]
+            moved = pltpu.roll(jnp.where(mask, upper, later), LANES - core & LANES - 1, 1)
+            ping[tile, pl.ds(vector, SUBLANES, stride=SUBLANES), :] = raw[tile, low, :] + moved
+            upper = later
     last = tree_levels(ping, pong, columns, 1, levels[1:], 1, lengths[1:])
     size = chan_rows // group_count
     own = reversed_bits(chip, bits_of(group_count))
-    for mask, block in enumerate(blocks):
+    for mask, block in zip(step_masks(group_count, core), blocks):
         start = pl.multiple_of((own ^ reversed_bits(mask, bits_of(group_count))) * size, size)
         for tile in range(out_tiles):
             block[tile, :, :] = last[tile, pl.ds(start, size), :].astype(jnp.bfloat16)
@@ -220,10 +258,8 @@
 
 def trial_kernel(plan, group_count, level_count, *refs):
     shifts, filters, refs = refs[0], refs[1], refs[2:]
-    parts = []
-    for _ in plan.tile_counts:
-        parts.append(refs[:group_count])
-        refs = refs[group_count:]
+    blocks, refs = refs[:group_count], refs[group_count:]
+    halos, refs = refs[: len(plan.halos)], refs[len(plan.halos) :]
     if plan.taken:
         carried, taps, so_far, refs = refs[0], refs[1], refs[2], refs[3:]
     out, refs = refs[0], refs[1:]
@@ -253,14 +289,15 @@
     transposed_table(rows, table, columns)
     if not plan.taken:
         toeplitz(filters, taps)
-    at = 0
-    for index, (blocks, tiles) in enumerate(zip(parts, plan.tile_counts)):
-        skip = plan.first if index == 0 else 0
-        for mask, block in enumerate(blocks):
-            start = pl.multiple_of((chip ^ mask) * block_rows, block_rows)
-            for tile in range(skip, tiles):
-                state[at + tile - skip, pl.ds(start, block_rows), :] = block[tile, :, :].astype(jnp.float32)
-        at += tiles - skip
+    placed(state, blocks, plan.main_tiles, plan.first)
+    at = plan.main_tiles - plan.first
+    for hop, (halo, tiles) in enumerate(zip(halos, plan.halos), 1):
+        there = lax.axis_index("tm") + hop < lax.axis_size("tm")
+        for tile in range(tiles):
+            state[at, :, :] = jnp.where(there, halo[tile, :, :].astype(jnp.float32), 0.0)
+            at += 1
+    for tile in range(at, at + plan.empty_tiles):
+        state[tile, :, :] = jnp.zeros((chan_rows, LANES), jnp.float32)
     last = tree_levels(state, other, columns, 0, levels, block_rows, plan.lengths)
     scale = 1.0 / math.sqrt(shifts.shape[1])
     kept = tap_count // LANES
@@ -306,8 +343,8 @@
 
 
 class Plan:
-    def __init__(self, tile_counts, out_first, out_tiles, taken, given, levels, tap_tiles):
-        self.tile_counts = tile_counts
+    def __init__(self, main_tiles, halos, empty_tiles, out_first, out_tiles, taken, given, levels, tap_tiles):
+        self.main_tiles, self.halos, self.empty_tiles = main_tiles, halos, empty_tiles
         self.out_first, self.out_tiles = out_first, out_tiles
         self.taken, self.given = taken, given
         self.made = out_tiles if taken else out_tiles + tap_tiles
@@ -316,7 +353,7 @@
         turns = -(-out_tiles // 6)
         ends = [out_tiles * turn // turns for turn in range(turns + 1)]
         self.chunks = [(start, end - start) for start, end in zip(ends, ends[1:])]
-        self.state_tiles = sum(tile_counts) - self.first + max(2 ** levels[-1] // LANES, 1) + 1
+        self.state_tiles = main_tiles + sum(halos) + empty_tiles - self.first + max(2 ** levels[-1] // LANES, 1) + 1
 
 
 def local(filterbank, delay_shifts, pulse_filters):
@@ -329,12 +366,8 @@
     time_tiles = time_len // LANES
     far_levels = range(level_count - bits_of(group_count), level_count)
     near_reach = 2 ** far_levels[0] - 1
-    margin_len = rounded_up(2**level_count - 1 + tap_count, LANES)
-    main_tiles = time_tiles - -(-near_reach // LANES)
-    whole_tiles = (time_len + rounded_up(2**level_count - 1 - near_reach + tap_count, LANES)) // LANES
-    late_tiles = whole_tiles - main_tiles
-    late_len = margin_len + time_len - main_tiles * LANES
-    hop_count = min(lax.axis_size("tm") - 1, -(-margin_len // time_len))
+    near_len = rounded_up(near_reach, LANES)
+    far_tiles = -(-(2**level_count - 1 - near_reach + tap_count) // LANES)
 
     in_vmem = pl.BlockSpec(memory_space=pltpu.VMEM)
     in_any = pl.BlockSpec(memory_space=pl.ANY)
@@ -360,16 +393,10 @@
             compiler_params=params,
         )(delay_shifts, *own, *other)
 
-    def exchanged(blocks):
-        order = sorted(range(1, group_count), key=lambda mask: -mask)
-        received = {mask: from_partner(blocks[mask], "freq", mask) for mask in order}
-        return [blocks[0]] + [received[mask] for mask in range(1, group_count)]
-
-    def between_chips(plan, parts, carried=()):
+    def between_chips(plan, blocks, halos, carried=()):
         state = pltpu.VMEM((plan.state_tiles, chan_rows, LANES), jnp.float32)
         taps = ((width_count * LANES, tap_count + LANES), jnp.bfloat16)
-        operands = [delay_shifts, pulse_filters] + [block for blocks in parts for block in blocks]
-        operands += carried
+        operands = [delay_shifts, pulse_filters, *blocks, *halos, *carried]
         in_specs = [in_vmem] * len(operands)
         aliases = {}
         if plan.taken:
@@ -408,32 +435,50 @@
         )(*operands)
 
     other_core = from_partner(filterbank, "sub", 1)
-    halos, spans = ([], []), [(main_tiles * LANES, time_len - main_tiles * LANES, 0)]
-    collected = 0
-    for hop in range(1, hop_count + 1):
-        take_len = min(time_len, margin_len - collected)
-        ahead = filterbank[:, :take_len]
+    own, ahead = pl.pallas_call(
+        load_kernel,
+        out_shape=[
+            jax.ShapeDtypeStruct(filterbank.shape, filterbank.dtype),
+            jax.ShapeDtypeStruct((chan_rows, near_len), filterbank.dtype),
+        ],
+        in_specs=[in_vmem],
+        out_specs=[in_vmem] * 2,
+        compiler_params=params,
+    )(filterbank)
+    both, spans = ([own], [other_core]), [(0, time_len, 0)]
+    if lax.axis_size("tm") > 1:
         for crossed in range(2):
-            halos[crossed].append(from_ahead(ahead, hop, crossed))
-        spans.append((0, take_len, hop))
-        collected += take_len
-    main = within_chip([filterbank], [other_core], [(0, time_len, 0)], time_tiles, main_tiles)
-    main = exchanged(main)
-    late = within_chip(
-        [filterbank] + halos[0], [other_core] + halos[1], spans, late_len // LANES, late_tiles
-    )
-    late = exchanged(late)
+            both[crossed].append(from_ahead(ahead, 1, crossed))
+        spans.append((0, near_len, 1))
+    main = exchanged(within_chip(*both, spans, time_tiles + near_len // LANES, time_tiles))
+
+    halos, takes = [], []
+    rest = far_tiles
+    if lax.axis_size("tm") > 1:
+        first_tiles = min(time_tiles, far_tiles)
+        gathered_rows = pl.pallas_call(
+            gather_kernel,
+            out_shape=jax.ShapeDtypeStruct((first_tiles, chan_rows, LANES), jnp.bfloat16),
+            in_specs=[in_vmem] * group_count,
+            out_specs=in_vmem,
+            scratch_shapes=[pltpu.VMEM((first_tiles, chan_rows, LANES), jnp.float32)],
+            compiler_params=params,
+        )(*main)
+        for hop in range(1, lax.axis_size("tm")):
+            if rest > 0:
+                takes.append(min(time_tiles, rest))
+                halos.append(from_ahead(gathered_rows[: takes[-1]], hop, 0))
+                rest -= takes[-1]
     lost = -(-sum(2**level for level in far_levels) // LANES) + tap_tiles
-    early_tiles = main_tiles - lost
+    early_tiles = time_tiles - lost
     if early_tiles <= 0:
-        plan = Plan([main_tiles, late_tiles], 0, time_tiles, False, False, far_levels, tap_tiles)
-        return between_chips(plan, [main, late])[0]
-    plan = Plan([main_tiles], 0, early_tiles, False, True, far_levels, tap_tiles)
-    out, *carried = between_chips(plan, [main])
-    plan = Plan(
-        [main_tiles, late_tiles], early_tiles, time_tiles - early_tiles, True, False, far_levels, tap_tiles
-    )
-    return between_chips(plan, [main, late], [*carried, out])[0]
+        plan = Plan(time_tiles, takes, rest, 0, time_tiles, False, False, far_levels, tap_tiles)
+        return between_chips(plan, main, halos)[0]
+    plan = Plan(time_tiles, [], 0, 0, early_tiles, False, True, far_levels, tap_tiles)
+    out, *carried = between_chips(plan, main, [])
+    late_tiles = time_tiles - early_tiles
+    plan = Plan(time_tiles, takes, rest, early_tiles, late_tiles, True, False, far_levels, tap_tiles)
+    return between_chips(plan, main, halos, [*carried, out])[0]
 
 
 def solution(mesh):

time: 27 us -> 27.1 us (level)
  waiting for transfers between devices: 3.27 us -> 10.1 us
  starting transfers between devices: 12.3 us -> 8.37 us
  Pallas kernels: 9.33 us -> 7.45 us
  local copies, waits for them, and re-layouts: 1.85 us -> 0.96 us
    ppermute x7 -> x1, starting transfers between devices: 9.65 us -> 0.45 us  [from_partner(): lax.ppermute(value, axis, [(source, source ^ mask) for source in range(co...]
    ppermute x0 -> x3, waiting for transfers between devices: none -> 5.07 us  [exchanged(): received.append(lax.ppermute(block, ('freq', 'sub'), route))]
    ppermute x2 -> x3, waiting for transfers between devices: 0.01 us -> 5.02 us  [from_ahead(): return lax.ppermute(value, ('tm', 'sub'), route)]
    ppermute x0 -> x3, starting transfers between devices: none -> 4.45 us  [exchanged(): received.append(lax.ppermute(block, ('freq', 'sub'), route))]
    ppermute x7 -> x1, waiting for transfers between devices: 3.26 us -> 0.01 us  [from_partner(): lax.ppermute(value, axis, [(source, source ^ mask) for source in range(co...]
    pallas_call x2 -> x1, Pallas kernels: 5.12 us -> 3.23 us  [within_chip(): pl.pallas_call(functools.partial(chip_kernel, spans, out_tiles, group_cou...]
    slice x1 -> x0, local copies, waits for them, and re-layouts: 0.9 us -> none  [local(): ahead = filterbank[:, :take_len]]
    ppermute x2 -> x3, starting transfers between devices: 2.62 us -> 3.46 us  [from_ahead(): return lax.ppermute(value, ('tm', 'sub'), route)]
  transfers between devices with their start and end apart: 9 -> 7, of which waited for: 2 -> 5; matrix products, arithmetic and copies ran while one was open for 3% -> 0% of each run, Pallas kernels for 28% -> 9%
where the time goes in v2:
time: 27.1 us; the launch traced here: 26.9 us
  waiting for transfers between devices  10.1 us (37%)
  starting transfers between devices  8.37 us (31%)
  Pallas kernels  7.45 us (27%)
  local copies, waits for them, and re-layouts  0.96 us (4%)
    ppermute x3, waiting for transfers between devices, exchanged(): received.append(lax.ppermute(block, ('freq', 'sub'), route))  5.07 us
    ppermute x3, waiting for transfers between devices, from_ahead(): return lax.ppermute(value, ('tm', 'sub'), route)  5.02 us
    ppermute x3, starting transfers between devices, exchanged(): received.append(lax.ppermute(block, ('freq', 'sub'), route))  4.45 us
    pallas_call x2, Pallas kernels, between_chips(): pl.pallas_call(functools.partial(trial_kernel, plan, group_count, level_c...  4.17 us
    ppermute x3, starting transfers between devices, from_ahead(): return lax.ppermute(value, ('tm', 'sub'), route)  3.46 us
    pallas_call x1, Pallas kernels, within_chip(): pl.pallas_call(functools.partial(chip_kernel, spans, out_tiles, group_cou...  3.23 us
    unnamed x6, local copies, waits for them, and re-layouts  0.96 us
  transfers between devices with their start and end apart: 7, of which 5 were waited for; matrix products, arithmetic and copies ran while one was open for 0% of the time, Pallas kernels for 9%

profile of v2, /device:TPU:0, one launch (start us, length us, event | category | flops | bytes accessed | tf_op | source)
XLA Modules:
  0.0 26.9 jit_solution(11823509204459906787)
XLA Ops:
  0.0 0.0 copy-start
  0.0 0.5 %collective-permute-start.1 = (bf16[64,2048]{1,0:T(8,128)(2,1)}, bf16[64,2048]{1,0:T(8,128)(2,1)S(1)}, u32[]{:S(2)}, u32[]{:S(2)}) collective-permute-start(bf16[64,2048]{1,0:T(8,128)(2,1)} %whole.1), channel_id=1, source_target_pairs={{0,1},{1,0},{2,3},{3,2},{4,5},{5,4},{6,7},{7,6},{8,9},{9,8},{10,11... | collective-permute-start | bytes 786440 | tf_op jit(solution)/shard_map/ppermute | solution.py:45
  0.5 0.0 copy-start.1
  0.5 0.9 %copy-done.1 = bf16[64,2048]{1,0:T(8,128)(2,1)S(1)} copy-done((bf16[64,2048]{1,0:T(8,128)(2,1)S(1)}, bf16[64,2048]{1,0:T(8,128)(2,1)}, u32[]{:S(2)}) %copy-start.1) | copy-done | bytes 262168
  1.4 2.7 %collective-permute-start.2 = (bf16[64,128]{1,0:T(8,128)(2,1)S(1)}, bf16[64,128]{1,0:T(8,128)(2,1)S(1)}, u32[]{:S(2)}, u32[]{:S(2)}) collective-permute-start(bf16[64,128]{1,0:T(8,128)(2,1)S(1)} %get-tuple-element.15), channel_id=1, source_target_pairs={{2,1},{3,0},{0,3},{1,2},{6,5},{7,4},{4,7},{5,6},{10,9},{11,8},{8,1... | collective-permute-start | bytes 49160 | tf_op jit(solution)/shard_map/ppermute | solution.py:40
  4.1 0.0 collective-permute-start
  4.1 1.4 %collective-permute-done.2.refs_3_ = bf16[64,128]{1,0:T(8,128)(2,1)S(1)} collective-permute-done((bf16[64,128]{1,0:T(8,128)(2,1)S(1)}, bf16[64,128]{1,0:T(8,128)(2,1)S(1)}, u32[]{:S(2)}, u32[]{:S(2)}) %collective-permute-start.2) | collective-permute-done | bytes 16416 | tf_op jit(solution)/shard_map/ppermute | solution.py:40
  5.6 2.3 %collective-permute-done.refs_1_ = bf16[64,128]{1,0:T(8,128)(2,1)S(1)} collective-permute-done((bf16[64,128]{1,0:T(8,128)(2,1)S(1)}, bf16[64,128]{1,0:T(8,128)(2,1)S(1)}, u32[]{:S(2)}, u32[]{:S(2)}) %collective-permute-start) | collective-permute-done | bytes 16416 | tf_op jit(solution)/shard_map/ppermute | solution.py:40
  7.9 0.0 collective-permute-done.1.refs_2_
  7.9 0.0 copy-done
  7.9 3.2 %shard_map.38 = (bf16[16,16,128]{2,1,0:T(8,128)(2,1)S(1)}, bf16[16,16,128]{2,1,0:T(8,128)(2,1)S(1)}, bf16[16,16,128]{2,1,0:T(8,128)(2,1)S(1)}, bf16[16,16,128]{2,1,0:T(8,128)(2,1)S(1)}) custom-call(s32[9,512]{1,0:T(8,128)S(1)} %copy-done, bf16[64,2048]{1,0:T(8,128)(2,1)S(1)} %get-tuple-element.14.refs_0_, bf16[64,128]{1,0:T(8,128)(2,1)S(1)} %collective-permute-done.refs_1_, ...), custom_call_target="tpu_custom_call" | custom-call | tf_op jit(solution)/shard_map/pallas_call | solution.py:381
  11.1 3.7 %collective-permute-start.3 = (bf16[16,16,128]{2,1,0:T(8,128)(2,1)S(1)}, bf16[16,16,128]{2,1,0:T(8,128)(2,1)S(1)}, u32[]{:S(2)}, u32[]{:S(2)}) collective-permute-start(bf16[16,16,128]{2,1,0:T(8,128)(2,1)S(1)} %get-tuple-element.17), channel_id=1, source_target_pairs={{0,12},{1,5},{4,8},{5,1},{8,4},{9,13},{12,0},{13,9},{2,14},{3,7},{... | collective-permute-start | bytes 196616 | tf_op jit(solution)/shard_map/ppermute | solution.py:65
  14.8 0.0 collective-permute-start.4
  14.8 0.8 %collective-permute-start.5 = (bf16[16,16,128]{2,1,0:T(8,128)(2,1)S(1)}, bf16[16,16,128]{2,1,0:T(8,128)(2,1)S(1)}, u32[]{:S(2)}, u32[]{:S(2)}) collective-permute-start(bf16[16,16,128]{2,1,0:T(8,128)(2,1)S(1)} %get-tuple-element.19), channel_id=1, source_target_pairs={{0,4},{1,9},{4,0},{5,13},{8,12},{9,1},{12,8},{13,5},{2,6},{3,11},{... | collective-permute-start | bytes 196616 | tf_op jit(solution)/shard_map/ppermute | solution.py:65
  15.6 1.9 %collective-permute-done.3.refs_1_.refs_3_ = bf16[16,16,128]{2,1,0:T(8,128)(2,1)S(1)} collective-permute-done((bf16[16,16,128]{2,1,0:T(8,128)(2,1)S(1)}, bf16[16,16,128]{2,1,0:T(8,128)(2,1)S(1)}, u32[]{:S(2)}, u32[]{:S(2)}) %collective-permute-start.3) | collective-permute-done | bytes 65568 | tf_op jit(solution)/shard_map/ppermute | solution.py:65
  17.4 3.2 %collective-permute-done.4.refs_2_.refs_4_ = bf16[16,16,128]{2,1,0:T(8,128)(2,1)S(1)} collective-permute-done((bf16[16,16,128]{2,1,0:T(8,128)(2,1)S(1)}, bf16[16,16,128]{2,1,0:T(8,128)(2,1)S(1)}, u32[]{:S(2)}, u32[]{:S(2)}) %collective-permute-start.4) | collective-permute-done | bytes 65568 | tf_op jit(solution)/shard_map/ppermute | solution.py:65
  20.6 0.0 collective-permute-done.5.refs_3_.refs_5_
  20.6 0.0 copy-start.2
  20.7 0.8 %collective-permute-start.6 = (bf16[5,64,128]{2,1,0:T(8,128)(2,1)S(1)}, bf16[5,64,128]{2,1,0:T(8,128)(2,1)S(1)}, u32[]{:S(2)}, u32[]{:S(2)}) collective-permute-start(bf16[5,64,128]{2,1,0:T(8,128)(2,1)S(1)} %shard_map.39), channel_id=1, source_target_pairs={{2,0},{3,1},{0,2},{1,3},{6,4},{7,5},{4,6},{5,7},{10,8},{11,9},{8,1... | collective-permute-start | bytes 245768 | tf_op jit(solution)/shard_map/ppermute | solution.py:40
  21.4 0.0 copy-done.2
  21.4 2.4 %shard_map.40 = (f32[64,2048]{1,0:T(8,128)}, bf16[2,64,128]{2,1,0:T(8,128)(2,1)S(1)}, bf16[768,384]{1,0:T(8,128)(2,1)S(1)}) custom-call(s32[9,512]{1,0:T(8,128)S(1)} %copy-done, bf16[6,256]{1,0:T(8,128)(2,1)S(1)} %copy-done.2, bf16[16,16,128]{2,1,0:T(8,128)(2,1)S(1)} %get-tuple-element.16.refs_0_.refs_2_, ...), custom_call_target="tpu_custom_call" | custom-call | tf_op jit(solution)/shard_map/pallas_call | solution.py:417
  23.9 1.3 %collective-permute-done.6.refs_6_ = bf16[5,64,128]{2,1,0:T(8,128)(2,1)S(1)} collective-permute-done((bf16[5,64,128]{2,1,0:T(8,128)(2,1)S(1)}, bf16[5,64,128]{2,1,0:T(8,128)(2,1)S(1)}, u32[]{:S(2)}, u32[]{:S(2)}) %collective-permute-start.6) | collective-permute-done | bytes 81952 | tf_op jit(solution)/shard_map/ppermute | solution.py:40
  25.2 1.7 %shard_map.41 = f32[64,2048]{1,0:T(8,128)} custom-call(s32[9,512]{1,0:T(8,128)S(1)} %copy-done, bf16[6,256]{1,0:T(8,128)(2,1)S(1)} %copy-done.2, bf16[16,16,128]{2,1,0:T(8,128)(2,1)S(1)} %get-tuple-element.16.refs_0_.refs_2_, bf16[16,16,128]{2,1,0:T(8,128)(2,1)S(1)} %collective-permute-done.3.refs_1_.refs_3_, ...), custom_call_target="tpu_custom_call", output_to_operand_aliasing={{}: (9, {})} | custom-call | tf_op jit(solution)/shard_map/pallas_call | solution.py:417
  (2 shorter events, 0.1 us)
Async XLA Ops:
  0.0 7.9 %copy-start = (s32[9,512]{1,0:T(8,128)S(1)}, s32[9,512]{1,0:T(8,128)}, u32[]{:S(2)}) copy-start(s32[9,512]{1,0:T(8,128)} %refs_0_.3) | copy-start | bytes 55300
  0.0 7.9 %collective-permute-start.1 = (bf16[64,2048]{1,0:T(8,128)(2,1)}, bf16[64,2048]{1,0:T(8,128)(2,1)S(1)}, u32[]{:S(2)}, u32[]{:S(2)}) collective-permute-start(bf16[64,2048]{1,0:T(8,128)(2,1)} %whole.1), channel_id=1, source_target_pairs={{0,1},{1,0},{2,3},{3,2},{4,5},{5,4},{6,7},{7,6},{8,9},{9,8},{10,11... | collective-permute-start | bytes 786440 | tf_op jit(solution)/shard_map/ppermute | solution.py:45
  0.5 0.9 %copy-start.1 = (bf16[64,2048]{1,0:T(8,128)(2,1)S(1)}, bf16[64,2048]{1,0:T(8,128)(2,1)}, u32[]{:S(2)}) copy-start(bf16[64,2048]{1,0:T(8,128)(2,1)} %whole.1) | copy-start | bytes 786436
  1.4 4.1 %collective-permute-start.2 = (bf16[64,128]{1,0:T(8,128)(2,1)S(1)}, bf16[64,128]{1,0:T(8,128)(2,1)S(1)}, u32[]{:S(2)}, u32[]{:S(2)}) collective-permute-start(bf16[64,128]{1,0:T(8,128)(2,1)S(1)} %get-tuple-element.15), channel_id=1, source_target_pairs={{2,1},{3,0},{0,3},{1,2},{6,5},{7,4},{4,7},{5,6},{10,9},{11,8},{8,1... | collective-permute-start | bytes 49160 | tf_op jit(solution)/shard_map/ppermute | solution.py:40
  4.1 3.7 %collective-permute-start = (bf16[64,128]{1,0:T(8,128)(2,1)S(1)}, bf16[64,128]{1,0:T(8,128)(2,1)S(1)}, u32[]{:S(2)}, u32[]{:S(2)}) collective-permute-start(bf16[64,128]{1,0:T(8,128)(2,1)S(1)} %get-tuple-element.15), channel_id=1, source_target_pairs={{2,0},{3,1},{0,2},{1,3},{6,4},{7,5},{4,6},{5,7},{10,8},{11,9},{8,1... | collective-permute-start | bytes 49160 | tf_op jit(solution)/shard_map/ppermute | solution.py:40
  11.1 6.3 %collective-permute-start.3 = (bf16[16,16,128]{2,1,0:T(8,128)(2,1)S(1)}, bf16[16,16,128]{2,1,0:T(8,128)(2,1)S(1)}, u32[]{:S(2)}, u32[]{:S(2)}) collective-permute-start(bf16[16,16,128]{2,1,0:T(8,128)(2,1)S(1)} %get-tuple-element.17), channel_id=1, source_target_pairs={{0,12},{1,5},{4,8},{5,1},{8,4},{9,13},{12,0},{13,9},{2,14},{3,7},{... | collective-permute-start | bytes 196616 | tf_op jit(solution)/shard_map/ppermute | solution.py:65
  14.8 5.9 %collective-permute-start.4 = (bf16[16,16,128]{2,1,0:T(8,128)(2,1)S(1)}, bf16[16,16,128]{2,1,0:T(8,128)(2,1)S(1)}, u32[]{:S(2)}, u32[]{:S(2)}) collective-permute-start(bf16[16,16,128]{2,1,0:T(8,128)(2,1)S(1)} %get-tuple-element.18), channel_id=1, source_target_pairs={{0,8},{1,13},{4,12},{5,9},{8,0},{9,5},{12,4},{13,1},{2,10},{3,15},... | collective-permute-start | bytes 196616 | tf_op jit(solution)/shard_map/ppermute | solution.py:65
  14.8 5.9 %collective-permute-start.5 = (bf16[16,16,128]{2,1,0:T(8,128)(2,1)S(1)}, bf16[16,16,128]{2,1,0:T(8,128)(2,1)S(1)}, u32[]{:S(2)}, u32[]{:S(2)}) collective-permute-start(bf16[16,16,128]{2,1,0:T(8,128)(2,1)S(1)} %get-tuple-element.19), channel_id=1, source_target_pairs={{0,4},{1,9},{4,0},{5,13},{8,12},{9,1},{12,8},{13,5},{2,6},{3,11},{... | collective-permute-start | bytes 196616 | tf_op jit(solution)/shard_map/ppermute | solution.py:65
  20.6 0.8 %copy-start.2 = (bf16[6,256]{1,0:T(8,128)(2,1)S(1)}, bf16[6,256]{1,0:T(8,128)(2,1)}, u32[]{:S(2)}) copy-start(bf16[6,256]{1,0:T(8,128)(2,1)} %refs_1_.3) | copy-start | bytes 9220
  20.7 4.5 %collective-permute-start.6 = (bf16[5,64,128]{2,1,0:T(8,128)(2,1)S(1)}, bf16[5,64,128]{2,1,0:T(8,128)(2,1)S(1)}, u32[]{:S(2)}, u32[]{:S(2)}) collective-permute-start(bf16[5,64,128]{2,1,0:T(8,128)(2,1)S(1)} %shard_map.39), channel_id=1, source_target_pairs={{2,0},{3,1},{0,2},{1,3},{6,4},{7,5},{4,6},{5,7},{10,8},{11,9},{8,1... | collective-permute-start | bytes 245768 | tf_op jit(solution)/shard_map/ppermute | solution.py:40

commit v3 on v2

--- a/solution.py
+++ b/solution.py
@@ -102,7 +102,7 @@
             upper = upper[1:]
 
 
-def tree_levels(state, other, columns, first, levels, held, lengths):
+def tree_levels(state, other, columns, first, levels, held, lengths, packed=False):
     rows = columns.shape[0] // 2
     source, target = state, other
     done = 0
@@ -112,9 +112,10 @@
         for turn in range(bits):
             level = levels[done + turn]
             inner = turn + 1 < bits
+            natural = turn == 0 and not (packed and done == 0)
 
             def rows_in(vector, start, stride):
-                return pl.ds(start, SUBLANES, stride=stride) if turn == 0 else pl.ds(vector * SUBLANES, SUBLANES)
+                return pl.ds(start, SUBLANES, stride=stride) if natural else pl.ds(vector * SUBLANES, SUBLANES)
 
             def rows_out(vector, start, stride):
                 return pl.ds(vector * SUBLANES, SUBLANES) if inner else pl.ds(start, SUBLANES, stride=stride)
@@ -192,18 +193,21 @@
         out[tile, :, :] = state[tile, :, :].astype(jnp.bfloat16)
 
 
-def chip_kernel(spans, out_tiles, group_count, shifts, *refs):
+def chip_kernel(spans, out_tiles, group_count, *refs):
     pieces = (refs[: len(spans)], refs[len(spans) : 2 * len(spans)])
-    blocks = refs[2 * len(spans) : 2 * len(spans) + group_count]
-    raw, ping, pong, table, columns = refs[2 * len(spans) + group_count :]
+    refs = refs[2 * len(spans) :]
     chan_rows = pieces[0][0].shape[0]
     local_count = bits_of(chan_rows)
     chip, core = lax.axis_index("freq"), lax.axis_index("sub")
-    chunk = shifts[0:SUBLANES, pl.ds(pl.multiple_of(chip * LANES, LANES), LANES)]
-    lane, level = lanes(), lax.broadcasted_iota(jnp.int32, (SUBLANES, LANES), 0)
-    kept = lane & (1 << level) - 1
-    picked = gathered(chunk, (2 * (lane - kept) + (core << level) + kept) & LANES - 1)
-    transposed_table([picked[at : at + 1, :] for at in range(local_count + 1)], table, columns)
+    if group_count:
+        (earlier, columns), blocks, (raw, ping, pong) = refs[:2], refs[2:-3], refs[-3:]
+    else:
+        shifts, rows, columns, raw, ping, pong, table = refs
+        chunk = shifts[0:SUBLANES, pl.ds(pl.multiple_of(chip * LANES, LANES), LANES)]
+        lane, level = lanes(), lax.broadcasted_iota(jnp.int32, (SUBLANES, LANES), 0)
+        kept = lane & (1 << level) - 1
+        picked = gathered(chunk, (2 * (lane - kept) + (core << level) + kept) & LANES - 1)
+        transposed_table([picked[at : at + 1, :] for at in range(local_count + 1)], table, columns)
     for side in range(2):
         place = pl.multiple_of((core ^ side) * chan_rows, chan_rows)
         tile = 0
@@ -226,15 +230,22 @@
         for tile in range(lengths[0]):
             later = raw[tile + 1, high, :]
             moved = pltpu.roll(jnp.where(mask, upper, later), LANES - core & LANES - 1, 1)
-            ping[tile, pl.ds(vector, SUBLANES, stride=SUBLANES), :] = raw[tile, low, :] + moved
+            ping[tile, pl.ds(vector * SUBLANES, SUBLANES), :] = raw[tile, low, :] + moved
             upper = later
-    last = tree_levels(ping, pong, columns, 1, levels[1:], 1, lengths[1:])
+    last = tree_levels(ping, pong, columns, 1, levels[1:], 1, lengths[1:], packed=True)
+    if not group_count:
+        for tile in range(out_tiles):
+            rows[tile, :, :] = last[tile, :, :]
+        return
     size = chan_rows // group_count
     own = reversed_bits(chip, bits_of(group_count))
+    first = earlier.shape[0]
     for mask, block in zip(step_masks(group_count, core), blocks):
         start = pl.multiple_of((own ^ reversed_bits(mask, bits_of(group_count))) * size, size)
+        for tile in range(first):
+            block[tile, :, :] = earlier[tile, pl.ds(start, size), :].astype(jnp.bfloat16)
         for tile in range(out_tiles):
-            block[tile, :, :] = last[tile, pl.ds(start, size), :].astype(jnp.bfloat16)
+            block[first + tile, :, :] = last[tile, pl.ds(start, size), :].astype(jnp.bfloat16)
 
 
 def toeplitz(filters, target):
@@ -256,30 +267,17 @@
             before = rolled
 
 
-def trial_kernel(plan, group_count, level_count, *refs):
-    shifts, filters, refs = refs[0], refs[1], refs[2:]
-    blocks, refs = refs[:group_count], refs[group_count:]
-    halos, refs = refs[: len(plan.halos)], refs[len(plan.halos) :]
-    if plan.taken:
-        carried, taps, so_far, refs = refs[0], refs[1], refs[2], refs[3:]
-    out, refs = refs[0], refs[1:]
-    if plan.given:
-        handed, taps, refs = refs[0], refs[1], refs[2:]
-    state, other, table, columns, normal, responses, result, arrived = refs[:8]
-    if not plan.given and not plan.taken:
-        taps = refs[8]
-    width_count, tap_count = filters.shape
-    chan_rows = result.shape[0]
-    block_rows = chan_rows // group_count
-    levels = list(range(level_count - bits_of(group_count), level_count))
+def table_kernel(group_count, block_rows, shifts, filters, columns, taps, table):
+    level_count = shifts.shape[0]
     chip, core = lax.axis_index("freq"), lax.axis_index("sub")
     own = reversed_bits(chip * 2 + core, bits_of(group_count) + 1)
     lane = lax.broadcasted_iota(jnp.int32, (1, LANES), 1)
     rows = []
-    for section, level in enumerate(levels):
+    for section in range(bits_of(group_count)):
+        level = level_count - bits_of(group_count) + section
         wide = block_rows * 2 ** (section + 1)
         row = jnp.zeros((1, LANES), jnp.int32)
-        for subband in range(chan_rows // wide):
+        for subband in range(block_rows * group_count // wide):
             start = subband * 2 ** (level + 1) + own * wide
             tile = pl.multiple_of(start >> bits_of(LANES) << bits_of(LANES), LANES)
             chunk = shifts[level : level + 1, pl.ds(tile, LANES)]
@@ -287,8 +285,22 @@
             row = jnp.where(lane >= subband * wide, moved, row)
         rows.append(row)
     transposed_table(rows, table, columns)
-    if not plan.taken:
-        toeplitz(filters, taps)
+    toeplitz(filters, taps)
+
+
+def trial_kernel(plan, group_count, level_count, scale, columns, taps, *refs):
+    blocks, refs = refs[:group_count], refs[group_count:]
+    halos, refs = refs[: len(plan.halos)], refs[len(plan.halos) :]
+    if plan.taken:
+        carried, so_far, refs = refs[0], refs[1], refs[2:]
+    out, refs = refs[0], refs[1:]
+    if plan.given:
+        handed, refs = refs[0], refs[1:]
+    state, other, normal, responses, result, arrived = refs
+    chan_rows = result.shape[0]
+    block_rows = chan_rows // group_count
+    width_count, kept = taps.shape[0] // LANES, taps.shape[1] // LANES - 1
+    levels = list(range(level_count - bits_of(group_count), level_count))
     placed(state, blocks, plan.main_tiles, plan.first)
     at = plan.main_tiles - plan.first
     for hop, (halo, tiles) in enumerate(zip(halos, plan.halos), 1):
@@ -299,8 +311,6 @@
     for tile in range(at, at + plan.empty_tiles):
         state[tile, :, :] = jnp.zeros((chan_rows, LANES), jnp.float32)
     last = tree_levels(state, other, columns, 0, levels, block_rows, plan.lengths)
-    scale = 1.0 / math.sqrt(shifts.shape[1])
-    kept = tap_count // LANES
     head = kept if plan.taken else 0
     for tile in range(head):
         normal[tile, :, :] = carried[tile, :, :]
@@ -375,28 +385,29 @@
     block_rows = chan_rows // group_count
     table = pltpu.VMEM((LANES, LANES), jnp.float32)
 
-    def within_chip(own, other, spans, tile_count, out_tiles):
-        state = pltpu.VMEM((tile_count + 1, chan_rows, LANES), jnp.float32)
-        block = jax.ShapeDtypeStruct((out_tiles, block_rows, LANES), jnp.bfloat16)
+    def within_chip(operands, spans, raw_tiles, out_tiles, sending):
+        state = pltpu.VMEM((raw_tiles + 1, chan_rows, LANES), jnp.float32)
+        if sending:
+            block = jax.ShapeDtypeStruct((time_tiles, block_rows, LANES), jnp.bfloat16)
+            out_shape = [block] * group_count
+        else:
+            out_shape = [
+                jax.ShapeDtypeStruct((out_tiles, chan_rows, LANES), jnp.float32),
+                jax.ShapeDtypeStruct((LANES, LANES), jnp.float32),
+            ]
         return pl.pallas_call(
-            functools.partial(chip_kernel, spans, out_tiles, group_count),
-            out_shape=[block] * group_count,
-            in_specs=[in_vmem] * (1 + 2 * len(spans)),
-            out_specs=[in_vmem] * group_count,
-            scratch_shapes=[
-                pltpu.VMEM((tile_count + 1, 2 * chan_rows, LANES), jnp.float32),
-                state,
-                state,
-                table,
-                table,
-            ],
+            functools.partial(chip_kernel, spans, out_tiles, group_count if sending else 0),
+            out_shape=out_shape,
+            in_specs=[in_vmem] * len(operands),
+            out_specs=[in_vmem] * len(out_shape),
+            scratch_shapes=[pltpu.VMEM((raw_tiles + 1, 2 * chan_rows, LANES), jnp.float32), state, state]
+            + ([] if sending else [table]),
             compiler_params=params,
-        )(delay_shifts, *own, *other)
+        )(*operands)
 
     def between_chips(plan, blocks, halos, carried=()):
         state = pltpu.VMEM((plan.state_tiles, chan_rows, LANES), jnp.float32)
-        taps = ((width_count * LANES, tap_count + LANES), jnp.bfloat16)
-        operands = [delay_shifts, pulse_filters, *blocks, *halos, *carried]
+        operands = [columns, taps, *blocks, *halos, *carried]
         in_specs = [in_vmem] * len(operands)
         aliases = {}
         if plan.taken:
@@ -404,32 +415,24 @@
             aliases = {len(operands) - 1: 0}
         out_shape = [jax.ShapeDtypeStruct((chan_rows, time_len), jnp.float32)]
         out_specs = [in_any]
-        scratch = []
         if plan.given:
-            out_shape += [
-                jax.ShapeDtypeStruct((tap_tiles, chan_rows, LANES), jnp.bfloat16),
-                jax.ShapeDtypeStruct(*taps),
-            ]
-            out_specs += [in_vmem] * 2
-        elif not plan.taken:
-            scratch = [pltpu.VMEM(*taps)]
+            out_shape.append(jax.ShapeDtypeStruct((tap_tiles, chan_rows, LANES), jnp.bfloat16))
+            out_specs.append(in_vmem)
         most = max(some for _, some in plan.chunks)
+        scale = 1.0 / math.sqrt(delay_shifts.shape[1])
         return pl.pallas_call(
-            functools.partial(trial_kernel, plan, group_count, level_count),
+            functools.partial(trial_kernel, plan, group_count, level_count, scale),
             out_shape=out_shape,
             in_specs=in_specs,
             out_specs=out_specs,
             scratch_shapes=[
                 state,
                 state,
-                table,
-                table,
                 pltpu.VMEM((plan.out_tiles + tap_tiles, chan_rows, LANES), jnp.bfloat16),
                 pltpu.VMEM((most * chan_rows, width_count * LANES), jnp.float32),
                 pltpu.VMEM((chan_rows, plan.out_tiles * LANES), jnp.float32),
                 pltpu.SemaphoreType.DMA((len(plan.chunks),)),
-            ]
-            + scratch,
+            ],
             input_output_aliases=aliases,
             compiler_params=params,
         )(*operands)
@@ -445,12 +448,32 @@
         out_specs=[in_vmem] * 2,
         compiler_params=params,
     )(filterbank)
-    both, spans = ([own], [other_core]), [(0, time_len, 0)]
+    near_tiles = near_len // LANES
+    early = time_tiles - near_tiles
+    rows, delays = within_chip(
+        [own, other_core, delay_shifts], [(0, time_len, 0)], time_tiles, early, False
+    )
+    both, spans = ([own], [other_core]), [(early * LANES, near_len, 0)]
     if lax.axis_size("tm") > 1:
         for crossed in range(2):
             both[crossed].append(from_ahead(ahead, 1, crossed))
         spans.append((0, near_len, 1))
-    main = exchanged(within_chip(*both, spans, time_tiles + near_len // LANES, time_tiles))
+    main = list(within_chip([*both[0], *both[1], rows, delays], spans, 2 * near_tiles, near_tiles, True))
+    late_shifts, late_filters, main[0] = lax.optimization_barrier((delay_shifts, pulse_filters, main[0]))
+    columns, taps = pl.pallas_call(
+        functools.partial(table_kernel, group_count, block_rows),
+        out_shape=[
+            jax.ShapeDtypeStruct((LANES, LANES), jnp.float32),
+            jax.ShapeDtypeStruct((width_count * LANES, tap_count + LANES), jnp.bfloat16),
+        ],
+        in_specs=[in_vmem] * 2,
+        out_specs=[in_vmem] * 2,
+        scratch_shapes=[table],
+        compiler_params=params,
+    )(late_shifts, late_filters)
+    *main, last = exchanged(main)
+    columns, taps, last = lax.optimization_barrier((columns, taps, last))
+    main.append(last)
 
     halos, takes = [], []
     rest = far_tiles

time: 27.1 us -> 24.7 us (0.911)
  waiting for transfers between devices: 10.1 us -> 7.11 us
  starting transfers between devices: 8.37 us -> 8.77 us
    ppermute x3, waiting for transfers between devices: 5.02 us -> 1.59 us  [from_ahead(): return lax.ppermute(value, ('tm', 'sub'), route)]
    ppermute x3, starting transfers between devices: 3.46 us -> 4.1 us  [from_ahead(): return lax.ppermute(value, ('tm', 'sub'), route)]
    pallas_call x1 -> x2, Pallas kernels: 3.23 us -> 3.69 us  [within_chip(): pl.pallas_call(functools.partial(chip_kernel, spans, out_tiles, group_cou...]
    ppermute x3, waiting for transfers between devices: 5.07 us -> 5.51 us  [exchanged(): received.append(lax.ppermute(block, ('freq', 'sub'), route))]
    pallas_call x2, Pallas kernels: 4.17 us -> 3.73 us  [between_chips(): pl.pallas_call(functools.partial(trial_kernel, plan, group_count, level_c...]
  transfers between devices with their start and end apart: 7 -> 7, of which waited for: 5 -> 4; matrix products, arithmetic and copies ran while one was open for 0% -> 0% of each run, Pallas kernels for 9% -> 22%
where the time goes in v3:
time: 24.7 us; the launch traced here: 24.6 us
  starting transfers between devices  8.77 us (36%)
  Pallas kernels  7.7 us (31%)
  waiting for transfers between devices  7.11 us (29%)
  local copies, waits for them, and re-layouts  0.96 us (4%)
    ppermute x3, waiting for transfers between devices, exchanged(): received.append(lax.ppermute(block, ('freq', 'sub'), route))  5.51 us
    ppermute x3, starting transfers between devices, exchanged(): received.append(lax.ppermute(block, ('freq', 'sub'), route))  4.22 us
    ppermute x3, starting transfers between devices, from_ahead(): return lax.ppermute(value, ('tm', 'sub'), route)  4.1 us
    pallas_call x2, Pallas kernels, between_chips(): pl.pallas_call(functools.partial(trial_kernel, plan, group_count, level_c...  3.73 us
    pallas_call x2, Pallas kernels, within_chip(): pl.pallas_call(functools.partial(chip_kernel, spans, out_tiles, group_cou...  3.69 us
    ppermute x3, waiting for transfers between devices, from_ahead(): return lax.ppermute(value, ('tm', 'sub'), route)  1.59 us
    unnamed x6, local copies, waits for them, and re-layouts  0.96 us
  transfers between devices with their start and end apart: 7, of which 4 were waited for; matrix products, arithmetic and copies ran while one was open for 0% of the time, Pallas kernels for 22%

profile of v3, /device:TPU:0, one launch (start us, length us, event | category | flops | bytes accessed | tf_op | source)
XLA Modules:
  0.0 24.6 jit_solution(2464797048711788729)
XLA Ops:
  0.0 0.5 %collective-permute-start.1 = (bf16[64,2048]{1,0:T(8,128)(2,1)}, bf16[64,2048]{1,0:T(8,128)(2,1)S(1)}, u32[]{:S(2)}, u32[]{:S(2)}) collective-permute-start(bf16[64,2048]{1,0:T(8,128)(2,1)} %whole.1), channel_id=1, source_target_pairs={{0,1},{1,0},{2,3},{3,2},{4,5},{5,4},{6,7},{7,6},{8,9},{9,8},{10,11... | collective-permute-start | bytes 786440 | tf_op jit(solution)/shard_map/ppermute | solution.py:45
  0.5 0.0 copy-start
  0.5 0.9 %copy-done = bf16[64,2048]{1,0:T(8,128)(2,1)S(1)} copy-done((bf16[64,2048]{1,0:T(8,128)(2,1)S(1)}, bf16[64,2048]{1,0:T(8,128)(2,1)}, u32[]{:S(2)}) %copy-start) | copy-done | bytes 262168
  1.4 2.7 %collective-permute-start.2 = (bf16[64,128]{1,0:T(8,128)(2,1)S(1)}, bf16[64,128]{1,0:T(8,128)(2,1)S(1)}, u32[]{:S(2)}, u32[]{:S(2)}) collective-permute-start(bf16[64,128]{1,0:T(8,128)(2,1)S(1)} %get-tuple-element.24), channel_id=1, source_target_pairs={{2,1},{3,0},{0,3},{1,2},{6,5},{7,4},{4,7},{5,6},{10,9},{11,8},{8,1... | collective-permute-start | bytes 49160 | tf_op jit(solution)/shard_map/ppermute | solution.py:40
  4.1 0.0 collective-permute-start
  4.1 0.0 collective-permute-done.1.refs_1_.refs_2_
  4.1 0.0 copy-done.1
  4.1 3.0 %shard_map.38 = (f32[15,64,128]{2,1,0:T(8,128)S(1)}, f32[128,128]{1,0:T(8,128)S(1)}) custom-call(bf16[64,2048]{1,0:T(8,128)(2,1)S(1)} %get-tuple-element.23.refs_0_, bf16[64,2048]{1,0:T(8,128)(2,1)S(1)} %collective-permute-done.1.refs_1_.refs_2_, s32[9,512]{1,0:T(8,128)S(1)} %copy-done.1), custom_call_target="tpu_custom_call" | custom-call | tf_op jit(solution)/shard_map/pallas_call | solution.py:398
  7.2 0.0 collective-permute-done.2.refs_3_
  7.2 0.7 %collective-permute-done.refs_1_ = bf16[64,128]{1,0:T(8,128)(2,1)S(1)} collective-permute-done((bf16[64,128]{1,0:T(8,128)(2,1)S(1)}, bf16[64,128]{1,0:T(8,128)(2,1)S(1)}, u32[]{:S(2)}, u32[]{:S(2)}) %collective-permute-start) | collective-permute-done | bytes 16416 | tf_op jit(solution)/shard_map/ppermute | solution.py:40
  7.9 0.7 %shard_map.39 = (bf16[16,16,128]{2,1,0:T(8,128)(2,1)S(1)}, bf16[16,16,128]{2,1,0:T(8,128)(2,1)S(1)}, bf16[16,16,128]{2,1,0:T(8,128)(2,1)S(1)}, bf16[16,16,128]{2,1,0:T(8,128)(2,1)S(1)}) custom-call(bf16[64,2048]{1,0:T(8,128)(2,1)S(1)} %get-tuple-element.23.refs_0_, bf16[64,128]{1,0:T(8,128)(2,1)S(1)} %collective-permute-done.refs_1_, ...), custom_call_target="tpu_custom_call" | custom-call | tf_op jit(solution)/shard_map/pallas_call | solution.py:398
  8.5 0.0 copy-start.2
  8.5 1.6 %collective-permute-start.3 = (bf16[16,16,128]{2,1,0:T(8,128)(2,1)S(1)}, bf16[16,16,128]{2,1,0:T(8,128)(2,1)S(1)}, u32[]{:S(2)}, u32[]{:S(2)}) collective-permute-start(bf16[16,16,128]{2,1,0:T(8,128)(2,1)S(1)} %get-tuple-element.32), channel_id=1, source_target_pairs={{0,4},{1,9},{4,0},{5,13},{8,12},{9,1},{12,8},{13,5},{2,6},{3,11},{... | collective-permute-start | bytes 196616 | tf_op jit(solution)/shard_map/ppermute | solution.py:65
  10.2 2.5 %collective-permute-start.4 = (bf16[16,16,128]{2,1,0:T(8,128)(2,1)S(1)}, bf16[16,16,128]{2,1,0:T(8,128)(2,1)S(1)}, u32[]{:S(2)}, u32[]{:S(2)}) collective-permute-start(bf16[16,16,128]{2,1,0:T(8,128)(2,1)S(1)} %get-tuple-element.36), channel_id=1, source_target_pairs={{0,12},{1,5},{4,8},{5,1},{8,4},{9,13},{12,0},{13,9},{2,14},{3,7},{... | collective-permute-start | bytes 196616 | tf_op jit(solution)/shard_map/ppermute | solution.py:65
  12.6 0.1 collective-permute-start.5
  12.8 0.0 copy-done.2
  12.8 0.2 shard_map.40
  13.0 0.0 collective-permute-done.3.refs_3_
  13.0 3.4 %collective-permute-done.4.refs_1_ = bf16[16,16,128]{2,1,0:T(8,128)(2,1)S(1)} collective-permute-done((bf16[16,16,128]{2,1,0:T(8,128)(2,1)S(1)}, bf16[16,16,128]{2,1,0:T(8,128)(2,1)S(1)}, u32[]{:S(2)}, u32[]{:S(2)}) %collective-permute-start.4) | collective-permute-done | bytes 65568 | tf_op jit(solution)/shard_map/ppermute | solution.py:65
  16.4 2.1 %collective-permute-done.5.refs_2_ = bf16[16,16,128]{2,1,0:T(8,128)(2,1)S(1)} collective-permute-done((bf16[16,16,128]{2,1,0:T(8,128)(2,1)S(1)}, bf16[16,16,128]{2,1,0:T(8,128)(2,1)S(1)}, u32[]{:S(2)}, u32[]{:S(2)}) %collective-permute-start.5) | collective-permute-done | bytes 65568 | tf_op jit(solution)/shard_map/ppermute | solution.py:65
  18.5 1.4 %collective-permute-start.6 = (bf16[5,64,128]{2,1,0:T(8,128)(2,1)S(1)}, bf16[5,64,128]{2,1,0:T(8,128)(2,1)S(1)}, u32[]{:S(2)}, u32[]{:S(2)}) collective-permute-start(bf16[5,64,128]{2,1,0:T(8,128)(2,1)S(1)} %shard_map.41), channel_id=1, source_target_pairs={{2,0},{3,1},{0,2},{1,3},{6,4},{7,5},{4,6},{5,7},{10,8},{11,9},{8,1... | collective-permute-start | bytes 245768 | tf_op jit(solution)/shard_map/ppermute | solution.py:40
  20.0 2.2 %shard_map.42 = (f32[64,2048]{1,0:T(8,128)}, bf16[2,64,128]{2,1,0:T(8,128)(2,1)S(1)}) custom-call(f32[128,128]{1,0:T(8,128)S(1)} %get-tuple-element.33.columns, bf16[768,384]{1,0:T(8,128)(2,1)S(1)} %get-tuple-element.34.taps, bf16[16,16,128]{2,1,0:T(8,128)(2,1)S(1)} %get-tuple-element.35.refs_0_, bf16[16,16,128]{2,1,0:T(8,128)(2,1)S(1)} %collective-permute-done.4.refs_1_, ...), custom_call_target="tpu_custom_call" | custom-call | tf_op jit(solution)/shard_map/pallas_call | solution.py:423
  22.1 0.9 %collective-permute-done.6.refs_4_ = bf16[5,64,128]{2,1,0:T(8,128)(2,1)S(1)} collective-permute-done((bf16[5,64,128]{2,1,0:T(8,128)(2,1)S(1)}, bf16[5,64,128]{2,1,0:T(8,128)(2,1)S(1)}, u32[]{:S(2)}, u32[]{:S(2)}) %collective-permute-start.6) | collective-permute-done | bytes 81952 | tf_op jit(solution)/shard_map/ppermute | solution.py:40
  23.0 1.5 %shard_map.43 = f32[64,2048]{1,0:T(8,128)} custom-call(f32[128,128]{1,0:T(8,128)S(1)} %get-tuple-element.33.columns, bf16[768,384]{1,0:T(8,128)(2,1)S(1)} %get-tuple-element.34.taps, bf16[16,16,128]{2,1,0:T(8,128)(2,1)S(1)} %get-tuple-element.35.refs_0_, bf16[16,16,128]{2,1,0:T(8,128)(2,1)S(1)} %collective-permute-done.4.refs_1_, ...), custom_call_target="tpu_custom_call", output_to_operand_aliasing={{}: (8, {})} | custom-call | tf_op jit(solution)/shard_map/pallas_call | solution.py:423
  (3 shorter events, 0.1 us)
Async XLA Ops:
  0.0 4.1 %collective-permute-start.1 = (bf16[64,2048]{1,0:T(8,128)(2,1)}, bf16[64,2048]{1,0:T(8,128)(2,1)S(1)}, u32[]{:S(2)}, u32[]{:S(2)}) collective-permute-start(bf16[64,2048]{1,0:T(8,128)(2,1)} %whole.1), channel_id=1, source_target_pairs={{0,1},{1,0},{2,3},{3,2},{4,5},{5,4},{6,7},{7,6},{8,9},{9,8},{10,11... | collective-permute-start | bytes 786440 | tf_op jit(solution)/shard_map/ppermute | solution.py:45
  0.5 0.9 %copy-start = (bf16[64,2048]{1,0:T(8,128)(2,1)S(1)}, bf16[64,2048]{1,0:T(8,128)(2,1)}, u32[]{:S(2)}) copy-start(bf16[64,2048]{1,0:T(8,128)(2,1)} %whole.1) | copy-start | bytes 786436
  1.4 2.7 %copy-start.1 = (s32[9,512]{1,0:T(8,128)S(1)}, s32[9,512]{1,0:T(8,128)}, u32[]{:S(2)}) copy-start(s32[9,512]{1,0:T(8,128)} %shifts) | copy-start | bytes 55300
  1.4 5.7 %collective-permute-start.2 = (bf16[64,128]{1,0:T(8,128)(2,1)S(1)}, bf16[64,128]{1,0:T(8,128)(2,1)S(1)}, u32[]{:S(2)}, u32[]{:S(2)}) collective-permute-start(bf16[64,128]{1,0:T(8,128)(2,1)S(1)} %get-tuple-element.24), channel_id=1, source_target_pairs={{2,1},{3,0},{0,3},{1,2},{6,5},{7,4},{4,7},{5,6},{10,9},{11,8},{8,1... | collective-permute-start | bytes 49160 | tf_op jit(solution)/shard_map/ppermute | solution.py:40
  4.1 3.7 %collective-permute-start = (bf16[64,128]{1,0:T(8,128)(2,1)S(1)}, bf16[64,128]{1,0:T(8,128)(2,1)S(1)}, u32[]{:S(2)}, u32[]{:S(2)}) collective-permute-start(bf16[64,128]{1,0:T(8,128)(2,1)S(1)} %get-tuple-element.24), channel_id=1, source_target_pairs={{2,0},{3,1},{0,2},{1,3},{6,4},{7,5},{4,6},{5,7},{10,8},{11,9},{8,1... | collective-permute-start | bytes 49160 | tf_op jit(solution)/shard_map/ppermute | solution.py:40
  8.5 4.2 %copy-start.2 = (bf16[6,256]{1,0:T(8,128)(2,1)S(1)}, bf16[6,256]{1,0:T(8,128)(2,1)}, u32[]{:S(2)}) copy-start(bf16[6,256]{1,0:T(8,128)(2,1)} %filters) | copy-start | bytes 9220
  8.5 4.5 %collective-permute-start.3 = (bf16[16,16,128]{2,1,0:T(8,128)(2,1)S(1)}, bf16[16,16,128]{2,1,0:T(8,128)(2,1)S(1)}, u32[]{:S(2)}, u32[]{:S(2)}) collective-permute-start(bf16[16,16,128]{2,1,0:T(8,128)(2,1)S(1)} %get-tuple-element.32), channel_id=1, source_target_pairs={{0,4},{1,9},{4,0},{5,13},{8,12},{9,1},{12,8},{13,5},{2,6},{3,11},{... | collective-permute-start | bytes 196616 | tf_op jit(solution)/shard_map/ppermute | solution.py:65
  10.2 6.3 %collective-permute-start.4 = (bf16[16,16,128]{2,1,0:T(8,128)(2,1)S(1)}, bf16[16,16,128]{2,1,0:T(8,128)(2,1)S(1)}, u32[]{:S(2)}, u32[]{:S(2)}) collective-permute-start(bf16[16,16,128]{2,1,0:T(8,128)(2,1)S(1)} %get-tuple-element.36), channel_id=1, source_target_pairs={{0,12},{1,5},{4,8},{5,1},{8,4},{9,13},{12,0},{13,9},{2,14},{3,7},{... | collective-permute-start | bytes 196616 | tf_op jit(solution)/shard_map/ppermute | solution.py:65
  12.6 5.9 %collective-permute-start.5 = (bf16[16,16,128]{2,1,0:T(8,128)(2,1)S(1)}, bf16[16,16,128]{2,1,0:T(8,128)(2,1)S(1)}, u32[]{:S(2)}, u32[]{:S(2)}) collective-permute-start(bf16[16,16,128]{2,1,0:T(8,128)(2,1)S(1)} %get-tuple-element.37), channel_id=1, source_target_pairs={{0,8},{1,13},{4,12},{5,9},{8,0},{9,5},{12,4},{13,1},{2,10},{3,15},... | collective-permute-start | bytes 196616 | tf_op jit(solution)/shard_map/ppermute | solution.py:65
  18.5 4.5 %collective-permute-start.6 = (bf16[5,64,128]{2,1,0:T(8,128)(2,1)S(1)}, bf16[5,64,128]{2,1,0:T(8,128)(2,1)S(1)}, u32[]{:S(2)}, u32[]{:S(2)}) collective-permute-start(bf16[5,64,128]{2,1,0:T(8,128)(2,1)S(1)} %shard_map.41), channel_id=1, source_target_pairs={{2,0},{3,1},{0,2},{1,3},{6,4},{7,5},{4,6},{5,7},{10,8},{11,9},{8,1... | collective-permute-start | bytes 245768 | tf_op jit(solution)/shard_map/ppermute | solution.py:40

commit v4 on v3

--- a/solution.py
+++ b/solution.py
@@ -186,10 +186,12 @@
             target[tile - skip, pl.ds(start, rows), :] = block[tile, :, :].astype(jnp.float32)
 
 
-def gather_kernel(*refs):
+def join_kernel(*refs):
     *blocks, out, state = refs
-    placed(state, blocks, out.shape[0], 0)
+    rows = blocks[0].shape[1]
     for tile in range(out.shape[0]):
+        for index, block in enumerate(blocks):
+            state[tile, index * rows : (index + 1) * rows, :] = block[tile, :, :].astype(jnp.float32)
         out[tile, :, :] = state[tile, :, :].astype(jnp.bfloat16)
 
 
@@ -290,23 +292,43 @@
 
 def trial_kernel(plan, group_count, level_count, scale, columns, taps, *refs):
     blocks, refs = refs[:group_count], refs[group_count:]
-    halos, refs = refs[: len(plan.halos)], refs[len(plan.halos) :]
+    halos, refs = refs[: 2 * len(plan.halos)], refs[2 * len(plan.halos) :]
     if plan.taken:
         carried, so_far, refs = refs[0], refs[1], refs[2:]
     out, refs = refs[0], refs[1:]
     if plan.given:
         handed, refs = refs[0], refs[1:]
-    state, other, normal, responses, result, arrived = refs
+    state, other, normal, responses, *refs = refs
+    if plan.given:
+        result = out
+    else:
+        result, arrived = refs
     chan_rows = result.shape[0]
     block_rows = chan_rows // group_count
     width_count, kept = taps.shape[0] // LANES, taps.shape[1] // LANES - 1
     levels = list(range(level_count - bits_of(group_count), level_count))
+    copies = []
+    if plan.taken:
+        place = out.at[:, pl.ds(0, plan.out_first * LANES)]
+        copies.append(pltpu.make_async_copy(so_far, place, arrived.at[len(plan.chunks)]))
+        copies[0].start()
     placed(state, blocks, plan.main_tiles, plan.first)
     at = plan.main_tiles - plan.first
-    for hop, (halo, tiles) in enumerate(zip(halos, plan.halos), 1):
+    chip, core = lax.axis_index("freq"), lax.axis_index("sub")
+    for hop, tiles in enumerate(plan.halos, 1):
         there = lax.axis_index("tm") + hop < lax.axis_size("tm")
         for tile in range(tiles):
-            state[at, :, :] = jnp.where(there, halo[tile, :, :].astype(jnp.float32), 0.0)
+            joined, single = [
+                jnp.where(there, halo[tile, :, :].astype(jnp.float32), 0.0)
+                for halo in halos[2 * hop - 2 : 2 * hop]
+            ]
+            for index, mask in enumerate(step_masks(group_count, core)):
+                start = pl.multiple_of((chip ^ mask) * block_rows, block_rows)
+                if index + 1 < group_count:
+                    part = joined[index * block_rows : (index + 1) * block_rows]
+                else:
+                    part = single
+                state[at, pl.ds(start, block_rows), :] = part
             at += 1
     for tile in range(at, at + plan.empty_tiles):
         state[tile, :, :] = jnp.zeros((chan_rows, LANES), jnp.float32)
@@ -320,7 +342,6 @@
     if plan.given:
         for tile in range(kept):
             handed[tile, :, :] = normal[count + tile, :, :]
-    copies = []
     for turn, (first_tile, some) in enumerate(plan.chunks):
         size = some * chan_rows
         windows = [
@@ -344,6 +365,8 @@
             result[row : row + PACKED, tile * LANES : (tile + 1) * LANES] = (
                 jnp.log2(total) + highest
             ) * (1.0 / LOG2_E)
+        if plan.given:
+            continue
         columns_now = pl.ds(first_tile * LANES, some * LANES)
         place = out.at[:, pl.ds((plan.out_first + first_tile) * LANES, some * LANES)]
         copies.append(pltpu.make_async_copy(result.at[:, columns_now], place, arrived.at[turn]))
@@ -408,32 +431,30 @@
     def between_chips(plan, blocks, halos, carried=()):
         state = pltpu.VMEM((plan.state_tiles, chan_rows, LANES), jnp.float32)
         operands = [columns, taps, *blocks, *halos, *carried]
-        in_specs = [in_vmem] * len(operands)
-        aliases = {}
-        if plan.taken:
-            in_specs[-1] = in_any
-            aliases = {len(operands) - 1: 0}
-        out_shape = [jax.ShapeDtypeStruct((chan_rows, time_len), jnp.float32)]
-        out_specs = [in_any]
+        result = (chan_rows, plan.out_tiles * LANES)
         if plan.given:
-            out_shape.append(jax.ShapeDtypeStruct((tap_tiles, chan_rows, LANES), jnp.bfloat16))
-            out_specs.append(in_vmem)
+            out_shape = [
+                jax.ShapeDtypeStruct(result, jnp.float32),
+                jax.ShapeDtypeStruct((tap_tiles, chan_rows, LANES), jnp.bfloat16),
+            ]
+            out_specs, scratch = [in_vmem] * 2, []
+        else:
+            out_shape, out_specs = [jax.ShapeDtypeStruct((chan_rows, time_len), jnp.float32)], [in_any]
+            scratch = [pltpu.VMEM(result, jnp.float32), pltpu.SemaphoreType.DMA((len(plan.chunks) + 1,))]
         most = max(some for _, some in plan.chunks)
         scale = 1.0 / math.sqrt(delay_shifts.shape[1])
         return pl.pallas_call(
             functools.partial(trial_kernel, plan, group_count, level_count, scale),
             out_shape=out_shape,
-            in_specs=in_specs,
+            in_specs=[in_vmem] * len(operands),
             out_specs=out_specs,
             scratch_shapes=[
                 state,
                 state,
                 pltpu.VMEM((plan.out_tiles + tap_tiles, chan_rows, LANES), jnp.bfloat16),
                 pltpu.VMEM((most * chan_rows, width_count * LANES), jnp.float32),
-                pltpu.VMEM((chan_rows, plan.out_tiles * LANES), jnp.float32),
-                pltpu.SemaphoreType.DMA((len(plan.chunks),)),
-            ],
-            input_output_aliases=aliases,
+            ]
+            + scratch,
             compiler_params=params,
         )(*operands)
 
@@ -479,18 +500,21 @@
     rest = far_tiles
     if lax.axis_size("tm") > 1:
         first_tiles = min(time_tiles, far_tiles)
-        gathered_rows = pl.pallas_call(
-            gather_kernel,
-            out_shape=jax.ShapeDtypeStruct((first_tiles, chan_rows, LANES), jnp.bfloat16),
-            in_specs=[in_vmem] * group_count,
+        joined = pl.pallas_call(
+            join_kernel,
+            out_shape=jax.ShapeDtypeStruct(
+                (first_tiles, chan_rows - block_rows, LANES), jnp.bfloat16
+            ),
+            in_specs=[in_vmem] * (group_count - 1),
             out_specs=in_vmem,
-            scratch_shapes=[pltpu.VMEM((first_tiles, chan_rows, LANES), jnp.float32)],
+            scratch_shapes=[pltpu.VMEM((first_tiles, chan_rows - block_rows, LANES), jnp.float32)],
             compiler_params=params,
-        )(*main)
+        )(*main[:-1])
         for hop in range(1, lax.axis_size("tm")):
             if rest > 0:
                 takes.append(min(time_tiles, rest))
-                halos.append(from_ahead(gathered_rows[: takes[-1]], hop, 0))
+                halos.append(from_ahead(joined[: takes[-1]], hop, 0))
+                halos.append(from_ahead(main[-1][: takes[-1]], hop, 0))
                 rest -= takes[-1]
     lost = -(-sum(2**level for level in far_levels) // LANES) + tap_tiles
     early_tiles = time_tiles - lost

time: 24.7 us -> 25.8 us (1.045)
  starting transfers between devices: 8.77 us -> 9.68 us
  waiting for transfers between devices: 7.11 us -> 7.98 us
  Pallas kernels: 7.7 us -> 6.99 us
    ppermute x3 -> x4, waiting for transfers between devices: 1.59 us -> 2.45 us  [from_ahead(): return lax.ppermute(value, ('tm', 'sub'), route)]
    pallas_call x2, Pallas kernels: 3.73 us -> 3.05 us  [between_chips(): pl.pallas_call(functools.partial(trial_kernel, plan, group_count, level_c...]
    ppermute x3 -> x4, starting transfers between devices: 4.1 us -> 4.77 us  [from_ahead(): return lax.ppermute(value, ('tm', 'sub'), route)]
  transfers between devices with their start and end apart: 7 -> 8, of which waited for: 4 -> 4; matrix products, arithmetic and copies ran while one was open for 0% -> 0% of each run, Pallas kernels for 22% -> 19%
where the time goes in v4:
time: 25.8 us; the launch traced here: 25.7 us
  starting transfers between devices  9.68 us (38%)
  waiting for transfers between devices  7.98 us (31%)
  Pallas kernels  6.99 us (27%)
  local copies, waits for them, and re-layouts  0.96 us (4%)
    ppermute x3, waiting for transfers between devices, exchanged(): received.append(lax.ppermute(block, ('freq', 'sub'), route))  5.53 us
    ppermute x4, starting transfers between devices, from_ahead(): return lax.ppermute(value, ('tm', 'sub'), route)  4.77 us
    ppermute x3, starting transfers between devices, exchanged(): received.append(lax.ppermute(block, ('freq', 'sub'), route))  4.45 us
    pallas_call x2, Pallas kernels, within_chip(): pl.pallas_call(functools.partial(chip_kernel, spans, out_tiles, group_cou...  3.69 us
    pallas_call x2, Pallas kernels, between_chips(): pl.pallas_call(functools.partial(trial_kernel, plan, group_count, level_c...  3.05 us
    ppermute x4, waiting for transfers between devices, from_ahead(): return lax.ppermute(value, ('tm', 'sub'), route)  2.45 us
    unnamed x6, local copies, waits for them, and re-layouts  0.96 us
  transfers between devices with their start and end apart: 8, of which 4 were waited for; matrix products, arithmetic and copies ran while one was open for 0% of the time, Pallas kernels for 19%

profile of v4, /device:TPU:0, one launch (start us, length us, event | category | flops | bytes accessed | tf_op | source)
XLA Modules:
  0.0 25.7 jit_solution(17194407078350880586)
XLA Ops:
  0.0 0.5 %collective-permute-start.1 = (bf16[64,2048]{1,0:T(8,128)(2,1)}, bf16[64,2048]{1,0:T(8,128)(2,1)S(1)}, u32[]{:S(2)}, u32[]{:S(2)}) collective-permute-start(bf16[64,2048]{1,0:T(8,128)(2,1)} %whole.1), channel_id=1, source_target_pairs={{0,1},{1,0},{2,3},{3,2},{4,5},{5,4},{6,7},{7,6},{8,9},{9,8},{10,11... | collective-permute-start | bytes 786440 | tf_op jit(solution)/shard_map/ppermute | solution.py:45
  0.5 0.9 %copy-done = bf16[64,2048]{1,0:T(8,128)(2,1)S(1)} copy-done((bf16[64,2048]{1,0:T(8,128)(2,1)S(1)}, bf16[64,2048]{1,0:T(8,128)(2,1)}, u32[]{:S(2)}) %copy-start) | copy-done | bytes 262168
  1.4 2.7 %collective-permute-start.2 = (bf16[64,128]{1,0:T(8,128)(2,1)S(1)}, bf16[64,128]{1,0:T(8,128)(2,1)S(1)}, u32[]{:S(2)}, u32[]{:S(2)}) collective-permute-start(bf16[64,128]{1,0:T(8,128)(2,1)S(1)} %get-tuple-element.24), channel_id=1, source_target_pairs={{2,1},{3,0},{0,3},{1,2},{6,5},{7,4},{4,7},{5,6},{10,9},{11,8},{8,1... | collective-permute-start | bytes 49160 | tf_op jit(solution)/shard_map/ppermute | solution.py:40
  4.1 0.0 collective-permute-start
  4.1 0.0 collective-permute-done.1.refs_1_.refs_2_
  4.1 0.0 copy-done.1
  4.1 3.0 %shard_map.38 = (f32[15,64,128]{2,1,0:T(8,128)S(1)}, f32[128,128]{1,0:T(8,128)S(1)}) custom-call(bf16[64,2048]{1,0:T(8,128)(2,1)S(1)} %get-tuple-element.23.refs_0_, bf16[64,2048]{1,0:T(8,128)(2,1)S(1)} %collective-permute-done.1.refs_1_.refs_2_, s32[9,512]{1,0:T(8,128)S(1)} %copy-done.1), custom_call_target="tpu_custom_call" | custom-call | tf_op jit(solution)/shard_map/pallas_call | solution.py:421
  7.2 0.0 collective-permute-done.2.refs_3_
  7.2 0.7 %collective-permute-done.refs_1_ = bf16[64,128]{1,0:T(8,128)(2,1)S(1)} collective-permute-done((bf16[64,128]{1,0:T(8,128)(2,1)S(1)}, bf16[64,128]{1,0:T(8,128)(2,1)S(1)}, u32[]{:S(2)}, u32[]{:S(2)}) %collective-permute-start) | collective-permute-done | bytes 16416 | tf_op jit(solution)/shard_map/ppermute | solution.py:40
  7.9 0.7 %shard_map.39 = (bf16[16,16,128]{2,1,0:T(8,128)(2,1)S(1)}, bf16[16,16,128]{2,1,0:T(8,128)(2,1)S(1)}, bf16[16,16,128]{2,1,0:T(8,128)(2,1)S(1)}, bf16[16,16,128]{2,1,0:T(8,128)(2,1)S(1)}) custom-call(bf16[64,2048]{1,0:T(8,128)(2,1)S(1)} %get-tuple-element.23.refs_0_, bf16[64,128]{1,0:T(8,128)(2,1)S(1)} %collective-permute-done.refs_1_, ...), custom_call_target="tpu_custom_call" | custom-call | tf_op jit(solution)/shard_map/pallas_call | solution.py:421
  8.5 3.7 %collective-permute-start.4 = (bf16[16,16,128]{2,1,0:T(8,128)(2,1)S(1)}, bf16[16,16,128]{2,1,0:T(8,128)(2,1)S(1)}, u32[]{:S(2)}, u32[]{:S(2)}) collective-permute-start(bf16[16,16,128]{2,1,0:T(8,128)(2,1)S(1)} %get-tuple-element.36), channel_id=1, source_target_pairs={{0,12},{1,5},{4,8},{5,1},{8,4},{9,13},{12,0},{13,9},{2,14},{3,7},{... | collective-permute-start | bytes 196616 | tf_op jit(solution)/shard_map/ppermute | solution.py:65
  12.2 0.0 collective-permute-start.5
  12.2 0.8 %collective-permute-start.3 = (bf16[16,16,128]{2,1,0:T(8,128)(2,1)S(1)}, bf16[16,16,128]{2,1,0:T(8,128)(2,1)S(1)}, u32[]{:S(2)}, u32[]{:S(2)}) collective-permute-start(bf16[16,16,128]{2,1,0:T(8,128)(2,1)S(1)} %get-tuple-element.32), channel_id=1, source_target_pairs={{0,4},{1,9},{4,0},{5,13},{8,12},{9,1},{12,8},{13,5},{2,6},{3,11},{... | collective-permute-start | bytes 196616 | tf_op jit(solution)/shard_map/ppermute | solution.py:65
  13.0 2.4 %collective-permute-done.4.refs_1_ = bf16[16,16,128]{2,1,0:T(8,128)(2,1)S(1)} collective-permute-done((bf16[16,16,128]{2,1,0:T(8,128)(2,1)S(1)}, bf16[16,16,128]{2,1,0:T(8,128)(2,1)S(1)}, u32[]{:S(2)}, u32[]{:S(2)}) %collective-permute-start.4) | collective-permute-done | bytes 65568 | tf_op jit(solution)/shard_map/ppermute | solution.py:65
  15.3 3.2 %collective-permute-done.5.refs_2_ = bf16[16,16,128]{2,1,0:T(8,128)(2,1)S(1)} collective-permute-done((bf16[16,16,128]{2,1,0:T(8,128)(2,1)S(1)}, bf16[16,16,128]{2,1,0:T(8,128)(2,1)S(1)}, u32[]{:S(2)}, u32[]{:S(2)}) %collective-permute-start.5) | collective-permute-done | bytes 65568 | tf_op jit(solution)/shard_map/ppermute | solution.py:65
  18.5 1.5 %collective-permute-start.6 = (bf16[5,48,128]{2,1,0:T(8,128)(2,1)S(1)}, bf16[5,48,128]{2,1,0:T(8,128)(2,1)S(1)}, u32[]{:S(2)}, u32[]{:S(2)}) collective-permute-start(bf16[5,48,128]{2,1,0:T(8,128)(2,1)S(1)} %shard_map.41), channel_id=1, source_target_pairs={{2,0},{3,1},{0,2},{1,3},{6,4},{7,5},{4,6},{5,7},{10,8},{11,9},{8,1... | collective-permute-start | bytes 184328 | tf_op jit(solution)/shard_map/ppermute | solution.py:40
  20.0 0.0 copy-done.2
  20.0 0.2 shard_map.40
  20.2 0.0 collective-permute-done.3.refs_3_
  20.3 0.6 %collective-permute-start.7 = (bf16[5,16,128]{2,1,0:T(8,128)(2,1)S(1)}, bf16[5,16,128]{2,1,0:T(8,128)(2,1)S(1)}, u32[]{:S(2)}, u32[]{:S(2)}) collective-permute-start(bf16[5,16,128]{2,1,0:T(8,128)(2,1)S(1)} %slice.3), channel_id=1, source_target_pairs={{2,0},{3,1},{0,2},{1,3},{6,4},{7,5},{4,6},{5,7},{10,8},{11,9},{8,1... | collective-permute-start | bytes 61448 | tf_op jit(solution)/shard_map/ppermute | solution.py:40
  20.9 1.5 %shard_map.42 = (f32[64,1408]{1,0:T(8,128)S(1)}, bf16[2,64,128]{2,1,0:T(8,128)(2,1)S(1)}) custom-call(f32[128,128]{1,0:T(8,128)S(1)} %get-tuple-element.33.columns, bf16[768,384]{1,0:T(8,128)(2,1)S(1)} %get-tuple-element.34.taps, bf16[16,16,128]{2,1,0:T(8,128)(2,1)S(1)} %get-tuple-element.35.refs_0_, ...), custom_call_target="tpu_custom_call" | custom-call | tf_op jit(solution)/shard_map/pallas_call | solution.py:446
  22.4 1.8 %collective-permute-done.7.refs_5_ = bf16[5,16,128]{2,1,0:T(8,128)(2,1)S(1)} collective-permute-done((bf16[5,16,128]{2,1,0:T(8,128)(2,1)S(1)}, bf16[5,16,128]{2,1,0:T(8,128)(2,1)S(1)}, u32[]{:S(2)}, u32[]{:S(2)}) %collective-permute-start.7) | collective-permute-done | bytes 20512 | tf_op jit(solution)/shard_map/ppermute | solution.py:40
  24.1 0.0 collective-permute-done.6.refs_4_
  24.1 1.6 %shard_map.43 = f32[64,2048]{1,0:T(8,128)} custom-call(f32[128,128]{1,0:T(8,128)S(1)} %get-tuple-element.33.columns, bf16[768,384]{1,0:T(8,128)(2,1)S(1)} %get-tuple-element.34.taps, bf16[16,16,128]{2,1,0:T(8,128)(2,1)S(1)} %get-tuple-element.35.refs_0_, bf16[16,16,128]{2,1,0:T(8,128)(2,1)S(1)} %collective-permute-done.4.refs_1_, ...), custom_call_target="tpu_custom_call" | custom-call | tf_op jit(solution)/shard_map/pallas_call | solution.py:446
  (6 shorter events, 0.0 us)
Async XLA Ops:
  0.0 4.1 %collective-permute-start.1 = (bf16[64,2048]{1,0:T(8,128)(2,1)}, bf16[64,2048]{1,0:T(8,128)(2,1)S(1)}, u32[]{:S(2)}, u32[]{:S(2)}) collective-permute-start(bf16[64,2048]{1,0:T(8,128)(2,1)} %whole.1), channel_id=1, source_target_pairs={{0,1},{1,0},{2,3},{3,2},{4,5},{5,4},{6,7},{7,6},{8,9},{9,8},{10,11... | collective-permute-start | bytes 786440 | tf_op jit(solution)/shard_map/ppermute | solution.py:45
  0.5 0.9 %copy-start = (bf16[64,2048]{1,0:T(8,128)(2,1)S(1)}, bf16[64,2048]{1,0:T(8,128)(2,1)}, u32[]{:S(2)}) copy-start(bf16[64,2048]{1,0:T(8,128)(2,1)} %whole.1) | copy-start | bytes 786436
  1.4 2.7 %copy-start.1 = (s32[9,512]{1,0:T(8,128)S(1)}, s32[9,512]{1,0:T(8,128)}, u32[]{:S(2)}) copy-start(s32[9,512]{1,0:T(8,128)} %shifts) | copy-start | bytes 55300
  1.4 5.7 %collective-permute-start.2 = (bf16[64,128]{1,0:T(8,128)(2,1)S(1)}, bf16[64,128]{1,0:T(8,128)(2,1)S(1)}, u32[]{:S(2)}, u32[]{:S(2)}) collective-permute-start(bf16[64,128]{1,0:T(8,128)(2,1)S(1)} %get-tuple-element.24), channel_id=1, source_target_pairs={{2,1},{3,0},{0,3},{1,2},{6,5},{7,4},{4,7},{5,6},{10,9},{11,8},{8,1... | collective-permute-start | bytes 49160 | tf_op jit(solution)/shard_map/ppermute | solution.py:40
  4.1 3.7 %collective-permute-start = (bf16[64,128]{1,0:T(8,128)(2,1)S(1)}, bf16[64,128]{1,0:T(8,128)(2,1)S(1)}, u32[]{:S(2)}, u32[]{:S(2)}) collective-permute-start(bf16[64,128]{1,0:T(8,128)(2,1)S(1)} %get-tuple-element.24), channel_id=1, source_target_pairs={{2,0},{3,1},{0,2},{1,3},{6,4},{7,5},{4,6},{5,7},{10,8},{11,9},{8,1... | collective-permute-start | bytes 49160 | tf_op jit(solution)/shard_map/ppermute | solution.py:40
  8.5 6.8 %collective-permute-start.4 = (bf16[16,16,128]{2,1,0:T(8,128)(2,1)S(1)}, bf16[16,16,128]{2,1,0:T(8,128)(2,1)S(1)}, u32[]{:S(2)}, u32[]{:S(2)}) collective-permute-start(bf16[16,16,128]{2,1,0:T(8,128)(2,1)S(1)} %get-tuple-element.36), channel_id=1, source_target_pairs={{0,12},{1,5},{4,8},{5,1},{8,4},{9,13},{12,0},{13,9},{2,14},{3,7},{... | collective-permute-start | bytes 196616 | tf_op jit(solution)/shard_map/ppermute | solution.py:65
  12.2 6.3 %collective-permute-start.5 = (bf16[16,16,128]{2,1,0:T(8,128)(2,1)S(1)}, bf16[16,16,128]{2,1,0:T(8,128)(2,1)S(1)}, u32[]{:S(2)}, u32[]{:S(2)}) collective-permute-start(bf16[16,16,128]{2,1,0:T(8,128)(2,1)S(1)} %get-tuple-element.37), channel_id=1, source_target_pairs={{0,8},{1,13},{4,12},{5,9},{8,0},{9,5},{12,4},{13,1},{2,10},{3,15},... | collective-permute-start | bytes 196616 | tf_op jit(solution)/shard_map/ppermute | solution.py:65
  12.2 8.1 %collective-permute-start.3 = (bf16[16,16,128]{2,1,0:T(8,128)(2,1)S(1)}, bf16[16,16,128]{2,1,0:T(8,128)(2,1)S(1)}, u32[]{:S(2)}, u32[]{:S(2)}) collective-permute-start(bf16[16,16,128]{2,1,0:T(8,128)(2,1)S(1)} %get-tuple-element.32), channel_id=1, source_target_pairs={{0,4},{1,9},{4,0},{5,13},{8,12},{9,1},{12,8},{13,5},{2,6},{3,11},{... | collective-permute-start | bytes 196616 | tf_op jit(solution)/shard_map/ppermute | solution.py:65
  13.0 7.0 %copy-start.2 = (bf16[6,256]{1,0:T(8,128)(2,1)S(1)}, bf16[6,256]{1,0:T(8,128)(2,1)}, u32[]{:S(2)}) copy-start(bf16[6,256]{1,0:T(8,128)(2,1)} %filters) | copy-start | bytes 9220
  18.5 5.6 %collective-permute-start.6 = (bf16[5,48,128]{2,1,0:T(8,128)(2,1)S(1)}, bf16[5,48,128]{2,1,0:T(8,128)(2,1)S(1)}, u32[]{:S(2)}, u32[]{:S(2)}) collective-permute-start(bf16[5,48,128]{2,1,0:T(8,128)(2,1)S(1)} %shard_map.41), channel_id=1, source_target_pairs={{2,0},{3,1},{0,2},{1,3},{6,4},{7,5},{4,6},{5,7},{10,8},{11,9},{8,1... | collective-permute-start | bytes 184328 | tf_op jit(solution)/shard_map/ppermute | solution.py:40
  20.3 3.8 %collective-permute-start.7 = (bf16[5,16,128]{2,1,0:T(8,128)(2,1)S(1)}, bf16[5,16,128]{2,1,0:T(8,128)(2,1)S(1)}, u32[]{:S(2)}, u32[]{:S(2)}) collective-permute-start(bf16[5,16,128]{2,1,0:T(8,128)(2,1)S(1)} %slice.3), channel_id=1, source_target_pairs={{2,0},{3,1},{0,2},{1,3},{6,4},{7,5},{4,6},{5,7},{10,8},{11,9},{8,1... | collective-permute-start | bytes 61448 | tf_op jit(solution)/shard_map/ppermute | solution.py:40

commit v5 on v4

--- a/solution.py
+++ b/solution.py
@@ -46,7 +46,7 @@
 
 
 def mask_orders(group_count):
-    order = list(range(group_count - 1, 0, -1))
+    order = [1, *range(group_count - 1, 1, -1)]
     return order, order[-1:] + order[:-1]
 
 
@@ -64,6 +64,21 @@
         ]
         received.append(lax.ppermute(block, ("freq", "sub"), route))
     return received
+
+
+def from_ahead_chip(block, steps):
+    chips, times = lax.axis_size("freq"), lax.axis_size("tm")
+    last = [order[-1] for order in mask_orders(chips)]
+    route = [
+        (
+            ((chip ^ last[core]) * times + (time + steps) % times) * 2 + core,
+            (chip * times + time) * 2 + core,
+        )
+        for chip in range(chips)
+        for time in range(times)
+        for core in range(2)
+    ]
+    return lax.ppermute(block, ("freq", "tm", "sub"), route)
 
 
 def lanes():
@@ -492,6 +507,7 @@
         scratch_shapes=[table],
         compiler_params=params,
     )(late_shifts, late_filters)
+    sent = main[-1]
     *main, last = exchanged(main)
     columns, taps, last = lax.optimization_barrier((columns, taps, last))
     main.append(last)
@@ -514,7 +530,7 @@
             if rest > 0:
                 takes.append(min(time_tiles, rest))
                 halos.append(from_ahead(joined[: takes[-1]], hop, 0))
-                halos.append(from_ahead(main[-1][: takes[-1]], hop, 0))
+                halos.append(from_ahead_chip(sent[: takes[-1]], hop))
                 rest -= takes[-1]
     lost = -(-sum(2**level for level in far_levels) // LANES) + tap_tiles
     early_tiles = time_tiles - lost

time: 25.8 us -> 25 us (0.969)
  waiting for transfers between devices: 7.98 us -> 5.27 us
  starting transfers between devices: 9.68 us -> 11.6 us
    ppermute x0 -> x1, starting transfers between devices: none -> 2.94 us  [from_ahead_chip(): return lax.ppermute(block, ('freq', 'tm', 'sub'), route)]
    ppermute x3, waiting for transfers between devices: 5.53 us -> 3.69 us  [exchanged(): received.append(lax.ppermute(block, ('freq', 'sub'), route))]
    ppermute x4 -> x3, waiting for transfers between devices: 2.45 us -> 0.69 us  [from_ahead(): return lax.ppermute(value, ('tm', 'sub'), route)]
    ppermute x0 -> x1, waiting for transfers between devices: none -> 0.89 us  [from_ahead_chip(): return lax.ppermute(block, ('freq', 'tm', 'sub'), route)]
    ppermute x4 -> x3, starting transfers between devices: 4.77 us -> 3.99 us  [from_ahead(): return lax.ppermute(value, ('tm', 'sub'), route)]
where the time goes in v5:
time: 25 us; the launch traced here: 24.9 us
  starting transfers between devices  11.6 us (46%)
  Pallas kernels  6.99 us (28%)
  waiting for transfers between devices  5.27 us (21%)
  local copies, waits for them, and re-layouts  0.96 us (4%)
    ppermute x3, starting transfers between devices, exchanged(): received.append(lax.ppermute(block, ('freq', 'sub'), route))  4.22 us
    ppermute x3, starting transfers between devices, from_ahead(): return lax.ppermute(value, ('tm', 'sub'), route)  3.99 us
    pallas_call x2, Pallas kernels, within_chip(): pl.pallas_call(functools.partial(chip_kernel, spans, out_tiles, group_cou...  3.69 us
    ppermute x3, waiting for transfers between devices, exchanged(): received.append(lax.ppermute(block, ('freq', 'sub'), route))  3.69 us
    pallas_call x2, Pallas kernels, between_chips(): pl.pallas_call(functools.partial(trial_kernel, plan, group_count, level_c...  3.05 us
    ppermute x1, starting transfers between devices, from_ahead_chip(): return lax.ppermute(block, ('freq', 'tm', 'sub'), route)  2.94 us
    unnamed x6, local copies, waits for them, and re-layouts  0.96 us
    ppermute x1, waiting for transfers between devices, from_ahead_chip(): return lax.ppermute(block, ('freq', 'tm', 'sub'), route)  0.89 us
  transfers between devices with their start and end apart: 8, of which 4 were waited for; matrix products, arithmetic and copies ran while one was open for 0% of the time, Pallas kernels for 19%

profile of v5, /device:TPU:0, one launch (start us, length us, event | category | flops | bytes accessed | tf_op | source)
XLA Modules:
  0.0 24.9 jit_solution(6828527139507037047)
XLA Ops:
  0.0 0.5 %collective-permute-start.1 = (bf16[64,2048]{1,0:T(8,128)(2,1)}, bf16[64,2048]{1,0:T(8,128)(2,1)S(1)}, u32[]{:S(2)}, u32[]{:S(2)}) collective-permute-start(bf16[64,2048]{1,0:T(8,128)(2,1)} %whole.1), channel_id=1, source_target_pairs={{0,1},{1,0},{2,3},{3,2},{4,5},{5,4},{6,7},{7,6},{8,9},{9,8},{10,11... | collective-permute-start | bytes 786440 | tf_op jit(solution)/shard_map/ppermute | solution.py:45
  0.5 0.9 %copy-done = bf16[64,2048]{1,0:T(8,128)(2,1)S(1)} copy-done((bf16[64,2048]{1,0:T(8,128)(2,1)S(1)}, bf16[64,2048]{1,0:T(8,128)(2,1)}, u32[]{:S(2)}) %copy-start) | copy-done | bytes 262168
  1.4 2.7 %collective-permute-start.2 = (bf16[64,128]{1,0:T(8,128)(2,1)S(1)}, bf16[64,128]{1,0:T(8,128)(2,1)S(1)}, u32[]{:S(2)}, u32[]{:S(2)}) collective-permute-start(bf16[64,128]{1,0:T(8,128)(2,1)S(1)} %get-tuple-element.24), channel_id=1, source_target_pairs={{2,1},{3,0},{0,3},{1,2},{6,5},{7,4},{4,7},{5,6},{10,9},{11,8},{8,1... | collective-permute-start | bytes 49160 | tf_op jit(solution)/shard_map/ppermute | solution.py:40
  4.1 0.0 collective-permute-start
  4.1 0.0 collective-permute-done.1.refs_1_.refs_2_
  4.1 0.0 copy-done.1
  4.1 3.0 %shard_map.38 = (f32[15,64,128]{2,1,0:T(8,128)S(1)}, f32[128,128]{1,0:T(8,128)S(1)}) custom-call(bf16[64,2048]{1,0:T(8,128)(2,1)S(1)} %get-tuple-element.23.refs_0_, bf16[64,2048]{1,0:T(8,128)(2,1)S(1)} %collective-permute-done.1.refs_1_.refs_2_, s32[9,512]{1,0:T(8,128)S(1)} %copy-done.1), custom_call_target="tpu_custom_call" | custom-call | tf_op jit(solution)/shard_map/pallas_call | solution.py:436
  7.2 0.0 collective-permute-done.2.refs_3_
  7.2 0.7 %collective-permute-done.refs_1_ = bf16[64,128]{1,0:T(8,128)(2,1)S(1)} collective-permute-done((bf16[64,128]{1,0:T(8,128)(2,1)S(1)}, bf16[64,128]{1,0:T(8,128)(2,1)S(1)}, u32[]{:S(2)}, u32[]{:S(2)}) %collective-permute-start) | collective-permute-done | bytes 16416 | tf_op jit(solution)/shard_map/ppermute | solution.py:40
  7.9 0.7 %shard_map.39 = (bf16[16,16,128]{2,1,0:T(8,128)(2,1)S(1)}, bf16[16,16,128]{2,1,0:T(8,128)(2,1)S(1)}, bf16[16,16,128]{2,1,0:T(8,128)(2,1)S(1)}, bf16[16,16,128]{2,1,0:T(8,128)(2,1)S(1)}) custom-call(bf16[64,2048]{1,0:T(8,128)(2,1)S(1)} %get-tuple-element.23.refs_0_, bf16[64,128]{1,0:T(8,128)(2,1)S(1)} %collective-permute-done.refs_1_, ...), custom_call_target="tpu_custom_call" | custom-call | tf_op jit(solution)/shard_map/pallas_call | solution.py:436
  8.5 1.6 %collective-permute-start.4 = (bf16[16,16,128]{2,1,0:T(8,128)(2,1)S(1)}, bf16[16,16,128]{2,1,0:T(8,128)(2,1)S(1)}, u32[]{:S(2)}, u32[]{:S(2)}) collective-permute-start(bf16[16,16,128]{2,1,0:T(8,128)(2,1)S(1)} %get-tuple-element.36), channel_id=1, source_target_pairs={{0,4},{1,9},{4,0},{5,13},{8,12},{9,1},{12,8},{13,5},{2,6},{3,11},{... | collective-permute-start | bytes 196616 | tf_op jit(solution)/shard_map/ppermute | solution.py:65
  10.1 2.5 %collective-permute-start.5 = (bf16[16,16,128]{2,1,0:T(8,128)(2,1)S(1)}, bf16[16,16,128]{2,1,0:T(8,128)(2,1)S(1)}, u32[]{:S(2)}, u32[]{:S(2)}) collective-permute-start(bf16[16,16,128]{2,1,0:T(8,128)(2,1)S(1)} %get-tuple-element.37), channel_id=1, source_target_pairs={{0,12},{1,5},{4,8},{5,1},{8,4},{9,13},{12,0},{13,9},{2,14},{3,7},{... | collective-permute-start | bytes 196616 | tf_op jit(solution)/shard_map/ppermute | solution.py:65
  12.6 0.1 collective-permute-start.3
  12.7 0.3 %collective-permute-done.4.refs_1_ = bf16[16,16,128]{2,1,0:T(8,128)(2,1)S(1)} collective-permute-done((bf16[16,16,128]{2,1,0:T(8,128)(2,1)S(1)}, bf16[16,16,128]{2,1,0:T(8,128)(2,1)S(1)}, u32[]{:S(2)}, u32[]{:S(2)}) %collective-permute-start.4) | collective-permute-done | bytes 65568 | tf_op jit(solution)/shard_map/ppermute | solution.py:65
  13.0 3.4 %collective-permute-done.5.refs_2_ = bf16[16,16,128]{2,1,0:T(8,128)(2,1)S(1)} collective-permute-done((bf16[16,16,128]{2,1,0:T(8,128)(2,1)S(1)}, bf16[16,16,128]{2,1,0:T(8,128)(2,1)S(1)}, u32[]{:S(2)}, u32[]{:S(2)}) %collective-permute-start.5) | collective-permute-done | bytes 65568 | tf_op jit(solution)/shard_map/ppermute | solution.py:65
  16.4 1.3 %collective-permute-start.6 = (bf16[5,48,128]{2,1,0:T(8,128)(2,1)S(1)}, bf16[5,48,128]{2,1,0:T(8,128)(2,1)S(1)}, u32[]{:S(2)}, u32[]{:S(2)}) collective-permute-start(bf16[5,48,128]{2,1,0:T(8,128)(2,1)S(1)} %shard_map.41), channel_id=1, source_target_pairs={{2,0},{3,1},{0,2},{1,3},{6,4},{7,5},{4,6},{5,7},{10,8},{11,9},{8,1... | collective-permute-start | bytes 184328 | tf_op jit(solution)/shard_map/ppermute | solution.py:40
  17.7 2.9 %collective-permute-start.7 = (bf16[5,16,128]{2,1,0:T(8,128)(2,1)S(1)}, bf16[5,16,128]{2,1,0:T(8,128)(2,1)S(1)}, u32[]{:S(2)}, u32[]{:S(2)}) collective-permute-start(bf16[5,16,128]{2,1,0:T(8,128)(2,1)S(1)} %slice.3), channel_id=1, source_target_pairs={{10,0},{15,1},{8,2},{13,3},{14,4},{11,5},{12,6},{9,7},{2,8},{7,9},... | collective-permute-start | bytes 61448 | tf_op jit(solution)/shard_map/ppermute | solution.py:81
  20.7 0.0 copy-done.2
  20.7 0.2 shard_map.40
  20.9 0.0 collective-permute-done.3.refs_3_
  20.9 1.5 %shard_map.42 = (f32[64,1408]{1,0:T(8,128)S(1)}, bf16[2,64,128]{2,1,0:T(8,128)(2,1)S(1)}) custom-call(f32[128,128]{1,0:T(8,128)S(1)} %get-tuple-element.33.columns, bf16[768,384]{1,0:T(8,128)(2,1)S(1)} %get-tuple-element.34.taps, bf16[16,16,128]{2,1,0:T(8,128)(2,1)S(1)} %get-tuple-element.35.refs_0_, ...), custom_call_target="tpu_custom_call" | custom-call | tf_op jit(solution)/shard_map/pallas_call | solution.py:461
  22.4 0.9 %collective-permute-done.7.refs_5_ = bf16[5,16,128]{2,1,0:T(8,128)(2,1)S(1)} collective-permute-done((bf16[5,16,128]{2,1,0:T(8,128)(2,1)S(1)}, bf16[5,16,128]{2,1,0:T(8,128)(2,1)S(1)}, u32[]{:S(2)}, u32[]{:S(2)}) %collective-permute-start.7) | collective-permute-done | bytes 20512 | tf_op jit(solution)/shard_map/ppermute | solution.py:81
  23.3 0.0 collective-permute-done.6.refs_4_
  23.3 1.6 %shard_map.43 = f32[64,2048]{1,0:T(8,128)} custom-call(f32[128,128]{1,0:T(8,128)S(1)} %get-tuple-element.33.columns, bf16[768,384]{1,0:T(8,128)(2,1)S(1)} %get-tuple-element.34.taps, bf16[16,16,128]{2,1,0:T(8,128)(2,1)S(1)} %get-tuple-element.35.refs_0_, bf16[16,16,128]{2,1,0:T(8,128)(2,1)S(1)} %collective-permute-done.4.refs_1_, ...), custom_call_target="tpu_custom_call" | custom-call | tf_op jit(solution)/shard_map/pallas_call | solution.py:461
  (6 shorter events, 0.0 us)
Async XLA Ops:
  0.0 4.1 %collective-permute-start.1 = (bf16[64,2048]{1,0:T(8,128)(2,1)}, bf16[64,2048]{1,0:T(8,128)(2,1)S(1)}, u32[]{:S(2)}, u32[]{:S(2)}) collective-permute-start(bf16[64,2048]{1,0:T(8,128)(2,1)} %whole.1), channel_id=1, source_target_pairs={{0,1},{1,0},{2,3},{3,2},{4,5},{5,4},{6,7},{7,6},{8,9},{9,8},{10,11... | collective-permute-start | bytes 786440 | tf_op jit(solution)/shard_map/ppermute | solution.py:45
  0.5 0.9 %copy-start = (bf16[64,2048]{1,0:T(8,128)(2,1)S(1)}, bf16[64,2048]{1,0:T(8,128)(2,1)}, u32[]{:S(2)}) copy-start(bf16[64,2048]{1,0:T(8,128)(2,1)} %whole.1) | copy-start | bytes 786436
  1.4 2.7 %copy-start.1 = (s32[9,512]{1,0:T(8,128)S(1)}, s32[9,512]{1,0:T(8,128)}, u32[]{:S(2)}) copy-start(s32[9,512]{1,0:T(8,128)} %shifts) | copy-start | bytes 55300
  1.4 5.7 %collective-permute-start.2 = (bf16[64,128]{1,0:T(8,128)(2,1)S(1)}, bf16[64,128]{1,0:T(8,128)(2,1)S(1)}, u32[]{:S(2)}, u32[]{:S(2)}) collective-permute-start(bf16[64,128]{1,0:T(8,128)(2,1)S(1)} %get-tuple-element.24), channel_id=1, source_target_pairs={{2,1},{3,0},{0,3},{1,2},{6,5},{7,4},{4,7},{5,6},{10,9},{11,8},{8,1... | collective-permute-start | bytes 49160 | tf_op jit(solution)/shard_map/ppermute | solution.py:40
  4.1 3.7 %collective-permute-start = (bf16[64,128]{1,0:T(8,128)(2,1)S(1)}, bf16[64,128]{1,0:T(8,128)(2,1)S(1)}, u32[]{:S(2)}, u32[]{:S(2)}) collective-permute-start(bf16[64,128]{1,0:T(8,128)(2,1)S(1)} %get-tuple-element.24), channel_id=1, source_target_pairs={{2,0},{3,1},{0,2},{1,3},{6,4},{7,5},{4,6},{5,7},{10,8},{11,9},{8,1... | collective-permute-start | bytes 49160 | tf_op jit(solution)/shard_map/ppermute | solution.py:40
  8.5 4.5 %collective-permute-start.4 = (bf16[16,16,128]{2,1,0:T(8,128)(2,1)S(1)}, bf16[16,16,128]{2,1,0:T(8,128)(2,1)S(1)}, u32[]{:S(2)}, u32[]{:S(2)}) collective-permute-start(bf16[16,16,128]{2,1,0:T(8,128)(2,1)S(1)} %get-tuple-element.36), channel_id=1, source_target_pairs={{0,4},{1,9},{4,0},{5,13},{8,12},{9,1},{12,8},{13,5},{2,6},{3,11},{... | collective-permute-start | bytes 196616 | tf_op jit(solution)/shard_map/ppermute | solution.py:65
  10.1 6.3 %collective-permute-start.5 = (bf16[16,16,128]{2,1,0:T(8,128)(2,1)S(1)}, bf16[16,16,128]{2,1,0:T(8,128)(2,1)S(1)}, u32[]{:S(2)}, u32[]{:S(2)}) collective-permute-start(bf16[16,16,128]{2,1,0:T(8,128)(2,1)S(1)} %get-tuple-element.37), channel_id=1, source_target_pairs={{0,12},{1,5},{4,8},{5,1},{8,4},{9,13},{12,0},{13,9},{2,14},{3,7},{... | collective-permute-start | bytes 196616 | tf_op jit(solution)/shard_map/ppermute | solution.py:65
  12.6 8.3 %collective-permute-start.3 = (bf16[16,16,128]{2,1,0:T(8,128)(2,1)S(1)}, bf16[16,16,128]{2,1,0:T(8,128)(2,1)S(1)}, u32[]{:S(2)}, u32[]{:S(2)}) collective-permute-start(bf16[16,16,128]{2,1,0:T(8,128)(2,1)S(1)} %get-tuple-element.32), channel_id=1, source_target_pairs={{0,8},{1,13},{4,12},{5,9},{8,0},{9,5},{12,4},{13,1},{2,10},{3,15},... | collective-permute-start | bytes 196616 | tf_op jit(solution)/shard_map/ppermute | solution.py:65
  16.4 4.3 %copy-start.2 = (bf16[6,256]{1,0:T(8,128)(2,1)S(1)}, bf16[6,256]{1,0:T(8,128)(2,1)}, u32[]{:S(2)}) copy-start(bf16[6,256]{1,0:T(8,128)(2,1)} %filters) | copy-start | bytes 9220
  16.4 6.9 %collective-permute-start.6 = (bf16[5,48,128]{2,1,0:T(8,128)(2,1)S(1)}, bf16[5,48,128]{2,1,0:T(8,128)(2,1)S(1)}, u32[]{:S(2)}, u32[]{:S(2)}) collective-permute-start(bf16[5,48,128]{2,1,0:T(8,128)(2,1)S(1)} %shard_map.41), channel_id=1, source_target_pairs={{2,0},{3,1},{0,2},{1,3},{6,4},{7,5},{4,6},{5,7},{10,8},{11,9},{8,1... | collective-permute-start | bytes 184328 | tf_op jit(solution)/shard_map/ppermute | solution.py:40
  17.7 5.6 %collective-permute-start.7 = (bf16[5,16,128]{2,1,0:T(8,128)(2,1)S(1)}, bf16[5,16,128]{2,1,0:T(8,128)(2,1)S(1)}, u32[]{:S(2)}, u32[]{:S(2)}) collective-permute-start(bf16[5,16,128]{2,1,0:T(8,128)(2,1)S(1)} %slice.3), channel_id=1, source_target_pairs={{10,0},{15,1},{8,2},{13,3},{14,4},{11,5},{12,6},{9,7},{2,8},{7,9},... | collective-permute-start | bytes 61448 | tf_op jit(solution)/shard_map/ppermute | solution.py:81

commit v6 on v4

--- a/solution.py
+++ b/solution.py
@@ -46,7 +46,7 @@
 
 
 def mask_orders(group_count):
-    order = list(range(group_count - 1, 0, -1))
+    order = [1, *range(group_count - 1, 1, -1)]
     return order, order[-1:] + order[:-1]
 
 
@@ -177,34 +177,36 @@
     ahead[...] = whole[:, : ahead.shape[1]]
 
 
-def placed(target, blocks, tiles, skip):
+def placed(target, blocks, first, skip):
     chip, core = lax.axis_index("freq"), lax.axis_index("sub")
-    rows = blocks[0].shape[1]
+    tiles, rows = blocks[0].shape[:2]
     for mask, block in zip(step_masks(len(blocks), core), blocks):
         start = pl.multiple_of((chip ^ mask) * rows, rows)
-        for tile in range(skip, tiles):
-            target[tile - skip, pl.ds(start, rows), :] = block[tile, :, :].astype(jnp.float32)
-
-
-def join_kernel(*refs):
+        for tile in range(max(skip - first, 0), tiles):
+            target[first + tile - skip, pl.ds(start, rows), :] = block[tile, :, :].astype(jnp.float32)
+
+
+def join_kernel(group_count, *refs):
     *blocks, out, state = refs
-    rows = blocks[0].shape[1]
+    split, rows = blocks[0].shape[:2]
     for tile in range(out.shape[0]):
-        for index, block in enumerate(blocks):
-            state[tile, index * rows : (index + 1) * rows, :] = block[tile, :, :].astype(jnp.float32)
+        for index in range(group_count):
+            block = blocks[tile // split * group_count + index]
+            state[tile, index * rows : (index + 1) * rows, :] = block[tile % split, :, :].astype(jnp.float32)
         out[tile, :, :] = state[tile, :, :].astype(jnp.bfloat16)
 
 
-def chip_kernel(spans, out_tiles, group_count, *refs):
+def chip_kernel(spans, out_tiles, group_count, tabled, *refs):
     pieces = (refs[: len(spans)], refs[len(spans) : 2 * len(spans)])
-    refs = refs[2 * len(spans) :]
+    given, *refs = refs[2 * len(spans) :]
+    blocks, refs = refs[:group_count], refs[group_count:]
     chan_rows = pieces[0][0].shape[0]
     local_count = bits_of(chan_rows)
     chip, core = lax.axis_index("freq"), lax.axis_index("sub")
-    if group_count:
-        (earlier, columns), blocks, (raw, ping, pong) = refs[:2], refs[2:-3], refs[-3:]
+    if tabled:
+        columns, (raw, ping, pong) = given, refs
     else:
-        shifts, rows, columns, raw, ping, pong, table = refs
+        shifts, (columns, raw, ping, pong, table) = given, refs
         chunk = shifts[0:SUBLANES, pl.ds(pl.multiple_of(chip * LANES, LANES), LANES)]
         lane, level = lanes(), lax.broadcasted_iota(jnp.int32, (SUBLANES, LANES), 0)
         kept = lane & (1 << level) - 1
@@ -235,19 +237,12 @@
             ping[tile, pl.ds(vector * SUBLANES, SUBLANES), :] = raw[tile, low, :] + moved
             upper = later
     last = tree_levels(ping, pong, columns, 1, levels[1:], 1, lengths[1:], packed=True)
-    if not group_count:
-        for tile in range(out_tiles):
-            rows[tile, :, :] = last[tile, :, :]
-        return
     size = chan_rows // group_count
     own = reversed_bits(chip, bits_of(group_count))
-    first = earlier.shape[0]
     for mask, block in zip(step_masks(group_count, core), blocks):
         start = pl.multiple_of((own ^ reversed_bits(mask, bits_of(group_count))) * size, size)
-        for tile in range(first):
-            block[tile, :, :] = earlier[tile, pl.ds(start, size), :].astype(jnp.bfloat16)
         for tile in range(out_tiles):
-            block[first + tile, :, :] = last[tile, pl.ds(start, size), :].astype(jnp.bfloat16)
+            block[tile, :, :] = last[tile, pl.ds(start, size), :].astype(jnp.bfloat16)
 
 
 def toeplitz(filters, target):
@@ -291,8 +286,11 @@
 
 
 def trial_kernel(plan, group_count, level_count, scale, columns, taps, *refs):
-    blocks, refs = refs[:group_count], refs[group_count:]
-    halos, refs = refs[: 2 * len(plan.halos)], refs[2 * len(plan.halos) :]
+    parts = []
+    for first in plan.parts:
+        parts.append((first, refs[:group_count]))
+        refs = refs[group_count:]
+    halos, refs = refs[: len(plan.halos)], refs[len(plan.halos) :]
     if plan.taken:
         carried, so_far, refs = refs[0], refs[1], refs[2:]
     out, refs = refs[0], refs[1:]
@@ -312,22 +310,17 @@
         place = out.at[:, pl.ds(0, plan.out_first * LANES)]
         copies.append(pltpu.make_async_copy(so_far, place, arrived.at[len(plan.chunks)]))
         copies[0].start()
-    placed(state, blocks, plan.main_tiles, plan.first)
+    for first, blocks in parts:
+        placed(state, blocks, first, plan.first)
     at = plan.main_tiles - plan.first
     chip, core = lax.axis_index("freq"), lax.axis_index("sub")
     for hop, tiles in enumerate(plan.halos, 1):
         there = lax.axis_index("tm") + hop < lax.axis_size("tm")
         for tile in range(tiles):
-            joined, single = [
-                jnp.where(there, halo[tile, :, :].astype(jnp.float32), 0.0)
-                for halo in halos[2 * hop - 2 : 2 * hop]
-            ]
+            joined = jnp.where(there, halos[hop - 1][tile, :, :].astype(jnp.float32), 0.0)
             for index, mask in enumerate(step_masks(group_count, core)):
                 start = pl.multiple_of((chip ^ mask) * block_rows, block_rows)
-                if index + 1 < group_count:
-                    part = joined[index * block_rows : (index + 1) * block_rows]
-                else:
-                    part = single
+                part = joined[index * block_rows : (index + 1) * block_rows]
                 state[at, pl.ds(start, block_rows), :] = part
             at += 1
     for tile in range(at, at + plan.empty_tiles):
@@ -376,7 +369,8 @@
 
 
 class Plan:
-    def __init__(self, main_tiles, halos, empty_tiles, out_first, out_tiles, taken, given, levels, tap_tiles):
+    def __init__(self, parts, main_tiles, halos, empty_tiles, out_first, out_tiles, taken, given, levels, tap_tiles):
+        self.parts = parts
         self.main_tiles, self.halos, self.empty_tiles = main_tiles, halos, empty_tiles
         self.out_first, self.out_tiles = out_first, out_tiles
         self.taken, self.given = taken, given
@@ -408,23 +402,18 @@
     block_rows = chan_rows // group_count
     table = pltpu.VMEM((LANES, LANES), jnp.float32)
 
-    def within_chip(operands, spans, raw_tiles, out_tiles, sending):
+    def within_chip(operands, spans, raw_tiles, out_tiles, tabled):
         state = pltpu.VMEM((raw_tiles + 1, chan_rows, LANES), jnp.float32)
-        if sending:
-            block = jax.ShapeDtypeStruct((time_tiles, block_rows, LANES), jnp.bfloat16)
-            out_shape = [block] * group_count
-        else:
-            out_shape = [
-                jax.ShapeDtypeStruct((out_tiles, chan_rows, LANES), jnp.float32),
-                jax.ShapeDtypeStruct((LANES, LANES), jnp.float32),
-            ]
+        out_shape = [jax.ShapeDtypeStruct((out_tiles, block_rows, LANES), jnp.bfloat16)] * group_count
+        if not tabled:
+            out_shape.append(jax.ShapeDtypeStruct((LANES, LANES), jnp.float32))
         return pl.pallas_call(
-            functools.partial(chip_kernel, spans, out_tiles, group_count if sending else 0),
+            functools.partial(chip_kernel, spans, out_tiles, group_count, tabled),
             out_shape=out_shape,
             in_specs=[in_vmem] * len(operands),
             out_specs=[in_vmem] * len(out_shape),
             scratch_shapes=[pltpu.VMEM((raw_tiles + 1, 2 * chan_rows, LANES), jnp.float32), state, state]
-            + ([] if sending else [table]),
+            + ([] if tabled else [table]),
             compiler_params=params,
         )(*operands)
 
@@ -470,17 +459,22 @@
         compiler_params=params,
     )(filterbank)
     near_tiles = near_len // LANES
-    early = time_tiles - near_tiles
-    rows, delays = within_chip(
-        [own, other_core, delay_shifts], [(0, time_len, 0)], time_tiles, early, False
+    split = time_tiles * 5 // 8
+    *front, delays = within_chip(
+        [own, other_core, delay_shifts], [(0, (split + near_tiles) * LANES, 0)], split + near_tiles, split, False
     )
-    both, spans = ([own], [other_core]), [(early * LANES, near_len, 0)]
+    front = exchanged(front)
+    both, spans = ([own], [other_core]), [(split * LANES, time_len - split * LANES, 0)]
     if lax.axis_size("tm") > 1:
         for crossed in range(2):
             both[crossed].append(from_ahead(ahead, 1, crossed))
         spans.append((0, near_len, 1))
-    main = list(within_chip([*both[0], *both[1], rows, delays], spans, 2 * near_tiles, near_tiles, True))
-    late_shifts, late_filters, main[0] = lax.optimization_barrier((delay_shifts, pulse_filters, main[0]))
+    back_tiles = time_tiles - split
+    back = within_chip([*both[0], *both[1], delays], spans, back_tiles + near_tiles, back_tiles, True)
+    back = list(back)
+    late_shifts, late_filters, back[0] = lax.optimization_barrier((delay_shifts, pulse_filters, back[0]))
+    front = list(lax.optimization_barrier((*front, back[0])))
+    back[0] = front.pop()
     columns, taps = pl.pallas_call(
         functools.partial(table_kernel, group_count, block_rows),
         out_shape=[
@@ -492,40 +486,39 @@
         scratch_shapes=[table],
         compiler_params=params,
     )(late_shifts, late_filters)
-    *main, last = exchanged(main)
+    *back, last = exchanged(back)
     columns, taps, last = lax.optimization_barrier((columns, taps, last))
-    main.append(last)
+    back.append(last)
 
     halos, takes = [], []
     rest = far_tiles
     if lax.axis_size("tm") > 1:
         first_tiles = min(time_tiles, far_tiles)
+        blocks = front if first_tiles <= split else front + back
         joined = pl.pallas_call(
-            join_kernel,
-            out_shape=jax.ShapeDtypeStruct(
-                (first_tiles, chan_rows - block_rows, LANES), jnp.bfloat16
-            ),
-            in_specs=[in_vmem] * (group_count - 1),
+            functools.partial(join_kernel, group_count),
+            out_shape=jax.ShapeDtypeStruct((first_tiles, chan_rows, LANES), jnp.bfloat16),
+            in_specs=[in_vmem] * len(blocks),
             out_specs=in_vmem,
-            scratch_shapes=[pltpu.VMEM((first_tiles, chan_rows - block_rows, LANES), jnp.float32)],
+            scratch_shapes=[pltpu.VMEM((first_tiles, chan_rows, LANES), jnp.float32)],
             compiler_params=params,
-        )(*main[:-1])
+        )(*blocks)
         for hop in range(1, lax.axis_size("tm")):
             if rest > 0:
                 takes.append(min(time_tiles, rest))
                 halos.append(from_ahead(joined[: takes[-1]], hop, 0))
-                halos.append(from_ahead(main[-1][: takes[-1]], hop, 0))
                 rest -= takes[-1]
     lost = -(-sum(2**level for level in far_levels) // LANES) + tap_tiles
     early_tiles = time_tiles - lost
     if early_tiles <= 0:
-        plan = Plan(time_tiles, takes, rest, 0, time_tiles, False, False, far_levels, tap_tiles)
-        return between_chips(plan, main, halos)[0]
-    plan = Plan(time_tiles, [], 0, 0, early_tiles, False, True, far_levels, tap_tiles)
-    out, *carried = between_chips(plan, main, [])
+        plan = Plan([0, split], time_tiles, takes, rest, 0, time_tiles, False, False, far_levels, tap_tiles)
+        return between_chips(plan, front + back, halos)[0]
+    plan = Plan([0, split], time_tiles, [], 0, 0, early_tiles, False, True, far_levels, tap_tiles)
+    out, *carried = between_chips(plan, front + back, [])
     late_tiles = time_tiles - early_tiles
-    plan = Plan(time_tiles, takes, rest, early_tiles, late_tiles, True, False, far_levels, tap_tiles)
-    return between_chips(plan, main, halos, [*carried, out])[0]
+    parts, blocks = ([split], back) if early_tiles + tap_tiles >= split else ([0, split], front + back)
+    plan = Plan(parts, time_tiles, takes, rest, early_tiles, late_tiles, True, False, far_levels, tap_tiles)
+    return between_chips(plan, blocks, halos, [*carried, out])[0]
 
 
 def solution(mesh):

time: 25.8 us -> 30.2 us (1.17)
  starting transfers between devices: 9.68 us -> 12.2 us
  waiting for transfers between devices: 7.98 us -> 8.72 us
  Pallas kernels: 6.99 us -> 7.62 us
  local copies, waits for them, and re-layouts: 0.96 us -> 1.29 us
    ppermute x3 -> x6, starting transfers between devices: 4.45 us -> 9.66 us  [exchanged(): received.append(lax.ppermute(block, ('freq', 'sub'), route))]
    ppermute x4 -> x3, starting transfers between devices: 4.77 us -> 2.14 us  [from_ahead(): return lax.ppermute(value, ('tm', 'sub'), route)]
    ppermute x4 -> x3, waiting for transfers between devices: 2.45 us -> 3.21 us  [from_ahead(): return lax.ppermute(value, ('tm', 'sub'), route)]
    pallas_call x2, Pallas kernels: 3.69 us -> 4.33 us  [within_chip(): pl.pallas_call(functools.partial(chip_kernel, spans, out_tiles, group_cou...]
    ppermute x3 -> x6, waiting for transfers between devices: 5.53 us -> 5.12 us  [exchanged(): received.append(lax.ppermute(block, ('freq', 'sub'), route))]
    ppermute x1, waiting for transfers between devices: 0.01 us -> 0.4 us  [from_partner(): lax.ppermute(value, axis, [(source, source ^ mask) for source in range(co...]
    unnamed x6, local copies, waits for them, and re-layouts: 0.96 us -> 1.29 us
  transfers between devices with their start and end apart: 8 -> 10, of which waited for: 4 -> 6; matrix products, arithmetic and copies ran while one was open for 0% -> 0% of each run, Pallas kernels for 19% -> 13%
where the time goes in v6:
time: 30.2 us; the launch traced here: 30 us
  starting transfers between devices  12.2 us (40%)
  waiting for transfers between devices  8.72 us (29%)
  Pallas kernels  7.62 us (25%)
  local copies, waits for them, and re-layouts  1.29 us (4%)
    ppermute x6, starting transfers between devices, exchanged(): received.append(lax.ppermute(block, ('freq', 'sub'), route))  9.66 us
    ppermute x6, waiting for transfers between devices, exchanged(): received.append(lax.ppermute(block, ('freq', 'sub'), route))  5.12 us
    pallas_call x2, Pallas kernels, within_chip(): pl.pallas_call(functools.partial(chip_kernel, spans, out_tiles, group_cou...  4.33 us
    ppermute x3, waiting for transfers between devices, from_ahead(): return lax.ppermute(value, ('tm', 'sub'), route)  3.21 us
    pallas_call x2, Pallas kernels, between_chips(): pl.pallas_call(functools.partial(trial_kernel, plan, group_count, level_c...  3.04 us
    ppermute x3, starting transfers between devices, from_ahead(): return lax.ppermute(value, ('tm', 'sub'), route)  2.14 us
    unnamed x6, local copies, waits for them, and re-layouts  1.29 us
  transfers between devices with their start and end apart: 10, of which 6 were waited for; matrix products, arithmetic and copies ran while one was open for 0% of the time, Pallas kernels for 13%

profile of v6, /device:TPU:0, one launch (start us, length us, event | category | flops | bytes accessed | tf_op | source)
XLA Modules:
  0.0 30.0 jit_solution(5406272656108683972)
XLA Ops:
  0.0 0.5 %collective-permute-start.1 = (bf16[64,2048]{1,0:T(8,128)(2,1)}, bf16[64,2048]{1,0:T(8,128)(2,1)S(1)}, u32[]{:S(2)}, u32[]{:S(2)}) collective-permute-start(bf16[64,2048]{1,0:T(8,128)(2,1)} %whole.1), channel_id=1, source_target_pairs={{0,1},{1,0},{2,3},{3,2},{4,5},{5,4},{6,7},{7,6},{8,9},{9,8},{10,11... | collective-permute-start | bytes 786440 | tf_op jit(solution)/shard_map/ppermute | solution.py:45
  0.5 0.9 %copy-done = bf16[64,2048]{1,0:T(8,128)(2,1)S(1)} copy-done((bf16[64,2048]{1,0:T(8,128)(2,1)S(1)}, bf16[64,2048]{1,0:T(8,128)(2,1)}, u32[]{:S(2)}) %copy-start) | copy-done | bytes 262168
  1.4 0.4 %collective-permute-done.1.refs_1_.refs_2_ = bf16[64,2048]{1,0:T(8,128)(2,1)S(1)} collective-permute-done((bf16[64,2048]{1,0:T(8,128)(2,1)}, bf16[64,2048]{1,0:T(8,128)(2,1)S(1)}, u32[]{:S(2)}, u32[]{:S(2)}) %collective-permute-start.1) | collective-permute-done | bytes 262176 | tf_op jit(solution)/shard_map/ppermute | solution.py:45
  1.8 0.3 %copy-done.1 = s32[9,512]{1,0:T(8,128)S(1)} copy-done((s32[9,512]{1,0:T(8,128)S(1)}, s32[9,512]{1,0:T(8,128)}, u32[]{:S(2)}) %copy-start.1) | copy-done | bytes 18456
  2.2 2.2 %shard_map.38 = (bf16[10,16,128]{2,1,0:T(8,128)(2,1)S(1)}, bf16[10,16,128]{2,1,0:T(8,128)(2,1)S(1)}, bf16[10,16,128]{2,1,0:T(8,128)(2,1)S(1)}, bf16[10,16,128]{2,1,0:T(8,128)(2,1)S(1)}, f32[128,128]{1,0:T(8,128)S(1)}) custom-call(bf16[64,2048]{1,0:T(8,128)(2,1)S(1)} %get-tuple-element.31.refs_0_, ...), custom_call_target="tpu_custom_call" | custom-call | tf_op jit(solution)/shard_map/pallas_call | solution.py:410
  4.4 2.7 %collective-permute-start.4 = (bf16[10,16,128]{2,1,0:T(8,128)(2,1)S(1)}, bf16[10,16,128]{2,1,0:T(8,128)(2,1)S(1)}, u32[]{:S(2)}, u32[]{:S(2)}) collective-permute-start(bf16[10,16,128]{2,1,0:T(8,128)(2,1)S(1)} %get-tuple-element.43), channel_id=1, source_target_pairs={{0,4},{1,9},{4,0},{5,13},{8,12},{9,1},{12,8},{13,5},{2,6},{3,11},{... | collective-permute-start | bytes 122888 | tf_op jit(solution)/shard_map/ppermute | solution.py:65
  7.1 2.5 %collective-permute-start.5 = (bf16[10,16,128]{2,1,0:T(8,128)(2,1)S(1)}, bf16[10,16,128]{2,1,0:T(8,128)(2,1)S(1)}, u32[]{:S(2)}, u32[]{:S(2)}) collective-permute-start(bf16[10,16,128]{2,1,0:T(8,128)(2,1)S(1)} %get-tuple-element.44), channel_id=1, source_target_pairs={{0,12},{1,5},{4,8},{5,1},{8,4},{9,13},{12,0},{13,9},{2,14},{3,7},{... | collective-permute-start | bytes 122888 | tf_op jit(solution)/shard_map/ppermute | solution.py:65
  9.6 0.1 collective-permute-start.6
  9.7 1.0 %collective-permute-start.2 = (bf16[64,128]{1,0:T(8,128)(2,1)S(1)}, bf16[64,128]{1,0:T(8,128)(2,1)S(1)}, u32[]{:S(2)}, u32[]{:S(2)}) collective-permute-start(bf16[64,128]{1,0:T(8,128)(2,1)S(1)} %get-tuple-element.32), channel_id=1, source_target_pairs={{2,1},{3,0},{0,3},{1,2},{6,5},{7,4},{4,7},{5,6},{10,9},{11,8},{8,1... | collective-permute-start | bytes 49160 | tf_op jit(solution)/shard_map/ppermute | solution.py:40
  10.7 0.5 %collective-permute-start = (bf16[64,128]{1,0:T(8,128)(2,1)S(1)}, bf16[64,128]{1,0:T(8,128)(2,1)S(1)}, u32[]{:S(2)}, u32[]{:S(2)}) collective-permute-start(bf16[64,128]{1,0:T(8,128)(2,1)S(1)} %get-tuple-element.32), channel_id=1, source_target_pairs={{2,0},{3,1},{0,2},{1,3},{6,4},{7,5},{4,6},{5,7},{10,8},{11,9},{8,1... | collective-permute-start | bytes 49160 | tf_op jit(solution)/shard_map/ppermute | solution.py:40
  11.2 1.7 %collective-permute-done.2.refs_3_ = bf16[64,128]{1,0:T(8,128)(2,1)S(1)} collective-permute-done((bf16[64,128]{1,0:T(8,128)(2,1)S(1)}, bf16[64,128]{1,0:T(8,128)(2,1)S(1)}, u32[]{:S(2)}, u32[]{:S(2)}) %collective-permute-start.2) | collective-permute-done | bytes 16416 | tf_op jit(solution)/shard_map/ppermute | solution.py:40
  12.9 1.5 %collective-permute-done.refs_1_ = bf16[64,128]{1,0:T(8,128)(2,1)S(1)} collective-permute-done((bf16[64,128]{1,0:T(8,128)(2,1)S(1)}, bf16[64,128]{1,0:T(8,128)(2,1)S(1)}, u32[]{:S(2)}, u32[]{:S(2)}) %collective-permute-start) | collective-permute-done | bytes 16416 | tf_op jit(solution)/shard_map/ppermute | solution.py:40
  14.4 2.1 %shard_map.39 = (bf16[6,16,128]{2,1,0:T(8,128)(2,1)S(1)}, bf16[6,16,128]{2,1,0:T(8,128)(2,1)S(1)}, bf16[6,16,128]{2,1,0:T(8,128)(2,1)S(1)}, bf16[6,16,128]{2,1,0:T(8,128)(2,1)S(1)}) custom-call(bf16[64,2048]{1,0:T(8,128)(2,1)S(1)} %get-tuple-element.31.refs_0_, bf16[64,128]{1,0:T(8,128)(2,1)S(1)} %collective-permute-done.refs_1_, ...), custom_call_target="tpu_custom_call" | custom-call | tf_op jit(solution)/shard_map/pallas_call | solution.py:410
  16.6 0.0 copy-start.2
  16.6 0.6 %collective-permute-start.9 = (bf16[5,64,128]{2,1,0:T(8,128)(2,1)S(1)}, bf16[5,64,128]{2,1,0:T(8,128)(2,1)S(1)}, u32[]{:S(2)}, u32[]{:S(2)}) collective-permute-start(bf16[5,64,128]{2,1,0:T(8,128)(2,1)S(1)} %shard_map.41), channel_id=1, source_target_pairs={{2,0},{3,1},{0,2},{1,3},{6,4},{7,5},{4,6},{5,7},{10,8},{11,9},{8,1... | collective-permute-start | bytes 245768 | tf_op jit(solution)/shard_map/ppermute | solution.py:40
  17.2 2.8 %collective-permute-start.3 = (bf16[6,16,128]{2,1,0:T(8,128)(2,1)S(1)}, bf16[6,16,128]{2,1,0:T(8,128)(2,1)S(1)}, u32[]{:S(2)}, u32[]{:S(2)}) collective-permute-start(bf16[6,16,128]{2,1,0:T(8,128)(2,1)S(1)} %get-tuple-element.39), channel_id=1, source_target_pairs={{0,8},{1,13},{4,12},{5,9},{8,0},{9,5},{12,4},{13,1},{2,10},{3,15},... | collective-permute-start | bytes 73736 | tf_op jit(solution)/shard_map/ppermute | solution.py:65
  20.0 1.3 %collective-permute-start.7 = (bf16[6,16,128]{2,1,0:T(8,128)(2,1)S(1)}, bf16[6,16,128]{2,1,0:T(8,128)(2,1)S(1)}, u32[]{:S(2)}, u32[]{:S(2)}) collective-permute-start(bf16[6,16,128]{2,1,0:T(8,128)(2,1)S(1)} %get-tuple-element.48), channel_id=1, source_target_pairs={{0,4},{1,9},{4,0},{5,13},{8,12},{9,1},{12,8},{13,5},{2,6},{3,11},{... | collective-permute-start | bytes 73736 | tf_op jit(solution)/shard_map/ppermute | solution.py:65
  21.3 0.3 collective-permute-start.8
  21.6 0.2 shard_map.40
  21.8 0.1 collective-permute-done.3.refs_7_.refs_3_
  21.9 1.9 %collective-permute-done.7.refs_5_.refs_1_ = bf16[6,16,128]{2,1,0:T(8,128)(2,1)S(1)} collective-permute-done((bf16[6,16,128]{2,1,0:T(8,128)(2,1)S(1)}, bf16[6,16,128]{2,1,0:T(8,128)(2,1)S(1)}, u32[]{:S(2)}, u32[]{:S(2)}) %collective-permute-start.7) | collective-permute-done | bytes 24608 | tf_op jit(solution)/shard_map/ppermute | solution.py:65
  23.8 3.1 %collective-permute-done.8.refs_6_.refs_2_ = bf16[6,16,128]{2,1,0:T(8,128)(2,1)S(1)} collective-permute-done((bf16[6,16,128]{2,1,0:T(8,128)(2,1)S(1)}, bf16[6,16,128]{2,1,0:T(8,128)(2,1)S(1)}, u32[]{:S(2)}, u32[]{:S(2)}) %collective-permute-start.8) | collective-permute-done | bytes 24608 | tf_op jit(solution)/shard_map/ppermute | solution.py:65
  26.9 1.5 %shard_map.42 = (f32[64,1408]{1,0:T(8,128)S(1)}, bf16[2,64,128]{2,1,0:T(8,128)(2,1)S(1)}) custom-call(f32[128,128]{1,0:T(8,128)S(1)} %get-tuple-element.40.columns, bf16[768,384]{1,0:T(8,128)(2,1)S(1)} %get-tuple-element.41.taps, bf16[10,16,128]{2,1,0:T(8,128)(2,1)S(1)} %get-tuple-element.51.refs_0_, ...), custom_call_target="tpu_custom_call" | custom-call | tf_op jit(solution)/shard_map/pallas_call | solution.py:435
  28.4 1.6 %shard_map.43 = f32[64,2048]{1,0:T(8,128)} custom-call(f32[128,128]{1,0:T(8,128)S(1)} %get-tuple-element.40.columns, bf16[768,384]{1,0:T(8,128)(2,1)S(1)} %get-tuple-element.41.taps, bf16[6,16,128]{2,1,0:T(8,128)(2,1)S(1)} %get-tuple-element.47.refs_4_.refs_0_, bf16[6,16,128]{2,1,0:T(8,128)(2,1)S(1)} %collective-permute-done.7.refs_5_.refs_1_, ...), custom_call_target="tpu_custom_call" | custom-call | tf_op jit(solution)/shard_map/pallas_call | solution.py:435
  (9 shorter events, 0.0 us)
Async XLA Ops:
  0.0 1.8 %collective-permute-start.1 = (bf16[64,2048]{1,0:T(8,128)(2,1)}, bf16[64,2048]{1,0:T(8,128)(2,1)S(1)}, u32[]{:S(2)}, u32[]{:S(2)}) collective-permute-start(bf16[64,2048]{1,0:T(8,128)(2,1)} %whole.1), channel_id=1, source_target_pairs={{0,1},{1,0},{2,3},{3,2},{4,5},{5,4},{6,7},{7,6},{8,9},{9,8},{10,11... | collective-permute-start | bytes 786440 | tf_op jit(solution)/shard_map/ppermute | solution.py:45
  0.5 0.9 %copy-start = (bf16[64,2048]{1,0:T(8,128)(2,1)S(1)}, bf16[64,2048]{1,0:T(8,128)(2,1)}, u32[]{:S(2)}) copy-start(bf16[64,2048]{1,0:T(8,128)(2,1)} %whole.1) | copy-start | bytes 786436
  1.4 0.8 %copy-start.1 = (s32[9,512]{1,0:T(8,128)S(1)}, s32[9,512]{1,0:T(8,128)}, u32[]{:S(2)}) copy-start(s32[9,512]{1,0:T(8,128)} %shifts) | copy-start | bytes 55300
  4.4 12.1 %collective-permute-start.4 = (bf16[10,16,128]{2,1,0:T(8,128)(2,1)S(1)}, bf16[10,16,128]{2,1,0:T(8,128)(2,1)S(1)}, u32[]{:S(2)}, u32[]{:S(2)}) collective-permute-start(bf16[10,16,128]{2,1,0:T(8,128)(2,1)S(1)} %get-tuple-element.43), channel_id=1, source_target_pairs={{0,4},{1,9},{4,0},{5,13},{8,12},{9,1},{12,8},{13,5},{2,6},{3,11},{... | collective-permute-start | bytes 122888 | tf_op jit(solution)/shard_map/ppermute | solution.py:65
  7.1 9.4 %collective-permute-start.5 = (bf16[10,16,128]{2,1,0:T(8,128)(2,1)S(1)}, bf16[10,16,128]{2,1,0:T(8,128)(2,1)S(1)}, u32[]{:S(2)}, u32[]{:S(2)}) collective-permute-start(bf16[10,16,128]{2,1,0:T(8,128)(2,1)S(1)} %get-tuple-element.44), channel_id=1, source_target_pairs={{0,12},{1,5},{4,8},{5,1},{8,4},{9,13},{12,0},{13,9},{2,14},{3,7},{... | collective-permute-start | bytes 122888 | tf_op jit(solution)/shard_map/ppermute | solution.py:65
  9.6 7.0 %collective-permute-start.6 = (bf16[10,16,128]{2,1,0:T(8,128)(2,1)S(1)}, bf16[10,16,128]{2,1,0:T(8,128)(2,1)S(1)}, u32[]{:S(2)}, u32[]{:S(2)}) collective-permute-start(bf16[10,16,128]{2,1,0:T(8,128)(2,1)S(1)} %get-tuple-element.45), channel_id=1, source_target_pairs={{0,8},{1,13},{4,12},{5,9},{8,0},{9,5},{12,4},{13,1},{2,10},{3,15},... | collective-permute-start | bytes 122888 | tf_op jit(solution)/shard_map/ppermute | solution.py:65
  9.7 3.2 %collective-permute-start.2 = (bf16[64,128]{1,0:T(8,128)(2,1)S(1)}, bf16[64,128]{1,0:T(8,128)(2,1)S(1)}, u32[]{:S(2)}, u32[]{:S(2)}) collective-permute-start(bf16[64,128]{1,0:T(8,128)(2,1)S(1)} %get-tuple-element.32), channel_id=1, source_target_pairs={{2,1},{3,0},{0,3},{1,2},{6,5},{7,4},{4,7},{5,6},{10,9},{11,8},{8,1... | collective-permute-start | bytes 49160 | tf_op jit(solution)/shard_map/ppermute | solution.py:40
  10.7 3.7 %collective-permute-start = (bf16[64,128]{1,0:T(8,128)(2,1)S(1)}, bf16[64,128]{1,0:T(8,128)(2,1)S(1)}, u32[]{:S(2)}, u32[]{:S(2)}) collective-permute-start(bf16[64,128]{1,0:T(8,128)(2,1)S(1)} %get-tuple-element.32), channel_id=1, source_target_pairs={{2,0},{3,1},{0,2},{1,3},{6,4},{7,5},{4,6},{5,7},{10,8},{11,9},{8,1... | collective-permute-start | bytes 49160 | tf_op jit(solution)/shard_map/ppermute | solution.py:40
  16.6 5.0 %copy-start.2 = (bf16[6,256]{1,0:T(8,128)(2,1)S(1)}, bf16[6,256]{1,0:T(8,128)(2,1)}, u32[]{:S(2)}) copy-start(bf16[6,256]{1,0:T(8,128)(2,1)} %filters) | copy-start | bytes 9220
  16.6 11.8 %collective-permute-start.9 = (bf16[5,64,128]{2,1,0:T(8,128)(2,1)S(1)}, bf16[5,64,128]{2,1,0:T(8,128)(2,1)S(1)}, u32[]{:S(2)}, u32[]{:S(2)}) collective-permute-start(bf16[5,64,128]{2,1,0:T(8,128)(2,1)S(1)} %shard_map.41), channel_id=1, source_target_pairs={{2,0},{3,1},{0,2},{1,3},{6,4},{7,5},{4,6},{5,7},{10,8},{11,9},{8,1... | collective-permute-start | bytes 245768 | tf_op jit(solution)/shard_map/ppermute | solution.py:40
  17.2 4.7 %collective-permute-start.3 = (bf16[6,16,128]{2,1,0:T(8,128)(2,1)S(1)}, bf16[6,16,128]{2,1,0:T(8,128)(2,1)S(1)}, u32[]{:S(2)}, u32[]{:S(2)}) collective-permute-start(bf16[6,16,128]{2,1,0:T(8,128)(2,1)S(1)} %get-tuple-element.39), channel_id=1, source_target_pairs={{0,8},{1,13},{4,12},{5,9},{8,0},{9,5},{12,4},{13,1},{2,10},{3,15},... | collective-permute-start | bytes 73736 | tf_op jit(solution)/shard_map/ppermute | solution.py:65
  20.0 3.8 %collective-permute-start.7 = (bf16[6,16,128]{2,1,0:T(8,128)(2,1)S(1)}, bf16[6,16,128]{2,1,0:T(8,128)(2,1)S(1)}, u32[]{:S(2)}, u32[]{:S(2)}) collective-permute-start(bf16[6,16,128]{2,1,0:T(8,128)(2,1)S(1)} %get-tuple-element.48), channel_id=1, source_target_pairs={{0,4},{1,9},{4,0},{5,13},{8,12},{9,1},{12,8},{13,5},{2,6},{3,11},{... | collective-permute-start | bytes 73736 | tf_op jit(solution)/shard_map/ppermute | solution.py:65
  21.3 5.6 %collective-permute-start.8 = (bf16[6,16,128]{2,1,0:T(8,128)(2,1)S(1)}, bf16[6,16,128]{2,1,0:T(8,128)(2,1)S(1)}, u32[]{:S(2)}, u32[]{:S(2)}) collective-permute-start(bf16[6,16,128]{2,1,0:T(8,128)(2,1)S(1)} %get-tuple-element.49), channel_id=1, source_target_pairs={{0,12},{1,5},{4,8},{5,1},{8,4},{9,13},{12,0},{13,9},{2,14},{3,7},{... | collective-permute-start | bytes 73736 | tf_op jit(solution)/shard_map/ppermute | solution.py:65

commit v7 on v4

--- a/solution.py
+++ b/solution.py
@@ -11,6 +11,7 @@
 LANES = 128
 SUBLANES = 8
 PACKED = 16
+SHORT = 4
 LOG2_E = 1.4426950408889634
 VMEM_LIMIT = 48 * 2**20
 
@@ -46,7 +47,7 @@
 
 
 def mask_orders(group_count):
-    order = list(range(group_count - 1, 0, -1))
+    order = [1, *range(group_count - 1, 1, -1)]
     return order, order[-1:] + order[:-1]
 
 
@@ -80,7 +81,30 @@
     columns[...] = table[...].T
 
 
+def merge_short(source, target, low, high, outs, tiles, most):
+    inside = [lanes() < LANES - delay for delay in range(1, most + 1)]
+    chosen = [([amount == delay for delay in range(1, most + 1)], place) for amount, place in outs]
+
+    def rolled(tile):
+        value = source[tile, high, :]
+        return value, [pltpu.roll(value, LANES - delay, 1) for delay in range(1, most + 1)]
+
+    now = rolled(0)
+    for tile in range(tiles):
+        later = rolled(tile + 1)
+        copies = [jnp.where(*parts) for parts in zip(inside, now[1], later[1])]
+        lower = source[tile, low, :]
+        for masks, place in chosen:
+            moved = now[0]
+            for mask, copy in zip(masks, copies):
+                moved = jnp.where(mask, copy, moved)
+            target[tile, place, :] = lower + moved
+        now = later
+
+
 def merge(source, target, low, high, outs, tiles, most):
+    if most <= SHORT:
+        return merge_short(source, target, low, high, outs, tiles, most)
     lane = lanes()
     apart = max(most // LANES, 1)
     chosen = []

time: 25.8 us -> 23.9 us (0.926)
  waiting for transfers between devices: 7.98 us -> 6.9 us
  starting transfers between devices: 9.68 us -> 9.22 us
  Pallas kernels: 6.99 us -> 6.67 us
    ppermute x3, waiting for transfers between devices: 5.53 us -> 4.73 us  [exchanged(): received.append(lax.ppermute(block, ('freq', 'sub'), route))]
    pallas_call x2, Pallas kernels: 3.69 us -> 3.38 us  [within_chip(): pl.pallas_call(functools.partial(chip_kernel, spans, out_tiles, group_cou...]
    ppermute x4, waiting for transfers between devices: 2.45 us -> 2.17 us  [from_ahead(): return lax.ppermute(value, ('tm', 'sub'), route)]
  transfers between devices with their start and end apart: 8 -> 8, of which waited for: 4 -> 5; matrix products, arithmetic and copies ran while one was open for 0% -> 0% of each run, Pallas kernels for 19% -> 19%
where the time goes in v7:
time: 23.9 us; the launch traced here: 23.8 us
  starting transfers between devices  9.22 us (39%)
  waiting for transfers between devices  6.9 us (29%)
  Pallas kernels  6.67 us (28%)
  local copies, waits for them, and re-layouts  0.96 us (4%)
    ppermute x3, waiting for transfers between devices, exchanged(): received.append(lax.ppermute(block, ('freq', 'sub'), route))  4.73 us
    ppermute x4, starting transfers between devices, from_ahead(): return lax.ppermute(value, ('tm', 'sub'), route)  4.54 us
    ppermute x3, starting transfers between devices, exchanged(): received.append(lax.ppermute(block, ('freq', 'sub'), route))  4.22 us
    pallas_call x2, Pallas kernels, within_chip(): pl.pallas_call(functools.partial(chip_kernel, spans, out_tiles, group_cou...  3.38 us
    pallas_call x2, Pallas kernels, between_chips(): pl.pallas_call(functools.partial(trial_kernel, plan, group_count, level_c...  3.04 us
    ppermute x4, waiting for transfers between devices, from_ahead(): return lax.ppermute(value, ('tm', 'sub'), route)  2.17 us
    unnamed x6, local copies, waits for them, and re-layouts  0.96 us
  transfers between devices with their start and end apart: 8, of which 5 were waited for; matrix products, arithmetic and copies ran while one was open for 0% of the time, Pallas kernels for 19%

profile of v7, /device:TPU:0, one launch (start us, length us, event | category | flops | bytes accessed | tf_op | source)
XLA Modules:
  0.0 23.8 jit_solution(16868321617476622256)
XLA Ops:
  0.0 0.5 %collective-permute-start.1 = (bf16[64,2048]{1,0:T(8,128)(2,1)}, bf16[64,2048]{1,0:T(8,128)(2,1)S(1)}, u32[]{:S(2)}, u32[]{:S(2)}) collective-permute-start(bf16[64,2048]{1,0:T(8,128)(2,1)} %whole.1), channel_id=1, source_target_pairs={{0,1},{1,0},{2,3},{3,2},{4,5},{5,4},{6,7},{7,6},{8,9},{9,8},{10,11... | collective-permute-start | bytes 786440 | tf_op jit(solution)/shard_map/ppermute | solution.py:46
  0.5 0.9 %copy-done = bf16[64,2048]{1,0:T(8,128)(2,1)S(1)} copy-done((bf16[64,2048]{1,0:T(8,128)(2,1)S(1)}, bf16[64,2048]{1,0:T(8,128)(2,1)}, u32[]{:S(2)}) %copy-start) | copy-done | bytes 262168
  1.4 2.7 %collective-permute-start.2 = (bf16[64,128]{1,0:T(8,128)(2,1)S(1)}, bf16[64,128]{1,0:T(8,128)(2,1)S(1)}, u32[]{:S(2)}, u32[]{:S(2)}) collective-permute-start(bf16[64,128]{1,0:T(8,128)(2,1)S(1)} %get-tuple-element.24), channel_id=1, source_target_pairs={{2,1},{3,0},{0,3},{1,2},{6,5},{7,4},{4,7},{5,6},{10,9},{11,8},{8,1... | collective-permute-start | bytes 49160 | tf_op jit(solution)/shard_map/ppermute | solution.py:41
  4.1 0.0 collective-permute-start
  4.1 0.0 collective-permute-done.1.refs_1_.refs_2_
  4.1 0.0 copy-done.1
  4.1 2.8 %shard_map.38 = (f32[15,64,128]{2,1,0:T(8,128)S(1)}, f32[128,128]{1,0:T(8,128)S(1)}) custom-call(bf16[64,2048]{1,0:T(8,128)(2,1)S(1)} %get-tuple-element.23.refs_0_, bf16[64,2048]{1,0:T(8,128)(2,1)S(1)} %collective-permute-done.1.refs_1_.refs_2_, s32[9,512]{1,0:T(8,128)S(1)} %copy-done.1), custom_call_target="tpu_custom_call" | custom-call | tf_op jit(solution)/shard_map/pallas_call | solution.py:445
  6.9 0.0 collective-permute-done.2.refs_3_
  6.9 1.0 %collective-permute-done.refs_1_ = bf16[64,128]{1,0:T(8,128)(2,1)S(1)} collective-permute-done((bf16[64,128]{1,0:T(8,128)(2,1)S(1)}, bf16[64,128]{1,0:T(8,128)(2,1)S(1)}, u32[]{:S(2)}, u32[]{:S(2)}) %collective-permute-start) | collective-permute-done | bytes 16416 | tf_op jit(solution)/shard_map/ppermute | solution.py:41
  7.9 0.6 %shard_map.39 = (bf16[16,16,128]{2,1,0:T(8,128)(2,1)S(1)}, bf16[16,16,128]{2,1,0:T(8,128)(2,1)S(1)}, bf16[16,16,128]{2,1,0:T(8,128)(2,1)S(1)}, bf16[16,16,128]{2,1,0:T(8,128)(2,1)S(1)}) custom-call(bf16[64,2048]{1,0:T(8,128)(2,1)S(1)} %get-tuple-element.23.refs_0_, bf16[64,128]{1,0:T(8,128)(2,1)S(1)} %collective-permute-done.refs_1_, ...), custom_call_target="tpu_custom_call" | custom-call | tf_op jit(solution)/shard_map/pallas_call | solution.py:445
  8.5 1.6 %collective-permute-start.4 = (bf16[16,16,128]{2,1,0:T(8,128)(2,1)S(1)}, bf16[16,16,128]{2,1,0:T(8,128)(2,1)S(1)}, u32[]{:S(2)}, u32[]{:S(2)}) collective-permute-start(bf16[16,16,128]{2,1,0:T(8,128)(2,1)S(1)} %get-tuple-element.36), channel_id=1, source_target_pairs={{0,4},{1,9},{4,0},{5,13},{8,12},{9,1},{12,8},{13,5},{2,6},{3,11},{... | collective-permute-start | bytes 196616 | tf_op jit(solution)/shard_map/ppermute | solution.py:66
  10.1 2.5 %collective-permute-start.5 = (bf16[16,16,128]{2,1,0:T(8,128)(2,1)S(1)}, bf16[16,16,128]{2,1,0:T(8,128)(2,1)S(1)}, u32[]{:S(2)}, u32[]{:S(2)}) collective-permute-start(bf16[16,16,128]{2,1,0:T(8,128)(2,1)S(1)} %get-tuple-element.37), channel_id=1, source_target_pairs={{0,12},{1,5},{4,8},{5,1},{8,4},{9,13},{12,0},{13,9},{2,14},{3,7},{... | collective-permute-start | bytes 196616 | tf_op jit(solution)/shard_map/ppermute | solution.py:66
  12.6 0.1 collective-permute-start.3
  12.7 0.2 collective-permute-done.4.refs_1_
  12.9 3.7 %collective-permute-done.5.refs_2_ = bf16[16,16,128]{2,1,0:T(8,128)(2,1)S(1)} collective-permute-done((bf16[16,16,128]{2,1,0:T(8,128)(2,1)S(1)}, bf16[16,16,128]{2,1,0:T(8,128)(2,1)S(1)}, u32[]{:S(2)}, u32[]{:S(2)}) %collective-permute-start.5) | collective-permute-done | bytes 65568 | tf_op jit(solution)/shard_map/ppermute | solution.py:66
  16.6 0.8 %collective-permute-start.6 = (bf16[5,48,128]{2,1,0:T(8,128)(2,1)S(1)}, bf16[5,48,128]{2,1,0:T(8,128)(2,1)S(1)}, u32[]{:S(2)}, u32[]{:S(2)}) collective-permute-start(bf16[5,48,128]{2,1,0:T(8,128)(2,1)S(1)} %shard_map.41), channel_id=1, source_target_pairs={{2,0},{3,1},{0,2},{1,3},{6,4},{7,5},{4,6},{5,7},{10,8},{11,9},{8,1... | collective-permute-start | bytes 184328 | tf_op jit(solution)/shard_map/ppermute | solution.py:41
  17.4 0.0 copy-done.2
  17.4 0.2 shard_map.40
  17.6 0.8 %collective-permute-done.3.refs_3_ = bf16[16,16,128]{2,1,0:T(8,128)(2,1)S(1)} collective-permute-done((bf16[16,16,128]{2,1,0:T(8,128)(2,1)S(1)}, bf16[16,16,128]{2,1,0:T(8,128)(2,1)S(1)}, u32[]{:S(2)}, u32[]{:S(2)}) %collective-permute-start.3) | collective-permute-done | bytes 65568 | tf_op jit(solution)/shard_map/ppermute | solution.py:66
  18.4 1.1 %collective-permute-start.7 = (bf16[5,16,128]{2,1,0:T(8,128)(2,1)S(1)}, bf16[5,16,128]{2,1,0:T(8,128)(2,1)S(1)}, u32[]{:S(2)}, u32[]{:S(2)}) collective-permute-start(bf16[5,16,128]{2,1,0:T(8,128)(2,1)S(1)} %slice.3), channel_id=1, source_target_pairs={{2,0},{3,1},{0,2},{1,3},{6,4},{7,5},{4,6},{5,7},{10,8},{11,9},{8,1... | collective-permute-start | bytes 61448 | tf_op jit(solution)/shard_map/ppermute | solution.py:41
  19.5 1.5 %shard_map.42 = (f32[64,1408]{1,0:T(8,128)S(1)}, bf16[2,64,128]{2,1,0:T(8,128)(2,1)S(1)}) custom-call(f32[128,128]{1,0:T(8,128)S(1)} %get-tuple-element.33.columns, bf16[768,384]{1,0:T(8,128)(2,1)S(1)} %get-tuple-element.34.taps, bf16[16,16,128]{2,1,0:T(8,128)(2,1)S(1)} %get-tuple-element.35.refs_0_, ...), custom_call_target="tpu_custom_call" | custom-call | tf_op jit(solution)/shard_map/pallas_call | solution.py:470
  21.0 1.2 %collective-permute-done.7.refs_5_ = bf16[5,16,128]{2,1,0:T(8,128)(2,1)S(1)} collective-permute-done((bf16[5,16,128]{2,1,0:T(8,128)(2,1)S(1)}, bf16[5,16,128]{2,1,0:T(8,128)(2,1)S(1)}, u32[]{:S(2)}, u32[]{:S(2)}) %collective-permute-start.7) | collective-permute-done | bytes 20512 | tf_op jit(solution)/shard_map/ppermute | solution.py:41
  22.2 0.0 collective-permute-done.6.refs_4_
  22.2 1.6 %shard_map.43 = f32[64,2048]{1,0:T(8,128)} custom-call(f32[128,128]{1,0:T(8,128)S(1)} %get-tuple-element.33.columns, bf16[768,384]{1,0:T(8,128)(2,1)S(1)} %get-tuple-element.34.taps, bf16[16,16,128]{2,1,0:T(8,128)(2,1)S(1)} %get-tuple-element.35.refs_0_, bf16[16,16,128]{2,1,0:T(8,128)(2,1)S(1)} %collective-permute-done.4.refs_1_, ...), custom_call_target="tpu_custom_call" | custom-call | tf_op jit(solution)/shard_map/pallas_call | solution.py:470
  (6 shorter events, 0.0 us)
Async XLA Ops:
  0.0 4.1 %collective-permute-start.1 = (bf16[64,2048]{1,0:T(8,128)(2,1)}, bf16[64,2048]{1,0:T(8,128)(2,1)S(1)}, u32[]{:S(2)}, u32[]{:S(2)}) collective-permute-start(bf16[64,2048]{1,0:T(8,128)(2,1)} %whole.1), channel_id=1, source_target_pairs={{0,1},{1,0},{2,3},{3,2},{4,5},{5,4},{6,7},{7,6},{8,9},{9,8},{10,11... | collective-permute-start | bytes 786440 | tf_op jit(solution)/shard_map/ppermute | solution.py:46
  0.5 0.9 %copy-start = (bf16[64,2048]{1,0:T(8,128)(2,1)S(1)}, bf16[64,2048]{1,0:T(8,128)(2,1)}, u32[]{:S(2)}) copy-start(bf16[64,2048]{1,0:T(8,128)(2,1)} %whole.1) | copy-start | bytes 786436
  1.4 2.7 %copy-start.1 = (s32[9,512]{1,0:T(8,128)S(1)}, s32[9,512]{1,0:T(8,128)}, u32[]{:S(2)}) copy-start(s32[9,512]{1,0:T(8,128)} %shifts) | copy-start | bytes 55300
  1.4 5.5 %collective-permute-start.2 = (bf16[64,128]{1,0:T(8,128)(2,1)S(1)}, bf16[64,128]{1,0:T(8,128)(2,1)S(1)}, u32[]{:S(2)}, u32[]{:S(2)}) collective-permute-start(bf16[64,128]{1,0:T(8,128)(2,1)S(1)} %get-tuple-element.24), channel_id=1, source_target_pairs={{2,1},{3,0},{0,3},{1,2},{6,5},{7,4},{4,7},{5,6},{10,9},{11,8},{8,1... | collective-permute-start | bytes 49160 | tf_op jit(solution)/shard_map/ppermute | solution.py:41
  4.1 3.7 %collective-permute-start = (bf16[64,128]{1,0:T(8,128)(2,1)S(1)}, bf16[64,128]{1,0:T(8,128)(2,1)S(1)}, u32[]{:S(2)}, u32[]{:S(2)}) collective-permute-start(bf16[64,128]{1,0:T(8,128)(2,1)S(1)} %get-tuple-element.24), channel_id=1, source_target_pairs={{2,0},{3,1},{0,2},{1,3},{6,4},{7,5},{4,6},{5,7},{10,8},{11,9},{8,1... | collective-permute-start | bytes 49160 | tf_op jit(solution)/shard_map/ppermute | solution.py:41
  8.5 4.4 %collective-permute-start.4 = (bf16[16,16,128]{2,1,0:T(8,128)(2,1)S(1)}, bf16[16,16,128]{2,1,0:T(8,128)(2,1)S(1)}, u32[]{:S(2)}, u32[]{:S(2)}) collective-permute-start(bf16[16,16,128]{2,1,0:T(8,128)(2,1)S(1)} %get-tuple-element.36), channel_id=1, source_target_pairs={{0,4},{1,9},{4,0},{5,13},{8,12},{9,1},{12,8},{13,5},{2,6},{3,11},{... | collective-permute-start | bytes 196616 | tf_op jit(solution)/shard_map/ppermute | solution.py:66
  10.1 6.5 %collective-permute-start.5 = (bf16[16,16,128]{2,1,0:T(8,128)(2,1)S(1)}, bf16[16,16,128]{2,1,0:T(8,128)(2,1)S(1)}, u32[]{:S(2)}, u32[]{:S(2)}) collective-permute-start(bf16[16,16,128]{2,1,0:T(8,128)(2,1)S(1)} %get-tuple-element.37), channel_id=1, source_target_pairs={{0,12},{1,5},{4,8},{5,1},{8,4},{9,13},{12,0},{13,9},{2,14},{3,7},{... | collective-permute-start | bytes 196616 | tf_op jit(solution)/shard_map/ppermute | solution.py:66
  12.6 5.9 %collective-permute-start.3 = (bf16[16,16,128]{2,1,0:T(8,128)(2,1)S(1)}, bf16[16,16,128]{2,1,0:T(8,128)(2,1)S(1)}, u32[]{:S(2)}, u32[]{:S(2)}) collective-permute-start(bf16[16,16,128]{2,1,0:T(8,128)(2,1)S(1)} %get-tuple-element.32), channel_id=1, source_target_pairs={{0,8},{1,13},{4,12},{5,9},{8,0},{9,5},{12,4},{13,1},{2,10},{3,15},... | collective-permute-start | bytes 196616 | tf_op jit(solution)/shard_map/ppermute | solution.py:66
  12.7 4.7 %copy-start.2 = (bf16[6,256]{1,0:T(8,128)(2,1)S(1)}, bf16[6,256]{1,0:T(8,128)(2,1)}, u32[]{:S(2)}) copy-start(bf16[6,256]{1,0:T(8,128)(2,1)} %filters) | copy-start | bytes 9220
  16.6 5.7 %collective-permute-start.6 = (bf16[5,48,128]{2,1,0:T(8,128)(2,1)S(1)}, bf16[5,48,128]{2,1,0:T(8,128)(2,1)S(1)}, u32[]{:S(2)}, u32[]{:S(2)}) collective-permute-start(bf16[5,48,128]{2,1,0:T(8,128)(2,1)S(1)} %shard_map.41), channel_id=1, source_target_pairs={{2,0},{3,1},{0,2},{1,3},{6,4},{7,5},{4,6},{5,7},{10,8},{11,9},{8,1... | collective-permute-start | bytes 184328 | tf_op jit(solution)/shard_map/ppermute | solution.py:41
  18.4 3.8 %collective-permute-start.7 = (bf16[5,16,128]{2,1,0:T(8,128)(2,1)S(1)}, bf16[5,16,128]{2,1,0:T(8,128)(2,1)S(1)}, u32[]{:S(2)}, u32[]{:S(2)}) collective-permute-start(bf16[5,16,128]{2,1,0:T(8,128)(2,1)S(1)} %slice.3), channel_id=1, source_target_pairs={{2,0},{3,1},{0,2},{1,3},{6,4},{7,5},{4,6},{5,7},{10,8},{11,9},{8,1... | collective-permute-start | bytes 61448 | tf_op jit(solution)/shard_map/ppermute | solution.py:41

commit v8 on v7

--- a/solution.py
+++ b/solution.py
@@ -31,14 +31,9 @@
     return count.bit_length() - 1
 
 
-def from_ahead(value, steps, crossed):
-    count, cores = lax.axis_size("tm"), lax.axis_size("sub")
-    route = [
-        ((block + steps) % count * cores + core, block * cores + (core ^ crossed))
-        for block in range(count)
-        for core in range(cores)
-    ]
-    return lax.ppermute(value, ("tm", "sub"), route)
+def from_ahead(value, steps):
+    count = lax.axis_size("tm")
+    return lax.ppermute(value, "tm", [((block + steps) % count, block) for block in range(count)])
 
 
 def from_partner(value, axis, mask):
@@ -47,8 +42,8 @@
 
 
 def mask_orders(group_count):
-    order = [1, *range(group_count - 1, 1, -1)]
-    return order, order[-1:] + order[:-1]
+    far = list(range(group_count - 1, 1, -1))
+    return [1, *far], far[-1:] + far[:-1] + [1]
 
 
 def step_masks(group_count, core):
@@ -196,9 +191,14 @@
     return [made + -(-sum(2**later for later in levels if later > level) // LANES) for level in levels]
 
 
-def load_kernel(whole, copied, ahead):
+def load_kernel(whole, copied):
     copied[...] = whole[...]
-    ahead[...] = whole[:, : ahead.shape[1]]
+
+
+def start_kernel(whole, other, ahead):
+    rows, length = whole.shape[0], ahead.shape[1]
+    ahead[:rows, :] = whole[:, :length]
+    ahead[rows:, :] = other[:, :length]
 
 
 def placed(target, blocks, tiles, skip):
@@ -220,9 +220,9 @@
 
 
 def chip_kernel(spans, out_tiles, group_count, *refs):
-    pieces = (refs[: len(spans)], refs[len(spans) : 2 * len(spans)])
-    refs = refs[2 * len(spans) :]
-    chan_rows = pieces[0][0].shape[0]
+    chan_rows = refs[0].shape[0]
+    pieces = [[(refs[side], 0)] + [(ref, side * chan_rows) for ref in refs[2 : len(spans) + 1]] for side in range(2)]
+    refs = refs[len(spans) + 1 :]
     local_count = bits_of(chan_rows)
     chip, core = lax.axis_index("freq"), lax.axis_index("sub")
     if group_count:
@@ -237,10 +237,10 @@
     for side in range(2):
         place = pl.multiple_of((core ^ side) * chan_rows, chan_rows)
         tile = 0
-        for piece, (column, length, ahead) in zip(pieces[side], spans):
+        for (piece, row), (column, length, ahead) in zip(pieces[side], spans):
             there = lax.axis_index("tm") + ahead < lax.axis_size("tm")
             for start in range(column, column + length, LANES):
-                part = piece[:, start : start + LANES].astype(jnp.float32)
+                part = piece[row : row + chan_rows, start : start + LANES].astype(jnp.float32)
                 if ahead:
                     part = jnp.where(there, part, 0.0)
                 raw[tile, pl.ds(place, chan_rows), :] = part
@@ -483,27 +483,30 @@
         )(*operands)
 
     other_core = from_partner(filterbank, "sub", 1)
-    own, ahead = pl.pallas_call(
+    own = pl.pallas_call(
         load_kernel,
-        out_shape=[
-            jax.ShapeDtypeStruct(filterbank.shape, filterbank.dtype),
-            jax.ShapeDtypeStruct((chan_rows, near_len), filterbank.dtype),
-        ],
+        out_shape=jax.ShapeDtypeStruct(filterbank.shape, filterbank.dtype),
         in_specs=[in_vmem],
-        out_specs=[in_vmem] * 2,
+        out_specs=in_vmem,
         compiler_params=params,
     )(filterbank)
+    ahead = pl.pallas_call(
+        start_kernel,
+        out_shape=jax.ShapeDtypeStruct((2 * chan_rows, near_len), filterbank.dtype),
+        in_specs=[in_vmem] * 2,
+        out_specs=in_vmem,
+        compiler_params=params,
+    )(own, other_core)
     near_tiles = near_len // LANES
     early = time_tiles - near_tiles
     rows, delays = within_chip(
         [own, other_core, delay_shifts], [(0, time_len, 0)], time_tiles, early, False
     )
-    both, spans = ([own], [other_core]), [(early * LANES, near_len, 0)]
+    operands, spans = [own, other_core], [(early * LANES, near_len, 0)]
     if lax.axis_size("tm") > 1:
-        for crossed in range(2):
-            both[crossed].append(from_ahead(ahead, 1, crossed))
+        operands.append(from_ahead(ahead, 1))
         spans.append((0, near_len, 1))
-    main = list(within_chip([*both[0], *both[1], rows, delays], spans, 2 * near_tiles, near_tiles, True))
+    main = list(within_chip([*operands, rows, delays], spans, 2 * near_tiles, near_tiles, True))
     late_shifts, late_filters, main[0] = lax.optimization_barrier((delay_shifts, pulse_filters, main[0]))
     columns, taps = pl.pallas_call(
         functools.partial(table_kernel, group_count, block_rows),
@@ -537,8 +540,8 @@
         for hop in range(1, lax.axis_size("tm")):
             if rest > 0:
                 takes.append(min(time_tiles, rest))
-                halos.append(from_ahead(joined[: takes[-1]], hop, 0))
-                halos.append(from_ahead(main[-1][: takes[-1]], hop, 0))
+                halos.append(from_ahead(joined[: takes[-1]], hop))
+                halos.append(from_ahead(main[-1][: takes[-1]], hop))
                 rest -= takes[-1]
     lost = -(-sum(2**level for level in far_levels) // LANES) + tap_tiles
     early_tiles = time_tiles - lost

time: 23.9 us -> 23.7 us (level)
  waiting for transfers between devices: 6.9 us -> 5.9 us
  starting transfers between devices: 9.22 us -> 9.9 us
    ppermute x4 -> x3, waiting for transfers between devices: 2.17 us -> 1.16 us  [from_ahead(): lax.ppermute(value, 'tm', [((block + steps) % count, block) for block in...]
    ppermute x4 -> x3, starting transfers between devices: 4.54 us -> 5.22 us  [from_ahead(): lax.ppermute(value, 'tm', [((block + steps) % count, block) for block in...]
    ppermute x1, waiting for transfers between devices: 0.01 us -> 0.39 us  [from_partner(): lax.ppermute(value, axis, [(source, source ^ mask) for source in range(co...]
    ppermute x3, waiting for transfers between devices: 4.73 us -> 4.35 us  [exchanged(): received.append(lax.ppermute(block, ('freq', 'sub'), route))]
  transfers between devices with their start and end apart: 8 -> 7, of which waited for: 5 -> 5; matrix products, arithmetic and copies ran while one was open for 0% -> 0% of each run, Pallas kernels for 19% -> 19%
where the time goes in v8:
time: 23.7 us; the launch traced here: 23.5 us
  starting transfers between devices  9.9 us (42%)
  Pallas kernels  6.68 us (28%)
  waiting for transfers between devices  5.9 us (25%)
  local copies, waits for them, and re-layouts  0.96 us (4%)
    ppermute x3, starting transfers between devices, from_ahead(): lax.ppermute(value, 'tm', [((block + steps) % count, block) for block in...  5.22 us
    ppermute x3, waiting for transfers between devices, exchanged(): received.append(lax.ppermute(block, ('freq', 'sub'), route))  4.35 us
    ppermute x3, starting transfers between devices, exchanged(): received.append(lax.ppermute(block, ('freq', 'sub'), route))  4.23 us
    pallas_call x2, Pallas kernels, within_chip(): pl.pallas_call(functools.partial(chip_kernel, spans, out_tiles, group_cou...  3.38 us
    pallas_call x2, Pallas kernels, between_chips(): pl.pallas_call(functools.partial(trial_kernel, plan, group_count, level_c...  3.04 us
    ppermute x3, waiting for transfers between devices, from_ahead(): lax.ppermute(value, 'tm', [((block + steps) % count, block) for block in...  1.16 us
    unnamed x6, local copies, waits for them, and re-layouts  0.96 us
  transfers between devices with their start and end apart: 7, of which 5 were waited for; matrix products, arithmetic and copies ran while one was open for 0% of the time, Pallas kernels for 19%

profile of v8, /device:TPU:0, one launch (start us, length us, event | category | flops | bytes accessed | tf_op | source)
XLA Modules:
  0.0 23.5 jit_solution(8038168170902850004)
XLA Ops:
  0.0 0.5 %collective-permute-start = (bf16[64,2048]{1,0:T(8,128)(2,1)}, bf16[64,2048]{1,0:T(8,128)(2,1)S(1)}, u32[]{:S(2)}, u32[]{:S(2)}) collective-permute-start(bf16[64,2048]{1,0:T(8,128)(2,1)} %whole.1), channel_id=1, source_target_pairs={{0,1},{1,0},{2,3},{3,2},{4,5},{5,4},{6,7},{7,6},{8,9},{9,8},{10,11... | collective-permute-start | bytes 786440 | tf_op jit(solution)/shard_map/ppermute | solution.py:41
  0.5 0.9 %copy-done = bf16[64,2048]{1,0:T(8,128)(2,1)S(1)} copy-done((bf16[64,2048]{1,0:T(8,128)(2,1)S(1)}, bf16[64,2048]{1,0:T(8,128)(2,1)}, u32[]{:S(2)}) %copy-start) | copy-done | bytes 262168
  1.4 0.0 copy-start.1
  1.4 0.4 %collective-permute-done.other.refs_1_ = bf16[64,2048]{1,0:T(8,128)(2,1)S(1)} collective-permute-done((bf16[64,2048]{1,0:T(8,128)(2,1)}, bf16[64,2048]{1,0:T(8,128)(2,1)S(1)}, u32[]{:S(2)}, u32[]{:S(2)}) %collective-permute-start) | collective-permute-done | bytes 262176 | tf_op jit(solution)/shard_map/ppermute | solution.py:41
  1.8 2.9 %collective-permute-start.1 = (bf16[128,128]{1,0:T(8,128)(2,1)S(1)}, bf16[128,128]{1,0:T(8,128)(2,1)S(1)}, u32[]{:S(2)}, u32[]{:S(2)}) collective-permute-start(bf16[128,128]{1,0:T(8,128)(2,1)S(1)} %shard_map.38), channel_id=1, source_target_pairs={{2,0},{0,2},{3,1},{1,3},{6,4},{4,6},{7,5},{5,7},{10,8},{8,10},{11,... | collective-permute-start | bytes 98312 | tf_op jit(solution)/shard_map/ppermute | solution.py:36
  4.8 0.0 copy-done.1
  4.8 2.8 %shard_map.39 = (f32[15,64,128]{2,1,0:T(8,128)S(1)}, f32[128,128]{1,0:T(8,128)S(1)}) custom-call(bf16[64,2048]{1,0:T(8,128)(2,1)S(1)} %shard_map.37.whole.refs_0_, bf16[64,2048]{1,0:T(8,128)(2,1)S(1)} %collective-permute-done.other.refs_1_, s32[9,512]{1,0:T(8,128)S(1)} %copy-done.1), custom_call_target="tpu_custom_call" | custom-call | tf_op jit(solution)/shard_map/pallas_call | solution.py:445
  7.5 0.0 collective-permute-done.1.refs_2_
  7.5 0.6 %shard_map.40 = (bf16[16,16,128]{2,1,0:T(8,128)(2,1)S(1)}, bf16[16,16,128]{2,1,0:T(8,128)(2,1)S(1)}, bf16[16,16,128]{2,1,0:T(8,128)(2,1)S(1)}, bf16[16,16,128]{2,1,0:T(8,128)(2,1)S(1)}) custom-call(bf16[64,2048]{1,0:T(8,128)(2,1)S(1)} %shard_map.37.whole.refs_0_, bf16[64,2048]{1,0:T(8,128)(2,1)S(1)} %collective-permute-done.other.refs_1_, ...), custom_call_target="tpu_custom_call" | custom-call | tf_op jit(solution)/shard_map/pallas_call | solution.py:445
  8.2 1.6 %collective-permute-start.3 = (bf16[16,16,128]{2,1,0:T(8,128)(2,1)S(1)}, bf16[16,16,128]{2,1,0:T(8,128)(2,1)S(1)}, u32[]{:S(2)}, u32[]{:S(2)}) collective-permute-start(bf16[16,16,128]{2,1,0:T(8,128)(2,1)S(1)} %get-tuple-element.32), channel_id=1, source_target_pairs={{0,4},{1,9},{4,0},{5,13},{8,12},{9,1},{12,8},{13,5},{2,6},{3,11},{... | collective-permute-start | bytes 196616 | tf_op jit(solution)/shard_map/ppermute | solution.py:61
  9.8 2.5 %collective-permute-start.4 = (bf16[16,16,128]{2,1,0:T(8,128)(2,1)S(1)}, bf16[16,16,128]{2,1,0:T(8,128)(2,1)S(1)}, u32[]{:S(2)}, u32[]{:S(2)}) collective-permute-start(bf16[16,16,128]{2,1,0:T(8,128)(2,1)S(1)} %get-tuple-element.33), channel_id=1, source_target_pairs={{0,12},{1,13},{4,8},{5,9},{8,4},{9,5},{12,0},{13,1},{2,14},{3,15},... | collective-permute-start | bytes 196616 | tf_op jit(solution)/shard_map/ppermute | solution.py:61
  12.3 0.1 collective-permute-start.2
  12.4 0.0 copy-start.2
  12.4 0.6 %collective-permute-done.3.refs_1_ = bf16[16,16,128]{2,1,0:T(8,128)(2,1)S(1)} collective-permute-done((bf16[16,16,128]{2,1,0:T(8,128)(2,1)S(1)}, bf16[16,16,128]{2,1,0:T(8,128)(2,1)S(1)}, u32[]{:S(2)}, u32[]{:S(2)}) %collective-permute-start.3) | collective-permute-done | bytes 65568 | tf_op jit(solution)/shard_map/ppermute | solution.py:61
  13.0 3.5 %collective-permute-done.4.refs_2_ = bf16[16,16,128]{2,1,0:T(8,128)(2,1)S(1)} collective-permute-done((bf16[16,16,128]{2,1,0:T(8,128)(2,1)S(1)}, bf16[16,16,128]{2,1,0:T(8,128)(2,1)S(1)}, u32[]{:S(2)}, u32[]{:S(2)}) %collective-permute-start.4) | collective-permute-done | bytes 65568 | tf_op jit(solution)/shard_map/ppermute | solution.py:61
  16.5 1.2 %collective-permute-start.5 = (bf16[5,48,128]{2,1,0:T(8,128)(2,1)S(1)}, bf16[5,48,128]{2,1,0:T(8,128)(2,1)S(1)}, u32[]{:S(2)}, u32[]{:S(2)}) collective-permute-start(bf16[5,48,128]{2,1,0:T(8,128)(2,1)S(1)} %shard_map.42), channel_id=1, source_target_pairs={{2,0},{0,2},{3,1},{1,3},{6,4},{4,6},{7,5},{5,7},{10,8},{8,10},{11,... | collective-permute-start | bytes 184328 | tf_op jit(solution)/shard_map/ppermute | solution.py:36
  17.7 0.0 copy-done.2
  17.7 0.2 shard_map.41
  17.9 0.2 collective-permute-done.2.refs_3_
  18.2 1.1 %collective-permute-start.6 = (bf16[5,16,128]{2,1,0:T(8,128)(2,1)S(1)}, bf16[5,16,128]{2,1,0:T(8,128)(2,1)S(1)}, u32[]{:S(2)}, u32[]{:S(2)}) collective-permute-start(bf16[5,16,128]{2,1,0:T(8,128)(2,1)S(1)} %slice.3), channel_id=1, source_target_pairs={{2,0},{0,2},{3,1},{1,3},{6,4},{4,6},{7,5},{5,7},{10,8},{8,10},{11,... | collective-permute-start | bytes 61448 | tf_op jit(solution)/shard_map/ppermute | solution.py:36
  19.3 1.5 %shard_map.43 = (f32[64,1408]{1,0:T(8,128)S(1)}, bf16[2,64,128]{2,1,0:T(8,128)(2,1)S(1)}) custom-call(f32[128,128]{1,0:T(8,128)S(1)} %get-tuple-element.29.columns, bf16[768,384]{1,0:T(8,128)(2,1)S(1)} %get-tuple-element.30.taps, bf16[16,16,128]{2,1,0:T(8,128)(2,1)S(1)} %get-tuple-element.31.refs_0_, ...), custom_call_target="tpu_custom_call" | custom-call | tf_op jit(solution)/shard_map/pallas_call | solution.py:470
  20.8 1.2 %collective-permute-done.6.refs_5_ = bf16[5,16,128]{2,1,0:T(8,128)(2,1)S(1)} collective-permute-done((bf16[5,16,128]{2,1,0:T(8,128)(2,1)S(1)}, bf16[5,16,128]{2,1,0:T(8,128)(2,1)S(1)}, u32[]{:S(2)}, u32[]{:S(2)}) %collective-permute-start.6) | collective-permute-done | bytes 20512 | tf_op jit(solution)/shard_map/ppermute | solution.py:36
  21.9 0.0 collective-permute-done.5.refs_4_
  21.9 1.6 %shard_map.44 = f32[64,2048]{1,0:T(8,128)} custom-call(f32[128,128]{1,0:T(8,128)S(1)} %get-tuple-element.29.columns, bf16[768,384]{1,0:T(8,128)(2,1)S(1)} %get-tuple-element.30.taps, bf16[16,16,128]{2,1,0:T(8,128)(2,1)S(1)} %get-tuple-element.31.refs_0_, bf16[16,16,128]{2,1,0:T(8,128)(2,1)S(1)} %collective-permute-done.3.refs_1_, ...), custom_call_target="tpu_custom_call" | custom-call | tf_op jit(solution)/shard_map/pallas_call | solution.py:470
  (5 shorter events, 0.0 us)
Async XLA Ops:
  0.0 1.8 %collective-permute-start = (bf16[64,2048]{1,0:T(8,128)(2,1)}, bf16[64,2048]{1,0:T(8,128)(2,1)S(1)}, u32[]{:S(2)}, u32[]{:S(2)}) collective-permute-start(bf16[64,2048]{1,0:T(8,128)(2,1)} %whole.1), channel_id=1, source_target_pairs={{0,1},{1,0},{2,3},{3,2},{4,5},{5,4},{6,7},{7,6},{8,9},{9,8},{10,11... | collective-permute-start | bytes 786440 | tf_op jit(solution)/shard_map/ppermute | solution.py:41
  0.5 0.9 %copy-start = (bf16[64,2048]{1,0:T(8,128)(2,1)S(1)}, bf16[64,2048]{1,0:T(8,128)(2,1)}, u32[]{:S(2)}) copy-start(bf16[64,2048]{1,0:T(8,128)(2,1)} %whole.1) | copy-start | bytes 786436
  1.4 3.3 %copy-start.1 = (s32[9,512]{1,0:T(8,128)S(1)}, s32[9,512]{1,0:T(8,128)}, u32[]{:S(2)}) copy-start(s32[9,512]{1,0:T(8,128)} %shifts) | copy-start | bytes 55300
  1.8 5.7 %collective-permute-start.1 = (bf16[128,128]{1,0:T(8,128)(2,1)S(1)}, bf16[128,128]{1,0:T(8,128)(2,1)S(1)}, u32[]{:S(2)}, u32[]{:S(2)}) collective-permute-start(bf16[128,128]{1,0:T(8,128)(2,1)S(1)} %shard_map.38), channel_id=1, source_target_pairs={{2,0},{0,2},{3,1},{1,3},{6,4},{4,6},{7,5},{5,7},{10,8},{8,10},{11,... | collective-permute-start | bytes 98312 | tf_op jit(solution)/shard_map/ppermute | solution.py:36
  8.2 4.8 %collective-permute-start.3 = (bf16[16,16,128]{2,1,0:T(8,128)(2,1)S(1)}, bf16[16,16,128]{2,1,0:T(8,128)(2,1)S(1)}, u32[]{:S(2)}, u32[]{:S(2)}) collective-permute-start(bf16[16,16,128]{2,1,0:T(8,128)(2,1)S(1)} %get-tuple-element.32), channel_id=1, source_target_pairs={{0,4},{1,9},{4,0},{5,13},{8,12},{9,1},{12,8},{13,5},{2,6},{3,11},{... | collective-permute-start | bytes 196616 | tf_op jit(solution)/shard_map/ppermute | solution.py:61
  9.8 6.7 %collective-permute-start.4 = (bf16[16,16,128]{2,1,0:T(8,128)(2,1)S(1)}, bf16[16,16,128]{2,1,0:T(8,128)(2,1)S(1)}, u32[]{:S(2)}, u32[]{:S(2)}) collective-permute-start(bf16[16,16,128]{2,1,0:T(8,128)(2,1)S(1)} %get-tuple-element.33), channel_id=1, source_target_pairs={{0,12},{1,13},{4,8},{5,9},{8,4},{9,5},{12,0},{13,1},{2,14},{3,15},... | collective-permute-start | bytes 196616 | tf_op jit(solution)/shard_map/ppermute | solution.py:61
  12.3 5.9 %collective-permute-start.2 = (bf16[16,16,128]{2,1,0:T(8,128)(2,1)S(1)}, bf16[16,16,128]{2,1,0:T(8,128)(2,1)S(1)}, u32[]{:S(2)}, u32[]{:S(2)}) collective-permute-start(bf16[16,16,128]{2,1,0:T(8,128)(2,1)S(1)} %get-tuple-element.28), channel_id=1, source_target_pairs={{0,8},{1,5},{4,12},{5,1},{8,0},{9,13},{12,4},{13,9},{2,10},{3,7},{... | collective-permute-start | bytes 196616 | tf_op jit(solution)/shard_map/ppermute | solution.py:61
  12.4 5.3 %copy-start.2 = (bf16[6,256]{1,0:T(8,128)(2,1)S(1)}, bf16[6,256]{1,0:T(8,128)(2,1)}, u32[]{:S(2)}) copy-start(bf16[6,256]{1,0:T(8,128)(2,1)} %filters) | copy-start | bytes 9220
  16.5 5.4 %collective-permute-start.5 = (bf16[5,48,128]{2,1,0:T(8,128)(2,1)S(1)}, bf16[5,48,128]{2,1,0:T(8,128)(2,1)S(1)}, u32[]{:S(2)}, u32[]{:S(2)}) collective-permute-start(bf16[5,48,128]{2,1,0:T(8,128)(2,1)S(1)} %shard_map.42), channel_id=1, source_target_pairs={{2,0},{0,2},{3,1},{1,3},{6,4},{4,6},{7,5},{5,7},{10,8},{8,10},{11,... | collective-permute-start | bytes 184328 | tf_op jit(solution)/shard_map/ppermute | solution.py:36
  18.2 3.8 %collective-permute-start.6 = (bf16[5,16,128]{2,1,0:T(8,128)(2,1)S(1)}, bf16[5,16,128]{2,1,0:T(8,128)(2,1)S(1)}, u32[]{:S(2)}, u32[]{:S(2)}) collective-permute-start(bf16[5,16,128]{2,1,0:T(8,128)(2,1)S(1)} %slice.3), channel_id=1, source_target_pairs={{2,0},{0,2},{3,1},{1,3},{6,4},{4,6},{7,5},{5,7},{10,8},{8,10},{11,... | collective-permute-start | bytes 61448 | tf_op jit(solution)/shard_map/ppermute | solution.py:36

commit v9 on v8

--- a/solution.py
+++ b/solution.py
@@ -51,14 +51,17 @@
     return [0] + [jnp.where(core == 0, first, second) for first, second in zip(*orders)]
 
 
-def exchanged(blocks):
+def exchanged(blocks, cut):
     count = lax.axis_size("freq")
-    received = [blocks[0]]
-    for block, masks in zip(blocks[1:], zip(*mask_orders(count))):
+    received = [(0, 0, blocks[0])]
+    for step, masks in enumerate(zip(*mask_orders(count)), 1):
         route = [
             (chip * 2 + core, (chip ^ masks[core]) * 2 + core) for chip in range(count) for core in range(2)
         ]
-        received.append(lax.ppermute(block, ("freq", "sub"), route))
+        tiles = blocks[step].shape[0]
+        ends = [0, cut, tiles] if step + 1 == count and 0 < cut < tiles else [0, tiles]
+        for first, end in zip(ends, ends[1:]):
+            received.append((step, first, lax.ppermute(blocks[step][first:end], ("freq", "sub"), route)))
     return received
 
 
@@ -201,13 +204,14 @@
     ahead[rows:, :] = other[:, :length]
 
 
-def placed(target, blocks, tiles, skip):
+def placed(target, blocks, group_count, skip):
     chip, core = lax.axis_index("freq"), lax.axis_index("sub")
-    rows = blocks[0].shape[1]
-    for mask, block in zip(step_masks(len(blocks), core), blocks):
-        start = pl.multiple_of((chip ^ mask) * rows, rows)
-        for tile in range(skip, tiles):
-            target[tile - skip, pl.ds(start, rows), :] = block[tile, :, :].astype(jnp.float32)
+    masks = step_masks(group_count, core)
+    for step, first, block in blocks:
+        tiles, rows = block.shape[:2]
+        start = pl.multiple_of((chip ^ masks[step]) * rows, rows)
+        for tile in range(max(skip - first, 0), tiles):
+            target[first + tile - skip, pl.ds(start, rows), :] = block[tile, :, :].astype(jnp.float32)
 
 
 def join_kernel(*refs):
@@ -315,8 +319,8 @@
 
 
 def trial_kernel(plan, group_count, level_count, scale, columns, taps, *refs):
-    blocks, refs = refs[:group_count], refs[group_count:]
-    halos, refs = refs[: 2 * len(plan.halos)], refs[2 * len(plan.halos) :]
+    blocks, refs = refs[: len(plan.pieces)], refs[len(plan.pieces) :]
+    halos, refs = refs[: len(plan.halos)], refs[len(plan.halos) :]
     if plan.taken:
         carried, so_far, refs = refs[0], refs[1], refs[2:]
     out, refs = refs[0], refs[1:]
@@ -336,22 +340,17 @@
         place = out.at[:, pl.ds(0, plan.out_first * LANES)]
         copies.append(pltpu.make_async_copy(so_far, place, arrived.at[len(plan.chunks)]))
         copies[0].start()
-    placed(state, blocks, plan.main_tiles, plan.first)
+    pieces = [(step, first, block) for (step, first), block in zip(plan.pieces, blocks)]
+    placed(state, pieces, group_count, plan.first)
     at = plan.main_tiles - plan.first
     chip, core = lax.axis_index("freq"), lax.axis_index("sub")
     for hop, tiles in enumerate(plan.halos, 1):
         there = lax.axis_index("tm") + hop < lax.axis_size("tm")
         for tile in range(tiles):
-            joined, single = [
-                jnp.where(there, halo[tile, :, :].astype(jnp.float32), 0.0)
-                for halo in halos[2 * hop - 2 : 2 * hop]
-            ]
+            joined = jnp.where(there, halos[hop - 1][tile, :, :].astype(jnp.float32), 0.0)
             for index, mask in enumerate(step_masks(group_count, core)):
                 start = pl.multiple_of((chip ^ mask) * block_rows, block_rows)
-                if index + 1 < group_count:
-                    part = joined[index * block_rows : (index + 1) * block_rows]
-                else:
-                    part = single
+                part = joined[index * block_rows : (index + 1) * block_rows]
                 state[at, pl.ds(start, block_rows), :] = part
             at += 1
     for tile in range(at, at + plan.empty_tiles):
@@ -400,7 +399,8 @@
 
 
 class Plan:
-    def __init__(self, main_tiles, halos, empty_tiles, out_first, out_tiles, taken, given, levels, tap_tiles):
+    def __init__(self, pieces, main_tiles, halos, empty_tiles, out_first, out_tiles, taken, given, levels, tap_tiles):
+        self.pieces = pieces
         self.main_tiles, self.halos, self.empty_tiles = main_tiles, halos, empty_tiles
         self.out_first, self.out_tiles = out_first, out_tiles
         self.taken, self.given = taken, given
@@ -480,6 +480,11 @@
             ]
             + scratch,
             compiler_params=params,
+            cost_estimate=pl.CostEstimate(
+                flops=2 * plan.out_tiles * LANES * chan_rows * width_count * (tap_count + LANES),
+                bytes_accessed=40 * plan.out_tiles * LANES * chan_rows * width_count,
+                transcendentals=plan.out_tiles * LANES * chan_rows * (width_count + 1),
+            ),
         )(*operands)
 
     other_core = from_partner(filterbank, "sub", 1)
@@ -519,39 +524,39 @@
         scratch_shapes=[table],
         compiler_params=params,
     )(late_shifts, late_filters)
-    *main, last = exchanged(main)
+    first_tiles = min(time_tiles, far_tiles) if lax.axis_size("tm") > 1 else 0
+    *arrived, (step, first, last) = exchanged(main, first_tiles)
     columns, taps, last = lax.optimization_barrier((columns, taps, last))
-    main.append(last)
+    arrived.append((step, first, last))
+    pieces = [(step, first) for step, first, _ in arrived]
+    main = [block for _, _, block in arrived]
 
     halos, takes = [], []
     rest = far_tiles
     if lax.axis_size("tm") > 1:
-        first_tiles = min(time_tiles, far_tiles)
+        heads = [block for _, first, block in arrived if first == 0]
         joined = pl.pallas_call(
             join_kernel,
-            out_shape=jax.ShapeDtypeStruct(
-                (first_tiles, chan_rows - block_rows, LANES), jnp.bfloat16
-            ),
-            in_specs=[in_vmem] * (group_count - 1),
+            out_shape=jax.ShapeDtypeStruct((first_tiles, chan_rows, LANES), jnp.bfloat16),
+            in_specs=[in_vmem] * len(heads),
             out_specs=in_vmem,
-            scratch_shapes=[pltpu.VMEM((first_tiles, chan_rows - block_rows, LANES), jnp.float32)],
+            scratch_shapes=[pltpu.VMEM((first_tiles, chan_rows, LANES), jnp.float32)],
             compiler_params=params,
-        )(*main[:-1])
+        )(*heads)
         for hop in range(1, lax.axis_size("tm")):
             if rest > 0:
                 takes.append(min(time_tiles, rest))
                 halos.append(from_ahead(joined[: takes[-1]], hop))
-                halos.append(from_ahead(main[-1][: takes[-1]], hop))
                 rest -= takes[-1]
     lost = -(-sum(2**level for level in far_levels) // LANES) + tap_tiles
     early_tiles = time_tiles - lost
     if early_tiles <= 0:
-        plan = Plan(time_tiles, takes, rest, 0, time_tiles, False, False, far_levels, tap_tiles)
+        plan = Plan(pieces, time_tiles, takes, rest, 0, time_tiles, False, False, far_levels, tap_tiles)
         return between_chips(plan, main, halos)[0]
-    plan = Plan(time_tiles, [], 0, 0, early_tiles, False, True, far_levels, tap_tiles)
+    plan = Plan(pieces, time_tiles, [], 0, 0, early_tiles, False, True, far_levels, tap_tiles)
     out, *carried = between_chips(plan, main, [])
     late_tiles = time_tiles - early_tiles
-    plan = Plan(time_tiles, takes, rest, early_tiles, late_tiles, True, False, far_levels, tap_tiles)
+    plan = Plan(pieces, time_tiles, takes, rest, early_tiles, late_tiles, True, False, far_levels, tap_tiles)
     return between_chips(plan, main, halos, [*carried, out])[0]
 
 

time: 23.7 us -> 23.4 us (0.987)
  waiting for transfers between devices: 5.9 us -> 3.93 us
  starting transfers between devices: 9.9 us -> 11.6 us
    ppermute x3 -> x4, starting transfers between devices: 4.23 us -> 7.04 us  [exchanged(): lax.ppermute(blocks[step][first:end], ('freq', 'sub'), route)]
    ppermute x3 -> x4, waiting for transfers between devices: 4.35 us -> 1.98 us  [exchanged(): lax.ppermute(blocks[step][first:end], ('freq', 'sub'), route)]
    ppermute x3 -> x2, starting transfers between devices: 5.22 us -> 4.12 us  [from_ahead(): lax.ppermute(value, 'tm', [((block + steps) % count, block) for block in...]
    ppermute x3 -> x2, waiting for transfers between devices: 1.16 us -> 1.57 us  [from_ahead(): lax.ppermute(value, 'tm', [((block + steps) % count, block) for block in...]
  transfers between devices with their start and end apart: 7 -> 7, of which waited for: 5 -> 3; matrix products, arithmetic and copies ran while one was open for 0% -> 0% of each run, Pallas kernels for 19% -> 19%
where the time goes in v9:
time: 23.4 us; the launch traced here: 23.3 us
  starting transfers between devices  11.6 us (50%)
  Pallas kernels  6.7 us (29%)
  waiting for transfers between devices  3.93 us (17%)
  local copies, waits for them, and re-layouts  0.97 us (4%)
    ppermute x4, starting transfers between devices, exchanged(): lax.ppermute(blocks[step][first:end], ('freq', 'sub'), route)  7.04 us
    ppermute x2, starting transfers between devices, from_ahead(): lax.ppermute(value, 'tm', [((block + steps) % count, block) for block in...  4.12 us
    pallas_call x2, Pallas kernels, within_chip(): pl.pallas_call(functools.partial(chip_kernel, spans, out_tiles, group_cou...  3.38 us
    pallas_call x2, Pallas kernels, between_chips(): pl.pallas_call(functools.partial(trial_kernel, plan, group_count, level_c...  3.05 us
    ppermute x4, waiting for transfers between devices, exchanged(): lax.ppermute(blocks[step][first:end], ('freq', 'sub'), route)  1.98 us
    ppermute x2, waiting for transfers between devices, from_ahead(): lax.ppermute(value, 'tm', [((block + steps) % count, block) for block in...  1.57 us
    unnamed x6, local copies, waits for them, and re-layouts  0.96 us
  transfers between devices with their start and end apart: 7, of which 3 were waited for; matrix products, arithmetic and copies ran while one was open for 0% of the time, Pallas kernels for 19%

profile of v9, /device:TPU:0, one launch (start us, length us, event | category | flops | bytes accessed | tf_op | source)
XLA Modules:
  0.0 23.3 jit_solution(6280029443959361378)
XLA Ops:
  0.0 0.5 %collective-permute-start = (bf16[64,2048]{1,0:T(8,128)(2,1)}, bf16[64,2048]{1,0:T(8,128)(2,1)S(1)}, u32[]{:S(2)}, u32[]{:S(2)}) collective-permute-start(bf16[64,2048]{1,0:T(8,128)(2,1)} %whole.1), channel_id=1, source_target_pairs={{0,1},{1,0},{2,3},{3,2},{4,5},{5,4},{6,7},{7,6},{8,9},{9,8},{10,11... | collective-permute-start | bytes 786440 | tf_op jit(solution)/shard_map/ppermute | solution.py:41
  0.5 0.0 copy-start
  0.5 0.9 %copy-done = bf16[64,2048]{1,0:T(8,128)(2,1)S(1)} copy-done((bf16[64,2048]{1,0:T(8,128)(2,1)S(1)}, bf16[64,2048]{1,0:T(8,128)(2,1)}, u32[]{:S(2)}) %copy-start) | copy-done | bytes 262168
  1.4 0.0 copy-start.1
  1.4 0.4 %collective-permute-done.other.refs_1_ = bf16[64,2048]{1,0:T(8,128)(2,1)S(1)} collective-permute-done((bf16[64,2048]{1,0:T(8,128)(2,1)}, bf16[64,2048]{1,0:T(8,128)(2,1)S(1)}, u32[]{:S(2)}, u32[]{:S(2)}) %collective-permute-start) | collective-permute-done | bytes 262176 | tf_op jit(solution)/shard_map/ppermute | solution.py:41
  1.8 2.9 %collective-permute-start.1 = (bf16[128,128]{1,0:T(8,128)(2,1)S(1)}, bf16[128,128]{1,0:T(8,128)(2,1)S(1)}, u32[]{:S(2)}, u32[]{:S(2)}) collective-permute-start(bf16[128,128]{1,0:T(8,128)(2,1)S(1)} %shard_map.38), channel_id=1, source_target_pairs={{2,0},{0,2},{3,1},{1,3},{6,4},{4,6},{7,5},{5,7},{10,8},{8,10},{11,... | collective-permute-start | bytes 98312 | tf_op jit(solution)/shard_map/ppermute | solution.py:36
  4.8 0.0 copy-done.1
  4.8 2.8 %shard_map.39 = (f32[15,64,128]{2,1,0:T(8,128)S(1)}, f32[128,128]{1,0:T(8,128)S(1)}) custom-call(bf16[64,2048]{1,0:T(8,128)(2,1)S(1)} %shard_map.37.whole.refs_0_, bf16[64,2048]{1,0:T(8,128)(2,1)S(1)} %collective-permute-done.other.refs_1_, s32[9,512]{1,0:T(8,128)S(1)} %copy-done.1), custom_call_target="tpu_custom_call" | custom-call | tf_op jit(solution)/shard_map/pallas_call | solution.py:445
  7.5 0.0 collective-permute-done.1.refs_2_
  7.5 0.6 %shard_map.40 = (bf16[16,16,128]{2,1,0:T(8,128)(2,1)S(1)}, bf16[16,16,128]{2,1,0:T(8,128)(2,1)S(1)}, bf16[16,16,128]{2,1,0:T(8,128)(2,1)S(1)}, bf16[16,16,128]{2,1,0:T(8,128)(2,1)S(1)}) custom-call(bf16[64,2048]{1,0:T(8,128)(2,1)S(1)} %shard_map.37.whole.refs_0_, bf16[64,2048]{1,0:T(8,128)(2,1)S(1)} %collective-permute-done.other.refs_1_, ...), custom_call_target="tpu_custom_call" | custom-call | tf_op jit(solution)/shard_map/pallas_call | solution.py:445
  8.2 1.6 %collective-permute-start.3 = (bf16[16,16,128]{2,1,0:T(8,128)(2,1)S(1)}, bf16[16,16,128]{2,1,0:T(8,128)(2,1)S(1)}, u32[]{:S(2)}, u32[]{:S(2)}) collective-permute-start(bf16[16,16,128]{2,1,0:T(8,128)(2,1)S(1)} %get-tuple-element.32), channel_id=1, source_target_pairs={{0,4},{1,9},{4,0},{5,13},{8,12},{9,1},{12,8},{13,5},{2,6},{3,11},{... | collective-permute-start | bytes 196616 | tf_op jit(solution)/shard_map/ppermute | solution.py:64
  9.8 2.5 %collective-permute-start.4 = (bf16[16,16,128]{2,1,0:T(8,128)(2,1)S(1)}, bf16[16,16,128]{2,1,0:T(8,128)(2,1)S(1)}, u32[]{:S(2)}, u32[]{:S(2)}) collective-permute-start(bf16[16,16,128]{2,1,0:T(8,128)(2,1)S(1)} %get-tuple-element.33), channel_id=1, source_target_pairs={{0,12},{1,13},{4,8},{5,9},{8,4},{9,5},{12,0},{13,1},{2,14},{3,15},... | collective-permute-start | bytes 196616 | tf_op jit(solution)/shard_map/ppermute | solution.py:64
  12.3 0.1 collective-permute-start.5
  12.4 2.8 %collective-permute-start.2 = (bf16[11,16,128]{2,1,0:T(8,128)(2,1)S(1)}, bf16[11,16,128]{2,1,0:T(8,128)(2,1)S(1)}, u32[]{:S(2)}, u32[]{:S(2)}) collective-permute-start(bf16[11,16,128]{2,1,0:T(8,128)(2,1)S(1)} %slice.6), channel_id=1, source_target_pairs={{0,8},{1,5},{4,12},{5,1},{8,0},{9,13},{12,4},{13,9},{2,10},{3,7},{... | collective-permute-start | bytes 135176 | tf_op jit(solution)/shard_map/ppermute | solution.py:64
  15.2 2.0 %collective-permute-done.5.refs_3_ = bf16[5,16,128]{2,1,0:T(8,128)(2,1)S(1)} collective-permute-done((bf16[5,16,128]{2,1,0:T(8,128)(2,1)S(1)}, bf16[5,16,128]{2,1,0:T(8,128)(2,1)S(1)}, u32[]{:S(2)}, u32[]{:S(2)}) %collective-permute-start.5) | collective-permute-done | bytes 20512 | tf_op jit(solution)/shard_map/ppermute | solution.py:64
  17.2 0.0 collective-permute-done.3.refs_1_
  17.2 0.0 collective-permute-done.4.refs_2_
  17.2 1.2 %collective-permute-start.6 = (bf16[5,64,128]{2,1,0:T(8,128)(2,1)S(1)}, bf16[5,64,128]{2,1,0:T(8,128)(2,1)S(1)}, u32[]{:S(2)}, u32[]{:S(2)}) collective-permute-start(bf16[5,64,128]{2,1,0:T(8,128)(2,1)S(1)} %shard_map.42), channel_id=1, source_target_pairs={{2,0},{0,2},{3,1},{1,3},{6,4},{4,6},{7,5},{5,7},{10,8},{8,10},{11,... | collective-permute-start | bytes 245768 | tf_op jit(solution)/shard_map/ppermute | solution.py:36
  18.4 0.0 copy-done.2
  18.4 0.2 shard_map.41
  18.6 0.0 collective-permute-done.2.refs_4_
  18.7 1.5 %shard_map.43 = (f32[64,1408]{1,0:T(8,128)S(1)}, bf16[2,64,128]{2,1,0:T(8,128)(2,1)S(1)}) custom-call(f32[128,128]{1,0:T(8,128)S(1)} %get-tuple-element.29.columns, bf16[768,384]{1,0:T(8,128)(2,1)S(1)} %get-tuple-element.30.taps, bf16[16,16,128]{2,1,0:T(8,128)(2,1)S(1)} %get-tuple-element.31.refs_0_, ...), custom_call_target="tpu_custom_call" | custom-call | flops 415236096 | bytes 21626880 | tf_op jit(solution)/shard_map/pallas_call | solution.py:470
  20.2 1.6 %collective-permute-done.6.refs_5_ = bf16[5,64,128]{2,1,0:T(8,128)(2,1)S(1)} collective-permute-done((bf16[5,64,128]{2,1,0:T(8,128)(2,1)S(1)}, bf16[5,64,128]{2,1,0:T(8,128)(2,1)S(1)}, u32[]{:S(2)}, u32[]{:S(2)}) %collective-permute-start.6) | collective-permute-done | bytes 81952 | tf_op jit(solution)/shard_map/ppermute | solution.py:36
  21.7 1.6 %shard_map.44 = f32[64,2048]{1,0:T(8,128)} custom-call(f32[128,128]{1,0:T(8,128)S(1)} %get-tuple-element.29.columns, bf16[768,384]{1,0:T(8,128)(2,1)S(1)} %get-tuple-element.30.taps, bf16[16,16,128]{2,1,0:T(8,128)(2,1)S(1)} %get-tuple-element.31.refs_0_, bf16[16,16,128]{2,1,0:T(8,128)(2,1)S(1)} %collective-permute-done.3.refs_1_, ...), custom_call_target="tpu_custom_call" | custom-call | flops 188743680 | bytes 9830400 | tf_op jit(solution)/shard_map/pallas_call | solution.py:470
  (6 shorter events, 0.0 us)
Async XLA Ops:
  0.0 1.8 %collective-permute-start = (bf16[64,2048]{1,0:T(8,128)(2,1)}, bf16[64,2048]{1,0:T(8,128)(2,1)S(1)}, u32[]{:S(2)}, u32[]{:S(2)}) collective-permute-start(bf16[64,2048]{1,0:T(8,128)(2,1)} %whole.1), channel_id=1, source_target_pairs={{0,1},{1,0},{2,3},{3,2},{4,5},{5,4},{6,7},{7,6},{8,9},{9,8},{10,11... | collective-permute-start | bytes 786440 | tf_op jit(solution)/shard_map/ppermute | solution.py:41
  0.5 0.9 %copy-start = (bf16[64,2048]{1,0:T(8,128)(2,1)S(1)}, bf16[64,2048]{1,0:T(8,128)(2,1)}, u32[]{:S(2)}) copy-start(bf16[64,2048]{1,0:T(8,128)(2,1)} %whole.1) | copy-start | bytes 786436
  1.4 3.3 %copy-start.1 = (s32[9,512]{1,0:T(8,128)S(1)}, s32[9,512]{1,0:T(8,128)}, u32[]{:S(2)}) copy-start(s32[9,512]{1,0:T(8,128)} %shifts) | copy-start | bytes 55300
  1.8 5.7 %collective-permute-start.1 = (bf16[128,128]{1,0:T(8,128)(2,1)S(1)}, bf16[128,128]{1,0:T(8,128)(2,1)S(1)}, u32[]{:S(2)}, u32[]{:S(2)}) collective-permute-start(bf16[128,128]{1,0:T(8,128)(2,1)S(1)} %shard_map.38), channel_id=1, source_target_pairs={{2,0},{0,2},{3,1},{1,3},{6,4},{4,6},{7,5},{5,7},{10,8},{8,10},{11,... | collective-permute-start | bytes 98312 | tf_op jit(solution)/shard_map/ppermute | solution.py:36
  8.2 9.0 %collective-permute-start.3 = (bf16[16,16,128]{2,1,0:T(8,128)(2,1)S(1)}, bf16[16,16,128]{2,1,0:T(8,128)(2,1)S(1)}, u32[]{:S(2)}, u32[]{:S(2)}) collective-permute-start(bf16[16,16,128]{2,1,0:T(8,128)(2,1)S(1)} %get-tuple-element.32), channel_id=1, source_target_pairs={{0,4},{1,9},{4,0},{5,13},{8,12},{9,1},{12,8},{13,5},{2,6},{3,11},{... | collective-permute-start | bytes 196616 | tf_op jit(solution)/shard_map/ppermute | solution.py:64
  9.8 7.4 %collective-permute-start.4 = (bf16[16,16,128]{2,1,0:T(8,128)(2,1)S(1)}, bf16[16,16,128]{2,1,0:T(8,128)(2,1)S(1)}, u32[]{:S(2)}, u32[]{:S(2)}) collective-permute-start(bf16[16,16,128]{2,1,0:T(8,128)(2,1)S(1)} %get-tuple-element.33), channel_id=1, source_target_pairs={{0,12},{1,13},{4,8},{5,9},{8,4},{9,5},{12,0},{13,1},{2,14},{3,15},... | collective-permute-start | bytes 196616 | tf_op jit(solution)/shard_map/ppermute | solution.py:64
  12.3 4.9 %collective-permute-start.5 = (bf16[5,16,128]{2,1,0:T(8,128)(2,1)S(1)}, bf16[5,16,128]{2,1,0:T(8,128)(2,1)S(1)}, u32[]{:S(2)}, u32[]{:S(2)}) collective-permute-start(bf16[5,16,128]{2,1,0:T(8,128)(2,1)S(1)} %slice.7), channel_id=1, source_target_pairs={{0,8},{1,5},{4,12},{5,1},{8,0},{9,13},{12,4},{13,9},{2,10},{3,7},{... | collective-permute-start | bytes 61448 | tf_op jit(solution)/shard_map/ppermute | solution.py:64
  12.4 6.2 %collective-permute-start.2 = (bf16[11,16,128]{2,1,0:T(8,128)(2,1)S(1)}, bf16[11,16,128]{2,1,0:T(8,128)(2,1)S(1)}, u32[]{:S(2)}, u32[]{:S(2)}) collective-permute-start(bf16[11,16,128]{2,1,0:T(8,128)(2,1)S(1)} %slice.6), channel_id=1, source_target_pairs={{0,8},{1,5},{4,12},{5,1},{8,0},{9,13},{12,4},{13,9},{2,10},{3,7},{... | collective-permute-start | bytes 135176 | tf_op jit(solution)/shard_map/ppermute | solution.py:64
  15.2 3.2 %copy-start.2 = (bf16[6,256]{1,0:T(8,128)(2,1)S(1)}, bf16[6,256]{1,0:T(8,128)(2,1)}, u32[]{:S(2)}) copy-start(bf16[6,256]{1,0:T(8,128)(2,1)} %filters) | copy-start | bytes 9220
  17.2 4.5 %collective-permute-start.6 = (bf16[5,64,128]{2,1,0:T(8,128)(2,1)S(1)}, bf16[5,64,128]{2,1,0:T(8,128)(2,1)S(1)}, u32[]{:S(2)}, u32[]{:S(2)}) collective-permute-start(bf16[5,64,128]{2,1,0:T(8,128)(2,1)S(1)} %shard_map.42), channel_id=1, source_target_pairs={{2,0},{0,2},{3,1},{1,3},{6,4},{4,6},{7,5},{5,7},{10,8},{8,10},{11,... | collective-permute-start | bytes 245768 | tf_op jit(solution)/shard_map/ppermute | solution.py:36

commit v10 on v8

--- a/solution.py
+++ b/solution.py
@@ -316,7 +316,7 @@
 
 def trial_kernel(plan, group_count, level_count, scale, columns, taps, *refs):
     blocks, refs = refs[:group_count], refs[group_count:]
-    halos, refs = refs[: 2 * len(plan.halos)], refs[2 * len(plan.halos) :]
+    halos, refs = refs[: 3 * len(plan.halos)], refs[3 * len(plan.halos) :]
     if plan.taken:
         carried, so_far, refs = refs[0], refs[1], refs[2:]
     out, refs = refs[0], refs[1:]
@@ -342,16 +342,16 @@
     for hop, tiles in enumerate(plan.halos, 1):
         there = lax.axis_index("tm") + hop < lax.axis_size("tm")
         for tile in range(tiles):
-            joined, single = [
+            joined, *single = [
                 jnp.where(there, halo[tile, :, :].astype(jnp.float32), 0.0)
-                for halo in halos[2 * hop - 2 : 2 * hop]
+                for halo in halos[3 * hop - 3 : 3 * hop]
             ]
             for index, mask in enumerate(step_masks(group_count, core)):
                 start = pl.multiple_of((chip ^ mask) * block_rows, block_rows)
-                if index + 1 < group_count:
+                if index + 2 < group_count:
                     part = joined[index * block_rows : (index + 1) * block_rows]
                 else:
-                    part = single
+                    part = single[index + 2 - group_count]
                 state[at, pl.ds(start, block_rows), :] = part
             at += 1
     for tile in range(at, at + plan.empty_tiles):
@@ -530,18 +530,18 @@
         joined = pl.pallas_call(
             join_kernel,
             out_shape=jax.ShapeDtypeStruct(
-                (first_tiles, chan_rows - block_rows, LANES), jnp.bfloat16
+                (first_tiles, chan_rows - 2 * block_rows, LANES), jnp.bfloat16
             ),
-            in_specs=[in_vmem] * (group_count - 1),
+            in_specs=[in_vmem] * (group_count - 2),
             out_specs=in_vmem,
-            scratch_shapes=[pltpu.VMEM((first_tiles, chan_rows - block_rows, LANES), jnp.float32)],
+            scratch_shapes=[pltpu.VMEM((first_tiles, chan_rows - 2 * block_rows, LANES), jnp.float32)],
             compiler_params=params,
-        )(*main[:-1])
+        )(*main[:-2])
         for hop in range(1, lax.axis_size("tm")):
             if rest > 0:
                 takes.append(min(time_tiles, rest))
                 halos.append(from_ahead(joined[: takes[-1]], hop))
-                halos.append(from_ahead(main[-1][: takes[-1]], hop))
+                halos += [from_ahead(block[: takes[-1]], hop) for block in main[-2:]]
                 rest -= takes[-1]
     lost = -(-sum(2**level for level in far_levels) // LANES) + tap_tiles
     early_tiles = time_tiles - lost

time: 23.7 us -> 23.7 us (level)
  waiting for transfers between devices: 5.9 us -> 5.25 us
  starting transfers between devices: 9.9 us -> 10.5 us
    ppermute x3, waiting for transfers between devices: 4.35 us -> 3.7 us  [exchanged(): received.append(lax.ppermute(block, ('freq', 'sub'), route))]
    ppermute x3 -> x4, starting transfers between devices: 5.22 us -> 5.86 us  [from_ahead(): lax.ppermute(value, 'tm', [((block + steps) % count, block) for block in...]
    ppermute x3 -> x4, waiting for transfers between devices: 1.16 us -> 1.16 us  [from_ahead(): lax.ppermute(value, 'tm', [((block + steps) % count, block) for block in...]
  transfers between devices with their start and end apart: 7 -> 8, of which waited for: 5 -> 5; matrix products, arithmetic and copies ran while one was open for 0% -> 0% of each run, Pallas kernels for 19% -> 19%
where the time goes in v10:
time: 23.7 us; the launch traced here: 23.5 us
  starting transfers between devices  10.5 us (44%)
  Pallas kernels  6.68 us (28%)
  waiting for transfers between devices  5.25 us (22%)
  local copies, waits for them, and re-layouts  0.96 us (4%)
    ppermute x4, starting transfers between devices, from_ahead(): lax.ppermute(value, 'tm', [((block + steps) % count, block) for block in...  5.86 us
    ppermute x3, starting transfers between devices, exchanged(): received.append(lax.ppermute(block, ('freq', 'sub'), route))  4.23 us
    ppermute x3, waiting for transfers between devices, exchanged(): received.append(lax.ppermute(block, ('freq', 'sub'), route))  3.7 us
    pallas_call x2, Pallas kernels, within_chip(): pl.pallas_call(functools.partial(chip_kernel, spans, out_tiles, group_cou...  3.38 us
    pallas_call x2, Pallas kernels, between_chips(): pl.pallas_call(functools.partial(trial_kernel, plan, group_count, level_c...  3.04 us
    ppermute x4, waiting for transfers between devices, from_ahead(): lax.ppermute(value, 'tm', [((block + steps) % count, block) for block in...  1.16 us
    unnamed x6, local copies, waits for them, and re-layouts  0.96 us
  transfers between devices with their start and end apart: 8, of which 5 were waited for; matrix products, arithmetic and copies ran while one was open for 0% of the time, Pallas kernels for 19%

profile of v10, /device:TPU:0, one launch (start us, length us, event | category | flops | bytes accessed | tf_op | source)
XLA Modules:
  0.0 23.5 jit_solution(684044096949270302)
XLA Ops:
  0.0 0.5 %collective-permute-start = (bf16[64,2048]{1,0:T(8,128)(2,1)}, bf16[64,2048]{1,0:T(8,128)(2,1)S(1)}, u32[]{:S(2)}, u32[]{:S(2)}) collective-permute-start(bf16[64,2048]{1,0:T(8,128)(2,1)} %whole.1), channel_id=1, source_target_pairs={{0,1},{1,0},{2,3},{3,2},{4,5},{5,4},{6,7},{7,6},{8,9},{9,8},{10,11... | collective-permute-start | bytes 786440 | tf_op jit(solution)/shard_map/ppermute | solution.py:41
  0.5 0.9 %copy-done = bf16[64,2048]{1,0:T(8,128)(2,1)S(1)} copy-done((bf16[64,2048]{1,0:T(8,128)(2,1)S(1)}, bf16[64,2048]{1,0:T(8,128)(2,1)}, u32[]{:S(2)}) %copy-start) | copy-done | bytes 262168
  1.4 0.0 copy-start.1
  1.4 0.4 %collective-permute-done.other.refs_1_ = bf16[64,2048]{1,0:T(8,128)(2,1)S(1)} collective-permute-done((bf16[64,2048]{1,0:T(8,128)(2,1)}, bf16[64,2048]{1,0:T(8,128)(2,1)S(1)}, u32[]{:S(2)}, u32[]{:S(2)}) %collective-permute-start) | collective-permute-done | bytes 262176 | tf_op jit(solution)/shard_map/ppermute | solution.py:41
  1.8 2.9 %collective-permute-start.1 = (bf16[128,128]{1,0:T(8,128)(2,1)S(1)}, bf16[128,128]{1,0:T(8,128)(2,1)S(1)}, u32[]{:S(2)}, u32[]{:S(2)}) collective-permute-start(bf16[128,128]{1,0:T(8,128)(2,1)S(1)} %shard_map.38), channel_id=1, source_target_pairs={{2,0},{0,2},{3,1},{1,3},{6,4},{4,6},{7,5},{5,7},{10,8},{8,10},{11,... | collective-permute-start | bytes 98312 | tf_op jit(solution)/shard_map/ppermute | solution.py:36
  4.8 2.8 %shard_map.39 = (f32[15,64,128]{2,1,0:T(8,128)S(1)}, f32[128,128]{1,0:T(8,128)S(1)}) custom-call(bf16[64,2048]{1,0:T(8,128)(2,1)S(1)} %shard_map.37.whole.refs_0_, bf16[64,2048]{1,0:T(8,128)(2,1)S(1)} %collective-permute-done.other.refs_1_, s32[9,512]{1,0:T(8,128)S(1)} %copy-done.1), custom_call_target="tpu_custom_call" | custom-call | tf_op jit(solution)/shard_map/pallas_call | solution.py:445
  7.5 0.0 collective-permute-done.1.refs_2_
  7.5 0.6 %shard_map.40 = (bf16[16,16,128]{2,1,0:T(8,128)(2,1)S(1)}, bf16[16,16,128]{2,1,0:T(8,128)(2,1)S(1)}, bf16[16,16,128]{2,1,0:T(8,128)(2,1)S(1)}, bf16[16,16,128]{2,1,0:T(8,128)(2,1)S(1)}) custom-call(bf16[64,2048]{1,0:T(8,128)(2,1)S(1)} %shard_map.37.whole.refs_0_, bf16[64,2048]{1,0:T(8,128)(2,1)S(1)} %collective-permute-done.other.refs_1_, ...), custom_call_target="tpu_custom_call" | custom-call | tf_op jit(solution)/shard_map/pallas_call | solution.py:445
  8.2 1.6 %collective-permute-start.3 = (bf16[16,16,128]{2,1,0:T(8,128)(2,1)S(1)}, bf16[16,16,128]{2,1,0:T(8,128)(2,1)S(1)}, u32[]{:S(2)}, u32[]{:S(2)}) collective-permute-start(bf16[16,16,128]{2,1,0:T(8,128)(2,1)S(1)} %get-tuple-element.32), channel_id=1, source_target_pairs={{0,4},{1,9},{4,0},{5,13},{8,12},{9,1},{12,8},{13,5},{2,6},{3,11},{... | collective-permute-start | bytes 196616 | tf_op jit(solution)/shard_map/ppermute | solution.py:61
  9.8 2.5 %collective-permute-start.4 = (bf16[16,16,128]{2,1,0:T(8,128)(2,1)S(1)}, bf16[16,16,128]{2,1,0:T(8,128)(2,1)S(1)}, u32[]{:S(2)}, u32[]{:S(2)}) collective-permute-start(bf16[16,16,128]{2,1,0:T(8,128)(2,1)S(1)} %get-tuple-element.33), channel_id=1, source_target_pairs={{0,12},{1,13},{4,8},{5,9},{8,4},{9,5},{12,0},{13,1},{2,14},{3,15},... | collective-permute-start | bytes 196616 | tf_op jit(solution)/shard_map/ppermute | solution.py:61
  12.3 0.1 collective-permute-start.2
  12.4 0.6 %collective-permute-done.3.refs_1_ = bf16[16,16,128]{2,1,0:T(8,128)(2,1)S(1)} collective-permute-done((bf16[16,16,128]{2,1,0:T(8,128)(2,1)S(1)}, bf16[16,16,128]{2,1,0:T(8,128)(2,1)S(1)}, u32[]{:S(2)}, u32[]{:S(2)}) %collective-permute-start.3) | collective-permute-done | bytes 65568 | tf_op jit(solution)/shard_map/ppermute | solution.py:61
  13.0 0.6 %collective-permute-start.5 = (bf16[5,32,128]{2,1,0:T(8,128)(2,1)S(1)}, bf16[5,32,128]{2,1,0:T(8,128)(2,1)S(1)}, u32[]{:S(2)}, u32[]{:S(2)}) collective-permute-start(bf16[5,32,128]{2,1,0:T(8,128)(2,1)S(1)} %shard_map.42), channel_id=1, source_target_pairs={{2,0},{0,2},{3,1},{1,3},{6,4},{4,6},{7,5},{5,7},{10,8},{8,10},{11,... | collective-permute-start | bytes 122888 | tf_op jit(solution)/shard_map/ppermute | solution.py:36
  13.6 0.0 copy-done.2
  13.6 0.2 shard_map.41
  13.9 2.7 %collective-permute-done.4.refs_2_ = bf16[16,16,128]{2,1,0:T(8,128)(2,1)S(1)} collective-permute-done((bf16[16,16,128]{2,1,0:T(8,128)(2,1)S(1)}, bf16[16,16,128]{2,1,0:T(8,128)(2,1)S(1)}, u32[]{:S(2)}, u32[]{:S(2)}) %collective-permute-start.4) | collective-permute-done | bytes 65568 | tf_op jit(solution)/shard_map/ppermute | solution.py:61
  16.5 1.2 %collective-permute-start.6 = (bf16[5,16,128]{2,1,0:T(8,128)(2,1)S(1)}, bf16[5,16,128]{2,1,0:T(8,128)(2,1)S(1)}, u32[]{:S(2)}, u32[]{:S(2)}) collective-permute-start(bf16[5,16,128]{2,1,0:T(8,128)(2,1)S(1)} %slice.8), channel_id=1, source_target_pairs={{2,0},{0,2},{3,1},{1,3},{6,4},{4,6},{7,5},{5,7},{10,8},{8,10},{11,... | collective-permute-start | bytes 61448 | tf_op jit(solution)/shard_map/ppermute | solution.py:36
  17.7 0.5 %collective-permute-done.2.refs_3_ = bf16[16,16,128]{2,1,0:T(8,128)(2,1)S(1)} collective-permute-done((bf16[16,16,128]{2,1,0:T(8,128)(2,1)S(1)}, bf16[16,16,128]{2,1,0:T(8,128)(2,1)S(1)}, u32[]{:S(2)}, u32[]{:S(2)}) %collective-permute-start.2) | collective-permute-done | bytes 65568 | tf_op jit(solution)/shard_map/ppermute | solution.py:61
  18.2 1.1 %collective-permute-start.7 = (bf16[5,16,128]{2,1,0:T(8,128)(2,1)S(1)}, bf16[5,16,128]{2,1,0:T(8,128)(2,1)S(1)}, u32[]{:S(2)}, u32[]{:S(2)}) collective-permute-start(bf16[5,16,128]{2,1,0:T(8,128)(2,1)S(1)} %slice.7), channel_id=1, source_target_pairs={{2,0},{0,2},{3,1},{1,3},{6,4},{4,6},{7,5},{5,7},{10,8},{8,10},{11,... | collective-permute-start | bytes 61448 | tf_op jit(solution)/shard_map/ppermute | solution.py:36
  19.3 1.5 %shard_map.43 = (f32[64,1408]{1,0:T(8,128)S(1)}, bf16[2,64,128]{2,1,0:T(8,128)(2,1)S(1)}) custom-call(f32[128,128]{1,0:T(8,128)S(1)} %get-tuple-element.29.columns, bf16[768,384]{1,0:T(8,128)(2,1)S(1)} %get-tuple-element.30.taps, bf16[16,16,128]{2,1,0:T(8,128)(2,1)S(1)} %get-tuple-element.31.refs_0_, ...), custom_call_target="tpu_custom_call" | custom-call | tf_op jit(solution)/shard_map/pallas_call | solution.py:470
  20.8 0.0 collective-permute-done.6.refs_5_
  20.8 1.1 %collective-permute-done.7.refs_6_ = bf16[5,16,128]{2,1,0:T(8,128)(2,1)S(1)} collective-permute-done((bf16[5,16,128]{2,1,0:T(8,128)(2,1)S(1)}, bf16[5,16,128]{2,1,0:T(8,128)(2,1)S(1)}, u32[]{:S(2)}, u32[]{:S(2)}) %collective-permute-start.7) | collective-permute-done | bytes 20512 | tf_op jit(solution)/shard_map/ppermute | solution.py:36
  21.9 0.0 collective-permute-done.5.refs_4_
  21.9 1.6 %shard_map.44 = f32[64,2048]{1,0:T(8,128)} custom-call(f32[128,128]{1,0:T(8,128)S(1)} %get-tuple-element.29.columns, bf16[768,384]{1,0:T(8,128)(2,1)S(1)} %get-tuple-element.30.taps, bf16[16,16,128]{2,1,0:T(8,128)(2,1)S(1)} %get-tuple-element.31.refs_0_, bf16[16,16,128]{2,1,0:T(8,128)(2,1)S(1)} %collective-permute-done.3.refs_1_, ...), custom_call_target="tpu_custom_call" | custom-call | tf_op jit(solution)/shard_map/pallas_call | solution.py:470
  (8 shorter events, 0.0 us)
Async XLA Ops:
  0.0 1.8 %collective-permute-start = (bf16[64,2048]{1,0:T(8,128)(2,1)}, bf16[64,2048]{1,0:T(8,128)(2,1)S(1)}, u32[]{:S(2)}, u32[]{:S(2)}) collective-permute-start(bf16[64,2048]{1,0:T(8,128)(2,1)} %whole.1), channel_id=1, source_target_pairs={{0,1},{1,0},{2,3},{3,2},{4,5},{5,4},{6,7},{7,6},{8,9},{9,8},{10,11... | collective-permute-start | bytes 786440 | tf_op jit(solution)/shard_map/ppermute | solution.py:41
  0.5 0.9 %copy-start = (bf16[64,2048]{1,0:T(8,128)(2,1)S(1)}, bf16[64,2048]{1,0:T(8,128)(2,1)}, u32[]{:S(2)}) copy-start(bf16[64,2048]{1,0:T(8,128)(2,1)} %whole.1) | copy-start | bytes 786436
  1.4 3.3 %copy-start.1 = (s32[9,512]{1,0:T(8,128)S(1)}, s32[9,512]{1,0:T(8,128)}, u32[]{:S(2)}) copy-start(s32[9,512]{1,0:T(8,128)} %shifts) | copy-start | bytes 55300
  1.8 5.7 %collective-permute-start.1 = (bf16[128,128]{1,0:T(8,128)(2,1)S(1)}, bf16[128,128]{1,0:T(8,128)(2,1)S(1)}, u32[]{:S(2)}, u32[]{:S(2)}) collective-permute-start(bf16[128,128]{1,0:T(8,128)(2,1)S(1)} %shard_map.38), channel_id=1, source_target_pairs={{2,0},{0,2},{3,1},{1,3},{6,4},{4,6},{7,5},{5,7},{10,8},{8,10},{11,... | collective-permute-start | bytes 98312 | tf_op jit(solution)/shard_map/ppermute | solution.py:36
  8.2 4.8 %collective-permute-start.3 = (bf16[16,16,128]{2,1,0:T(8,128)(2,1)S(1)}, bf16[16,16,128]{2,1,0:T(8,128)(2,1)S(1)}, u32[]{:S(2)}, u32[]{:S(2)}) collective-permute-start(bf16[16,16,128]{2,1,0:T(8,128)(2,1)S(1)} %get-tuple-element.32), channel_id=1, source_target_pairs={{0,4},{1,9},{4,0},{5,13},{8,12},{9,1},{12,8},{13,5},{2,6},{3,11},{... | collective-permute-start | bytes 196616 | tf_op jit(solution)/shard_map/ppermute | solution.py:61
  9.8 6.7 %collective-permute-start.4 = (bf16[16,16,128]{2,1,0:T(8,128)(2,1)S(1)}, bf16[16,16,128]{2,1,0:T(8,128)(2,1)S(1)}, u32[]{:S(2)}, u32[]{:S(2)}) collective-permute-start(bf16[16,16,128]{2,1,0:T(8,128)(2,1)S(1)} %get-tuple-element.33), channel_id=1, source_target_pairs={{0,12},{1,13},{4,8},{5,9},{8,4},{9,5},{12,0},{13,1},{2,14},{3,15},... | collective-permute-start | bytes 196616 | tf_op jit(solution)/shard_map/ppermute | solution.py:61
  12.3 5.9 %collective-permute-start.2 = (bf16[16,16,128]{2,1,0:T(8,128)(2,1)S(1)}, bf16[16,16,128]{2,1,0:T(8,128)(2,1)S(1)}, u32[]{:S(2)}, u32[]{:S(2)}) collective-permute-start(bf16[16,16,128]{2,1,0:T(8,128)(2,1)S(1)} %get-tuple-element.28), channel_id=1, source_target_pairs={{0,8},{1,5},{4,12},{5,1},{8,0},{9,13},{12,4},{13,9},{2,10},{3,7},{... | collective-permute-start | bytes 196616 | tf_op jit(solution)/shard_map/ppermute | solution.py:61
  12.4 1.2 %copy-start.2 = (bf16[6,256]{1,0:T(8,128)(2,1)S(1)}, bf16[6,256]{1,0:T(8,128)(2,1)}, u32[]{:S(2)}) copy-start(bf16[6,256]{1,0:T(8,128)(2,1)} %filters) | copy-start | bytes 9220
  13.0 8.9 %collective-permute-start.5 = (bf16[5,32,128]{2,1,0:T(8,128)(2,1)S(1)}, bf16[5,32,128]{2,1,0:T(8,128)(2,1)S(1)}, u32[]{:S(2)}, u32[]{:S(2)}) collective-permute-start(bf16[5,32,128]{2,1,0:T(8,128)(2,1)S(1)} %shard_map.42), channel_id=1, source_target_pairs={{2,0},{0,2},{3,1},{1,3},{6,4},{4,6},{7,5},{5,7},{10,8},{8,10},{11,... | collective-permute-start | bytes 122888 | tf_op jit(solution)/shard_map/ppermute | solution.py:36
  16.5 4.2 %collective-permute-start.6 = (bf16[5,16,128]{2,1,0:T(8,128)(2,1)S(1)}, bf16[5,16,128]{2,1,0:T(8,128)(2,1)S(1)}, u32[]{:S(2)}, u32[]{:S(2)}) collective-permute-start(bf16[5,16,128]{2,1,0:T(8,128)(2,1)S(1)} %slice.8), channel_id=1, source_target_pairs={{2,0},{0,2},{3,1},{1,3},{6,4},{4,6},{7,5},{5,7},{10,8},{8,10},{11,... | collective-permute-start | bytes 61448 | tf_op jit(solution)/shard_map/ppermute | solution.py:36
  18.2 3.8 %collective-permute-start.7 = (bf16[5,16,128]{2,1,0:T(8,128)(2,1)S(1)}, bf16[5,16,128]{2,1,0:T(8,128)(2,1)S(1)}, u32[]{:S(2)}, u32[]{:S(2)}) collective-permute-start(bf16[5,16,128]{2,1,0:T(8,128)(2,1)S(1)} %slice.7), channel_id=1, source_target_pairs={{2,0},{0,2},{3,1},{1,3},{6,4},{4,6},{7,5},{5,7},{10,8},{8,10},{11,... | collective-permute-start | bytes 61448 | tf_op jit(solution)/shard_map/ppermute | solution.py:36

commit v11 on v8

--- a/solution.py
+++ b/solution.py
@@ -43,7 +43,7 @@
 
 def mask_orders(group_count):
     far = list(range(group_count - 1, 1, -1))
-    return [1, *far], far[-1:] + far[:-1] + [1]
+    return [*far[:-1], 1, *far[-1:]], [*far[-1:], *far[:-1], 1]
 
 
 def step_masks(group_count, core):

time: 23.7 us -> 23.4 us (0.987)
  waiting for transfers between devices: 5.9 us -> 5.58 us
    ppermute x3, waiting for transfers between devices: 1.16 us -> 0.61 us  [from_ahead(): lax.ppermute(value, 'tm', [((block + steps) % count, block) for block in...]
  transfers between devices with their start and end apart: 7 -> 7, of which waited for: 5 -> 4; matrix products, arithmetic and copies ran while one was open for 0% -> 0% of each run, Pallas kernels for 19% -> 19%
where the time goes in v11:
time: 23.4 us; the launch traced here: 23.2 us
  starting transfers between devices  9.92 us (42%)
  Pallas kernels  6.69 us (29%)
  waiting for transfers between devices  5.58 us (24%)
  local copies, waits for them, and re-layouts  0.96 us (4%)
    ppermute x3, starting transfers between devices, from_ahead(): lax.ppermute(value, 'tm', [((block + steps) % count, block) for block in...  5.02 us
    ppermute x3, waiting for transfers between devices, exchanged(): received.append(lax.ppermute(block, ('freq', 'sub'), route))  4.58 us
    ppermute x3, starting transfers between devices, exchanged(): received.append(lax.ppermute(block, ('freq', 'sub'), route))  4.45 us
    pallas_call x2, Pallas kernels, within_chip(): pl.pallas_call(functools.partial(chip_kernel, spans, out_tiles, group_cou...  3.38 us
    pallas_call x2, Pallas kernels, between_chips(): pl.pallas_call(functools.partial(trial_kernel, plan, group_count, level_c...  3.04 us
    unnamed x6, local copies, waits for them, and re-layouts  0.96 us
    ppermute x3, waiting for transfers between devices, from_ahead(): lax.ppermute(value, 'tm', [((block + steps) % count, block) for block in...  0.61 us
  transfers between devices with their start and end apart: 7, of which 4 were waited for; matrix products, arithmetic and copies ran while one was open for 0% of the time, Pallas kernels for 19%

profile of v11, /device:TPU:0, one launch (start us, length us, event | category | flops | bytes accessed | tf_op | source)
XLA Modules:
  0.0 23.2 jit_solution(10357111170011220474)
XLA Ops:
  0.0 0.5 %collective-permute-start = (bf16[64,2048]{1,0:T(8,128)(2,1)}, bf16[64,2048]{1,0:T(8,128)(2,1)S(1)}, u32[]{:S(2)}, u32[]{:S(2)}) collective-permute-start(bf16[64,2048]{1,0:T(8,128)(2,1)} %whole.1), channel_id=1, source_target_pairs={{0,1},{1,0},{2,3},{3,2},{4,5},{5,4},{6,7},{7,6},{8,9},{9,8},{10,11... | collective-permute-start | bytes 786440 | tf_op jit(solution)/shard_map/ppermute | solution.py:41
  0.5 0.9 %copy-done = bf16[64,2048]{1,0:T(8,128)(2,1)S(1)} copy-done((bf16[64,2048]{1,0:T(8,128)(2,1)S(1)}, bf16[64,2048]{1,0:T(8,128)(2,1)}, u32[]{:S(2)}) %copy-start) | copy-done | bytes 262168
  1.4 0.0 copy-start.1
  1.4 0.4 %collective-permute-done.other.refs_1_ = bf16[64,2048]{1,0:T(8,128)(2,1)S(1)} collective-permute-done((bf16[64,2048]{1,0:T(8,128)(2,1)}, bf16[64,2048]{1,0:T(8,128)(2,1)S(1)}, u32[]{:S(2)}, u32[]{:S(2)}) %collective-permute-start) | collective-permute-done | bytes 262176 | tf_op jit(solution)/shard_map/ppermute | solution.py:41
  1.8 2.9 %collective-permute-start.1 = (bf16[128,128]{1,0:T(8,128)(2,1)S(1)}, bf16[128,128]{1,0:T(8,128)(2,1)S(1)}, u32[]{:S(2)}, u32[]{:S(2)}) collective-permute-start(bf16[128,128]{1,0:T(8,128)(2,1)S(1)} %shard_map.38), channel_id=1, source_target_pairs={{2,0},{0,2},{3,1},{1,3},{6,4},{4,6},{7,5},{5,7},{10,8},{8,10},{11,... | collective-permute-start | bytes 98312 | tf_op jit(solution)/shard_map/ppermute | solution.py:36
  4.8 0.0 copy-done.1
  4.8 2.8 %shard_map.39 = (f32[15,64,128]{2,1,0:T(8,128)S(1)}, f32[128,128]{1,0:T(8,128)S(1)}) custom-call(bf16[64,2048]{1,0:T(8,128)(2,1)S(1)} %shard_map.37.whole.refs_0_, bf16[64,2048]{1,0:T(8,128)(2,1)S(1)} %collective-permute-done.other.refs_1_, s32[9,512]{1,0:T(8,128)S(1)} %copy-done.1), custom_call_target="tpu_custom_call" | custom-call | tf_op jit(solution)/shard_map/pallas_call | solution.py:445
  7.5 0.0 collective-permute-done.1.refs_2_
  7.5 0.6 %shard_map.40 = (bf16[16,16,128]{2,1,0:T(8,128)(2,1)S(1)}, bf16[16,16,128]{2,1,0:T(8,128)(2,1)S(1)}, bf16[16,16,128]{2,1,0:T(8,128)(2,1)S(1)}, bf16[16,16,128]{2,1,0:T(8,128)(2,1)S(1)}) custom-call(bf16[64,2048]{1,0:T(8,128)(2,1)S(1)} %shard_map.37.whole.refs_0_, bf16[64,2048]{1,0:T(8,128)(2,1)S(1)} %collective-permute-done.other.refs_1_, ...), custom_call_target="tpu_custom_call" | custom-call | tf_op jit(solution)/shard_map/pallas_call | solution.py:445
  8.2 3.7 %collective-permute-start.3 = (bf16[16,16,128]{2,1,0:T(8,128)(2,1)S(1)}, bf16[16,16,128]{2,1,0:T(8,128)(2,1)S(1)}, u32[]{:S(2)}, u32[]{:S(2)}) collective-permute-start(bf16[16,16,128]{2,1,0:T(8,128)(2,1)S(1)} %get-tuple-element.32), channel_id=1, source_target_pairs={{0,12},{1,9},{4,8},{5,13},{8,4},{9,1},{12,0},{13,5},{2,14},{3,11},... | collective-permute-start | bytes 196616 | tf_op jit(solution)/shard_map/ppermute | solution.py:61
  11.8 0.0 collective-permute-start.4
  11.8 0.8 %collective-permute-start.2 = (bf16[16,16,128]{2,1,0:T(8,128)(2,1)S(1)}, bf16[16,16,128]{2,1,0:T(8,128)(2,1)S(1)}, u32[]{:S(2)}, u32[]{:S(2)}) collective-permute-start(bf16[16,16,128]{2,1,0:T(8,128)(2,1)S(1)} %get-tuple-element.28), channel_id=1, source_target_pairs={{0,8},{1,5},{4,12},{5,1},{8,0},{9,13},{12,4},{13,9},{2,10},{3,7},{... | collective-permute-start | bytes 196616 | tf_op jit(solution)/shard_map/ppermute | solution.py:61
  12.6 0.0 copy-start.2
  12.6 1.8 %collective-permute-done.3.refs_1_ = bf16[16,16,128]{2,1,0:T(8,128)(2,1)S(1)} collective-permute-done((bf16[16,16,128]{2,1,0:T(8,128)(2,1)S(1)}, bf16[16,16,128]{2,1,0:T(8,128)(2,1)S(1)}, u32[]{:S(2)}, u32[]{:S(2)}) %collective-permute-start.3) | collective-permute-done | bytes 65568 | tf_op jit(solution)/shard_map/ppermute | solution.py:61
  14.5 2.8 %collective-permute-done.4.refs_2_ = bf16[16,16,128]{2,1,0:T(8,128)(2,1)S(1)} collective-permute-done((bf16[16,16,128]{2,1,0:T(8,128)(2,1)S(1)}, bf16[16,16,128]{2,1,0:T(8,128)(2,1)S(1)}, u32[]{:S(2)}, u32[]{:S(2)}) %collective-permute-start.4) | collective-permute-done | bytes 65568 | tf_op jit(solution)/shard_map/ppermute | solution.py:61
  17.2 0.3 %collective-permute-start.5 = (bf16[5,48,128]{2,1,0:T(8,128)(2,1)S(1)}, bf16[5,48,128]{2,1,0:T(8,128)(2,1)S(1)}, u32[]{:S(2)}, u32[]{:S(2)}) collective-permute-start(bf16[5,48,128]{2,1,0:T(8,128)(2,1)S(1)} %shard_map.42), channel_id=1, source_target_pairs={{2,0},{0,2},{3,1},{1,3},{6,4},{4,6},{7,5},{5,7},{10,8},{8,10},{11,... | collective-permute-start | bytes 184328 | tf_op jit(solution)/shard_map/ppermute | solution.py:36
  17.5 0.0 copy-done.2
  17.5 0.2 shard_map.41
  17.7 0.0 collective-permute-done.2.refs_3_
  17.7 1.8 %collective-permute-start.6 = (bf16[5,16,128]{2,1,0:T(8,128)(2,1)S(1)}, bf16[5,16,128]{2,1,0:T(8,128)(2,1)S(1)}, u32[]{:S(2)}, u32[]{:S(2)}) collective-permute-start(bf16[5,16,128]{2,1,0:T(8,128)(2,1)S(1)} %slice.3), channel_id=1, source_target_pairs={{2,0},{0,2},{3,1},{1,3},{6,4},{4,6},{7,5},{5,7},{10,8},{8,10},{11,... | collective-permute-start | bytes 61448 | tf_op jit(solution)/shard_map/ppermute | solution.py:36
  19.6 1.5 %shard_map.43 = (f32[64,1408]{1,0:T(8,128)S(1)}, bf16[2,64,128]{2,1,0:T(8,128)(2,1)S(1)}) custom-call(f32[128,128]{1,0:T(8,128)S(1)} %get-tuple-element.29.columns, bf16[768,384]{1,0:T(8,128)(2,1)S(1)} %get-tuple-element.30.taps, bf16[16,16,128]{2,1,0:T(8,128)(2,1)S(1)} %get-tuple-element.31.refs_0_, ...), custom_call_target="tpu_custom_call" | custom-call | tf_op jit(solution)/shard_map/pallas_call | solution.py:470
  21.1 0.6 %collective-permute-done.6.refs_5_ = bf16[5,16,128]{2,1,0:T(8,128)(2,1)S(1)} collective-permute-done((bf16[5,16,128]{2,1,0:T(8,128)(2,1)S(1)}, bf16[5,16,128]{2,1,0:T(8,128)(2,1)S(1)}, u32[]{:S(2)}, u32[]{:S(2)}) %collective-permute-start.6) | collective-permute-done | bytes 20512 | tf_op jit(solution)/shard_map/ppermute | solution.py:36
  21.7 0.0 collective-permute-done.5.refs_4_
  21.7 1.6 %shard_map.44 = f32[64,2048]{1,0:T(8,128)} custom-call(f32[128,128]{1,0:T(8,128)S(1)} %get-tuple-element.29.columns, bf16[768,384]{1,0:T(8,128)(2,1)S(1)} %get-tuple-element.30.taps, bf16[16,16,128]{2,1,0:T(8,128)(2,1)S(1)} %get-tuple-element.31.refs_0_, bf16[16,16,128]{2,1,0:T(8,128)(2,1)S(1)} %collective-permute-done.3.refs_1_, ...), custom_call_target="tpu_custom_call" | custom-call | tf_op jit(solution)/shard_map/pallas_call | solution.py:470
  (5 shorter events, 0.0 us)
Async XLA Ops:
  0.0 1.8 %collective-permute-start = (bf16[64,2048]{1,0:T(8,128)(2,1)}, bf16[64,2048]{1,0:T(8,128)(2,1)S(1)}, u32[]{:S(2)}, u32[]{:S(2)}) collective-permute-start(bf16[64,2048]{1,0:T(8,128)(2,1)} %whole.1), channel_id=1, source_target_pairs={{0,1},{1,0},{2,3},{3,2},{4,5},{5,4},{6,7},{7,6},{8,9},{9,8},{10,11... | collective-permute-start | bytes 786440 | tf_op jit(solution)/shard_map/ppermute | solution.py:41
  0.5 0.9 %copy-start = (bf16[64,2048]{1,0:T(8,128)(2,1)S(1)}, bf16[64,2048]{1,0:T(8,128)(2,1)}, u32[]{:S(2)}) copy-start(bf16[64,2048]{1,0:T(8,128)(2,1)} %whole.1) | copy-start | bytes 786436
  1.4 3.3 %copy-start.1 = (s32[9,512]{1,0:T(8,128)S(1)}, s32[9,512]{1,0:T(8,128)}, u32[]{:S(2)}) copy-start(s32[9,512]{1,0:T(8,128)} %shifts) | copy-start | bytes 55300
  1.8 5.7 %collective-permute-start.1 = (bf16[128,128]{1,0:T(8,128)(2,1)S(1)}, bf16[128,128]{1,0:T(8,128)(2,1)S(1)}, u32[]{:S(2)}, u32[]{:S(2)}) collective-permute-start(bf16[128,128]{1,0:T(8,128)(2,1)S(1)} %shard_map.38), channel_id=1, source_target_pairs={{2,0},{0,2},{3,1},{1,3},{6,4},{4,6},{7,5},{5,7},{10,8},{8,10},{11,... | collective-permute-start | bytes 98312 | tf_op jit(solution)/shard_map/ppermute | solution.py:36
  8.2 6.3 %collective-permute-start.3 = (bf16[16,16,128]{2,1,0:T(8,128)(2,1)S(1)}, bf16[16,16,128]{2,1,0:T(8,128)(2,1)S(1)}, u32[]{:S(2)}, u32[]{:S(2)}) collective-permute-start(bf16[16,16,128]{2,1,0:T(8,128)(2,1)S(1)} %get-tuple-element.32), channel_id=1, source_target_pairs={{0,12},{1,9},{4,8},{5,13},{8,4},{9,1},{12,0},{13,5},{2,14},{3,11},... | collective-permute-start | bytes 196616 | tf_op jit(solution)/shard_map/ppermute | solution.py:61
  11.8 5.4 %collective-permute-start.4 = (bf16[16,16,128]{2,1,0:T(8,128)(2,1)S(1)}, bf16[16,16,128]{2,1,0:T(8,128)(2,1)S(1)}, u32[]{:S(2)}, u32[]{:S(2)}) collective-permute-start(bf16[16,16,128]{2,1,0:T(8,128)(2,1)S(1)} %get-tuple-element.33), channel_id=1, source_target_pairs={{0,4},{1,13},{4,0},{5,9},{8,12},{9,5},{12,8},{13,1},{2,6},{3,15},{... | collective-permute-start | bytes 196616 | tf_op jit(solution)/shard_map/ppermute | solution.py:61
  11.8 5.9 %collective-permute-start.2 = (bf16[16,16,128]{2,1,0:T(8,128)(2,1)S(1)}, bf16[16,16,128]{2,1,0:T(8,128)(2,1)S(1)}, u32[]{:S(2)}, u32[]{:S(2)}) collective-permute-start(bf16[16,16,128]{2,1,0:T(8,128)(2,1)S(1)} %get-tuple-element.28), channel_id=1, source_target_pairs={{0,8},{1,5},{4,12},{5,1},{8,0},{9,13},{12,4},{13,9},{2,10},{3,7},{... | collective-permute-start | bytes 196616 | tf_op jit(solution)/shard_map/ppermute | solution.py:61
  12.6 4.8 %copy-start.2 = (bf16[6,256]{1,0:T(8,128)(2,1)S(1)}, bf16[6,256]{1,0:T(8,128)(2,1)}, u32[]{:S(2)}) copy-start(bf16[6,256]{1,0:T(8,128)(2,1)} %filters) | copy-start | bytes 9220
  17.2 4.4 %collective-permute-start.5 = (bf16[5,48,128]{2,1,0:T(8,128)(2,1)S(1)}, bf16[5,48,128]{2,1,0:T(8,128)(2,1)S(1)}, u32[]{:S(2)}, u32[]{:S(2)}) collective-permute-start(bf16[5,48,128]{2,1,0:T(8,128)(2,1)S(1)} %shard_map.42), channel_id=1, source_target_pairs={{2,0},{0,2},{3,1},{1,3},{6,4},{4,6},{7,5},{5,7},{10,8},{8,10},{11,... | collective-permute-start | bytes 184328 | tf_op jit(solution)/shard_map/ppermute | solution.py:36
  17.7 3.9 %collective-permute-start.6 = (bf16[5,16,128]{2,1,0:T(8,128)(2,1)S(1)}, bf16[5,16,128]{2,1,0:T(8,128)(2,1)S(1)}, u32[]{:S(2)}, u32[]{:S(2)}) collective-permute-start(bf16[5,16,128]{2,1,0:T(8,128)(2,1)S(1)} %slice.3), channel_id=1, source_target_pairs={{2,0},{0,2},{3,1},{1,3},{6,4},{4,6},{7,5},{5,7},{10,8},{8,10},{11,... | collective-permute-start | bytes 61448 | tf_op jit(solution)/shard_map/ppermute | solution.py:36

commit v12 on v9

--- a/solution.py
+++ b/solution.py
@@ -43,7 +43,7 @@
 
 def mask_orders(group_count):
     far = list(range(group_count - 1, 1, -1))
-    return [1, *far], far[-1:] + far[:-1] + [1]
+    return [*far[:-1], 1, *far[-1:]], [*far[-1:], *far[:-1], 1]
 
 
 def step_masks(group_count, core):
@@ -320,7 +320,7 @@
 
 def trial_kernel(plan, group_count, level_count, scale, columns, taps, *refs):
     blocks, refs = refs[: len(plan.pieces)], refs[len(plan.pieces) :]
-    halos, refs = refs[: len(plan.halos)], refs[len(plan.halos) :]
+    halos, refs = refs[: 2 * len(plan.halos)], refs[2 * len(plan.halos) :]
     if plan.taken:
         carried, so_far, refs = refs[0], refs[1], refs[2:]
     out, refs = refs[0], refs[1:]
@@ -347,10 +347,15 @@
     for hop, tiles in enumerate(plan.halos, 1):
         there = lax.axis_index("tm") + hop < lax.axis_size("tm")
         for tile in range(tiles):
-            joined = jnp.where(there, halos[hop - 1][tile, :, :].astype(jnp.float32), 0.0)
-            for index, mask in enumerate(step_masks(group_count, core)):
+            joined = [
+                jnp.where(there, halo[tile, :, :].astype(jnp.float32), 0.0)
+                for halo in halos[2 * hop - 2 : 2 * hop]
+            ]
+            parts = [
+                value[row : row + block_rows] for value in joined for row in range(0, value.shape[0], block_rows)
+            ]
+            for part, mask in zip(parts, step_masks(group_count, core)):
                 start = pl.multiple_of((chip ^ mask) * block_rows, block_rows)
-                part = joined[index * block_rows : (index + 1) * block_rows]
                 state[at, pl.ds(start, block_rows), :] = part
             at += 1
     for tile in range(at, at + plan.empty_tiles):
@@ -525,7 +530,7 @@
         compiler_params=params,
     )(late_shifts, late_filters)
     first_tiles = min(time_tiles, far_tiles) if lax.axis_size("tm") > 1 else 0
-    *arrived, (step, first, last) = exchanged(main, first_tiles)
+    *arrived, (step, first, last) = exchanged(main, max(first_tiles, time_tiles // 2 + 1))
     columns, taps, last = lax.optimization_barrier((columns, taps, last))
     arrived.append((step, first, last))
     pieces = [(step, first) for step, first, _ in arrived]
@@ -535,18 +540,23 @@
     rest = far_tiles
     if lax.axis_size("tm") > 1:
         heads = [block for _, first, block in arrived if first == 0]
-        joined = pl.pallas_call(
-            join_kernel,
-            out_shape=jax.ShapeDtypeStruct((first_tiles, chan_rows, LANES), jnp.bfloat16),
-            in_specs=[in_vmem] * len(heads),
-            out_specs=in_vmem,
-            scratch_shapes=[pltpu.VMEM((first_tiles, chan_rows, LANES), jnp.float32)],
-            compiler_params=params,
-        )(*heads)
+        joined = []
+        for some in (heads[:-2], heads[-2:]):
+            shape = (first_tiles, len(some) * block_rows, LANES)
+            joined.append(
+                pl.pallas_call(
+                    join_kernel,
+                    out_shape=jax.ShapeDtypeStruct(shape, jnp.bfloat16),
+                    in_specs=[in_vmem] * len(some),
+                    out_specs=in_vmem,
+                    scratch_shapes=[pltpu.VMEM(shape, jnp.float32)],
+                    compiler_params=params,
+                )(*some)
+            )
         for hop in range(1, lax.axis_size("tm")):
             if rest > 0:
                 takes.append(min(time_tiles, rest))
-                halos.append(from_ahead(joined[: takes[-1]], hop))
+                halos += [from_ahead(rows_now[: takes[-1]], hop) for rows_now in joined]
                 rest -= takes[-1]
     lost = -(-sum(2**level for level in far_levels) // LANES) + tap_tiles
     early_tiles = time_tiles - lost

time: 23.4 us -> 22.6 us (0.966)
  waiting for transfers between devices: 3.93 us -> 2.54 us
  starting transfers between devices: 11.6 us -> 12.2 us
    ppermute x4, waiting for transfers between devices: 1.98 us -> 0.92 us  [exchanged(): lax.ppermute(blocks[step][first:end], ('freq', 'sub'), route)]
    ppermute x2 -> x3, starting transfers between devices: 4.12 us -> 5.14 us  [from_ahead(): lax.ppermute(value, 'tm', [((block + steps) % count, block) for block in...]
    ppermute x4, starting transfers between devices: 7.04 us -> 6.59 us  [exchanged(): lax.ppermute(blocks[step][first:end], ('freq', 'sub'), route)]
    ppermute x2 -> x3, waiting for transfers between devices: 1.57 us -> 1.24 us  [from_ahead(): lax.ppermute(value, 'tm', [((block + steps) % count, block) for block in...]
  transfers between devices with their start and end apart: 7 -> 8, of which waited for: 3 -> 4; matrix products, arithmetic and copies ran while one was open for 0% -> 0% of each run, Pallas kernels for 19% -> 20%
where the time goes in v12:
time: 22.6 us; the launch traced here: 22.5 us
  starting transfers between devices  12.2 us (54%)
  Pallas kernels  6.69 us (30%)
  waiting for transfers between devices  2.54 us (11%)
  local copies, waits for them, and re-layouts  0.97 us (4%)
    ppermute x4, starting transfers between devices, exchanged(): lax.ppermute(blocks[step][first:end], ('freq', 'sub'), route)  6.59 us
    ppermute x3, starting transfers between devices, from_ahead(): lax.ppermute(value, 'tm', [((block + steps) % count, block) for block in...  5.14 us
    pallas_call x2, Pallas kernels, within_chip(): pl.pallas_call(functools.partial(chip_kernel, spans, out_tiles, group_cou...  3.38 us
    pallas_call x2, Pallas kernels, between_chips(): pl.pallas_call(functools.partial(trial_kernel, plan, group_count, level_c...  3.05 us
    ppermute x3, waiting for transfers between devices, from_ahead(): lax.ppermute(value, 'tm', [((block + steps) % count, block) for block in...  1.24 us
    unnamed x6, local copies, waits for them, and re-layouts  0.96 us
    ppermute x4, waiting for transfers between devices, exchanged(): lax.ppermute(blocks[step][first:end], ('freq', 'sub'), route)  0.92 us
    ppermute x1, starting transfers between devices, from_partner(): lax.ppermute(value, axis, [(source, source ^ mask) for source in range(co...  0.45 us
  transfers between devices with their start and end apart: 8, of which 4 were waited for; matrix products, arithmetic and copies ran while one was open for 0% of the time, Pallas kernels for 20%

profile of v12, /device:TPU:0, one launch (start us, length us, event | category | flops | bytes accessed | tf_op | source)
XLA Modules:
  0.0 22.5 jit_solution(15131914906557597506)
XLA Ops:
  0.0 0.5 %collective-permute-start = (bf16[64,2048]{1,0:T(8,128)(2,1)}, bf16[64,2048]{1,0:T(8,128)(2,1)S(1)}, u32[]{:S(2)}, u32[]{:S(2)}) collective-permute-start(bf16[64,2048]{1,0:T(8,128)(2,1)} %whole.1), channel_id=1, source_target_pairs={{0,1},{1,0},{2,3},{3,2},{4,5},{5,4},{6,7},{7,6},{8,9},{9,8},{10,11... | collective-permute-start | bytes 786440 | tf_op jit(solution)/shard_map/ppermute | solution.py:41
  0.5 0.9 %copy-done = bf16[64,2048]{1,0:T(8,128)(2,1)S(1)} copy-done((bf16[64,2048]{1,0:T(8,128)(2,1)S(1)}, bf16[64,2048]{1,0:T(8,128)(2,1)}, u32[]{:S(2)}) %copy-start) | copy-done | bytes 262168
  1.4 0.0 copy-start.1
  1.4 0.4 %collective-permute-done.other.refs_1_ = bf16[64,2048]{1,0:T(8,128)(2,1)S(1)} collective-permute-done((bf16[64,2048]{1,0:T(8,128)(2,1)}, bf16[64,2048]{1,0:T(8,128)(2,1)S(1)}, u32[]{:S(2)}, u32[]{:S(2)}) %collective-permute-start) | collective-permute-done | bytes 262176 | tf_op jit(solution)/shard_map/ppermute | solution.py:41
  1.8 2.9 %collective-permute-start.1 = (bf16[128,128]{1,0:T(8,128)(2,1)S(1)}, bf16[128,128]{1,0:T(8,128)(2,1)S(1)}, u32[]{:S(2)}, u32[]{:S(2)}) collective-permute-start(bf16[128,128]{1,0:T(8,128)(2,1)S(1)} %shard_map.38), channel_id=1, source_target_pairs={{2,0},{0,2},{3,1},{1,3},{6,4},{4,6},{7,5},{5,7},{10,8},{8,10},{11,... | collective-permute-start | bytes 98312 | tf_op jit(solution)/shard_map/ppermute | solution.py:36
  4.8 0.0 copy-done.1
  4.8 2.8 %shard_map.39 = (f32[15,64,128]{2,1,0:T(8,128)S(1)}, f32[128,128]{1,0:T(8,128)S(1)}) custom-call(bf16[64,2048]{1,0:T(8,128)(2,1)S(1)} %shard_map.37.whole.refs_0_, bf16[64,2048]{1,0:T(8,128)(2,1)S(1)} %collective-permute-done.other.refs_1_, s32[9,512]{1,0:T(8,128)S(1)} %copy-done.1), custom_call_target="tpu_custom_call" | custom-call | tf_op jit(solution)/shard_map/pallas_call | solution.py:450
  7.5 0.0 collective-permute-done.1.refs_2_
  7.5 0.6 %shard_map.40 = (bf16[16,16,128]{2,1,0:T(8,128)(2,1)S(1)}, bf16[16,16,128]{2,1,0:T(8,128)(2,1)S(1)}, bf16[16,16,128]{2,1,0:T(8,128)(2,1)S(1)}, bf16[16,16,128]{2,1,0:T(8,128)(2,1)S(1)}) custom-call(bf16[64,2048]{1,0:T(8,128)(2,1)S(1)} %shard_map.37.whole.refs_0_, bf16[64,2048]{1,0:T(8,128)(2,1)S(1)} %collective-permute-done.other.refs_1_, ...), custom_call_target="tpu_custom_call" | custom-call | tf_op jit(solution)/shard_map/pallas_call | solution.py:450
  8.2 3.7 %collective-permute-start.3 = (bf16[16,16,128]{2,1,0:T(8,128)(2,1)S(1)}, bf16[16,16,128]{2,1,0:T(8,128)(2,1)S(1)}, u32[]{:S(2)}, u32[]{:S(2)}) collective-permute-start(bf16[16,16,128]{2,1,0:T(8,128)(2,1)S(1)} %get-tuple-element.32), channel_id=1, source_target_pairs={{0,12},{1,9},{4,8},{5,13},{8,4},{9,1},{12,0},{13,5},{2,14},{3,11},... | collective-permute-start | bytes 196616 | tf_op jit(solution)/shard_map/ppermute | solution.py:64
  11.8 0.0 collective-permute-start.4
  11.8 0.8 %collective-permute-start.5 = (bf16[9,16,128]{2,1,0:T(8,128)(2,1)S(1)}, bf16[9,16,128]{2,1,0:T(8,128)(2,1)S(1)}, u32[]{:S(2)}, u32[]{:S(2)}) collective-permute-start(bf16[9,16,128]{2,1,0:T(8,128)(2,1)S(1)} %slice.7), channel_id=1, source_target_pairs={{0,8},{1,5},{4,12},{5,1},{8,0},{9,13},{12,4},{13,9},{2,10},{3,7},{... | collective-permute-start | bytes 110600 | tf_op jit(solution)/shard_map/ppermute | solution.py:64
  12.6 2.1 %collective-permute-start.2 = (bf16[7,16,128]{2,1,0:T(8,128)(2,1)S(1)}, bf16[7,16,128]{2,1,0:T(8,128)(2,1)S(1)}, u32[]{:S(2)}, u32[]{:S(2)}) collective-permute-start(bf16[7,16,128]{2,1,0:T(8,128)(2,1)S(1)} %slice.6), channel_id=1, source_target_pairs={{0,8},{1,5},{4,12},{5,1},{8,0},{9,13},{12,4},{13,9},{2,10},{3,7},{... | collective-permute-start | bytes 86024 | tf_op jit(solution)/shard_map/ppermute | solution.py:64
  14.8 0.0 collective-permute-done.3.refs_1_
  14.8 1.2 %collective-permute-start.6 = (bf16[5,32,128]{2,1,0:T(8,128)(2,1)S(1)}, bf16[5,32,128]{2,1,0:T(8,128)(2,1)S(1)}, u32[]{:S(2)}, u32[]{:S(2)}) collective-permute-start(bf16[5,32,128]{2,1,0:T(8,128)(2,1)S(1)} %shard_map.42), channel_id=1, source_target_pairs={{2,0},{0,2},{3,1},{1,3},{6,4},{4,6},{7,5},{5,7},{10,8},{8,10},{11,... | collective-permute-start | bytes 122888 | tf_op jit(solution)/shard_map/ppermute | solution.py:36
  16.0 0.8 %collective-permute-done.5.refs_1_.refs_3_ = bf16[9,16,128]{2,1,0:T(8,128)(2,1)S(1)} collective-permute-done((bf16[9,16,128]{2,1,0:T(8,128)(2,1)S(1)}, bf16[9,16,128]{2,1,0:T(8,128)(2,1)S(1)}, u32[]{:S(2)}, u32[]{:S(2)}) %collective-permute-start.5) | collective-permute-done | bytes 36896 | tf_op jit(solution)/shard_map/ppermute | solution.py:64
  16.8 0.1 collective-permute-done.4.refs_0_.refs_2_
  16.9 1.0 %collective-permute-start.7 = (bf16[5,32,128]{2,1,0:T(8,128)(2,1)S(1)}, bf16[5,32,128]{2,1,0:T(8,128)(2,1)S(1)}, u32[]{:S(2)}, u32[]{:S(2)}) collective-permute-start(bf16[5,32,128]{2,1,0:T(8,128)(2,1)S(1)} %shard_map.43), channel_id=1, source_target_pairs={{2,0},{0,2},{3,1},{1,3},{6,4},{4,6},{7,5},{5,7},{10,8},{8,10},{11,... | collective-permute-start | bytes 122888 | tf_op jit(solution)/shard_map/ppermute | solution.py:36
  17.9 0.2 shard_map.41
  18.2 0.0 collective-permute-done.2.refs_4_
  18.2 1.5 %shard_map.44 = (f32[64,1408]{1,0:T(8,128)S(1)}, bf16[2,64,128]{2,1,0:T(8,128)(2,1)S(1)}) custom-call(f32[128,128]{1,0:T(8,128)S(1)} %get-tuple-element.29.columns, bf16[768,384]{1,0:T(8,128)(2,1)S(1)} %get-tuple-element.30.taps, bf16[16,16,128]{2,1,0:T(8,128)(2,1)S(1)} %get-tuple-element.31.refs_0_, ...), custom_call_target="tpu_custom_call" | custom-call | flops 415236096 | bytes 21626880 | tf_op jit(solution)/shard_map/pallas_call | solution.py:475
  19.7 0.0 collective-permute-done.6.refs_5_
  19.7 1.2 %collective-permute-done.7.refs_6_ = bf16[5,32,128]{2,1,0:T(8,128)(2,1)S(1)} collective-permute-done((bf16[5,32,128]{2,1,0:T(8,128)(2,1)S(1)}, bf16[5,32,128]{2,1,0:T(8,128)(2,1)S(1)}, u32[]{:S(2)}, u32[]{:S(2)}) %collective-permute-start.7) | collective-permute-done | bytes 40992 | tf_op jit(solution)/shard_map/ppermute | solution.py:36
  20.9 1.6 %shard_map.45 = f32[64,2048]{1,0:T(8,128)} custom-call(f32[128,128]{1,0:T(8,128)S(1)} %get-tuple-element.29.columns, bf16[768,384]{1,0:T(8,128)(2,1)S(1)} %get-tuple-element.30.taps, bf16[16,16,128]{2,1,0:T(8,128)(2,1)S(1)} %get-tuple-element.31.refs_0_, bf16[16,16,128]{2,1,0:T(8,128)(2,1)S(1)} %collective-permute-done.3.refs_1_, ...), custom_call_target="tpu_custom_call" | custom-call | flops 188743680 | bytes 9830400 | tf_op jit(solution)/shard_map/pallas_call | solution.py:475
  (9 shorter events, 0.0 us)
Async XLA Ops:
  0.0 1.8 %collective-permute-start = (bf16[64,2048]{1,0:T(8,128)(2,1)}, bf16[64,2048]{1,0:T(8,128)(2,1)S(1)}, u32[]{:S(2)}, u32[]{:S(2)}) collective-permute-start(bf16[64,2048]{1,0:T(8,128)(2,1)} %whole.1), channel_id=1, source_target_pairs={{0,1},{1,0},{2,3},{3,2},{4,5},{5,4},{6,7},{7,6},{8,9},{9,8},{10,11... | collective-permute-start | bytes 786440 | tf_op jit(solution)/shard_map/ppermute | solution.py:41
  0.5 0.9 %copy-start = (bf16[64,2048]{1,0:T(8,128)(2,1)S(1)}, bf16[64,2048]{1,0:T(8,128)(2,1)}, u32[]{:S(2)}) copy-start(bf16[64,2048]{1,0:T(8,128)(2,1)} %whole.1) | copy-start | bytes 786436
  1.4 3.3 %copy-start.1 = (s32[9,512]{1,0:T(8,128)S(1)}, s32[9,512]{1,0:T(8,128)}, u32[]{:S(2)}) copy-start(s32[9,512]{1,0:T(8,128)} %shifts) | copy-start | bytes 55300
  1.8 5.7 %collective-permute-start.1 = (bf16[128,128]{1,0:T(8,128)(2,1)S(1)}, bf16[128,128]{1,0:T(8,128)(2,1)S(1)}, u32[]{:S(2)}, u32[]{:S(2)}) collective-permute-start(bf16[128,128]{1,0:T(8,128)(2,1)S(1)} %shard_map.38), channel_id=1, source_target_pairs={{2,0},{0,2},{3,1},{1,3},{6,4},{4,6},{7,5},{5,7},{10,8},{8,10},{11,... | collective-permute-start | bytes 98312 | tf_op jit(solution)/shard_map/ppermute | solution.py:36
  8.2 6.6 %collective-permute-start.3 = (bf16[16,16,128]{2,1,0:T(8,128)(2,1)S(1)}, bf16[16,16,128]{2,1,0:T(8,128)(2,1)S(1)}, u32[]{:S(2)}, u32[]{:S(2)}) collective-permute-start(bf16[16,16,128]{2,1,0:T(8,128)(2,1)S(1)} %get-tuple-element.32), channel_id=1, source_target_pairs={{0,12},{1,9},{4,8},{5,13},{8,4},{9,1},{12,0},{13,5},{2,14},{3,11},... | collective-permute-start | bytes 196616 | tf_op jit(solution)/shard_map/ppermute | solution.py:64
  11.8 5.1 %collective-permute-start.4 = (bf16[16,16,128]{2,1,0:T(8,128)(2,1)S(1)}, bf16[16,16,128]{2,1,0:T(8,128)(2,1)S(1)}, u32[]{:S(2)}, u32[]{:S(2)}) collective-permute-start(bf16[16,16,128]{2,1,0:T(8,128)(2,1)S(1)} %get-tuple-element.33), channel_id=1, source_target_pairs={{0,4},{1,13},{4,0},{5,9},{8,12},{9,5},{12,8},{13,1},{2,6},{3,15},{... | collective-permute-start | bytes 196616 | tf_op jit(solution)/shard_map/ppermute | solution.py:64
  11.8 5.0 %collective-permute-start.5 = (bf16[9,16,128]{2,1,0:T(8,128)(2,1)S(1)}, bf16[9,16,128]{2,1,0:T(8,128)(2,1)S(1)}, u32[]{:S(2)}, u32[]{:S(2)}) collective-permute-start(bf16[9,16,128]{2,1,0:T(8,128)(2,1)S(1)} %slice.7), channel_id=1, source_target_pairs={{0,8},{1,5},{4,12},{5,1},{8,0},{9,13},{12,4},{13,9},{2,10},{3,7},{... | collective-permute-start | bytes 110600 | tf_op jit(solution)/shard_map/ppermute | solution.py:64
  12.6 5.5 %collective-permute-start.2 = (bf16[7,16,128]{2,1,0:T(8,128)(2,1)S(1)}, bf16[7,16,128]{2,1,0:T(8,128)(2,1)S(1)}, u32[]{:S(2)}, u32[]{:S(2)}) collective-permute-start(bf16[7,16,128]{2,1,0:T(8,128)(2,1)S(1)} %slice.6), channel_id=1, source_target_pairs={{0,8},{1,5},{4,12},{5,1},{8,0},{9,13},{12,4},{13,9},{2,10},{3,7},{... | collective-permute-start | bytes 86024 | tf_op jit(solution)/shard_map/ppermute | solution.py:64
  14.8 3.1 %copy-start.2 = (bf16[6,256]{1,0:T(8,128)(2,1)S(1)}, bf16[6,256]{1,0:T(8,128)(2,1)}, u32[]{:S(2)}) copy-start(bf16[6,256]{1,0:T(8,128)(2,1)} %filters) | copy-start | bytes 9220
  14.8 4.9 %collective-permute-start.6 = (bf16[5,32,128]{2,1,0:T(8,128)(2,1)S(1)}, bf16[5,32,128]{2,1,0:T(8,128)(2,1)S(1)}, u32[]{:S(2)}, u32[]{:S(2)}) collective-permute-start(bf16[5,32,128]{2,1,0:T(8,128)(2,1)S(1)} %shard_map.42), channel_id=1, source_target_pairs={{2,0},{0,2},{3,1},{1,3},{6,4},{4,6},{7,5},{5,7},{10,8},{8,10},{11,... | collective-permute-start | bytes 122888 | tf_op jit(solution)/shard_map/ppermute | solution.py:36
  16.9 4.0 %collective-permute-start.7 = (bf16[5,32,128]{2,1,0:T(8,128)(2,1)S(1)}, bf16[5,32,128]{2,1,0:T(8,128)(2,1)S(1)}, u32[]{:S(2)}, u32[]{:S(2)}) collective-permute-start(bf16[5,32,128]{2,1,0:T(8,128)(2,1)S(1)} %shard_map.43), channel_id=1, source_target_pairs={{2,0},{0,2},{3,1},{1,3},{6,4},{4,6},{7,5},{5,7},{10,8},{8,10},{11,... | collective-permute-start | bytes 122888 | tf_op jit(solution)/shard_map/ppermute | solution.py:36

commit v13 on v12

--- a/solution.py
+++ b/solution.py
@@ -530,9 +530,10 @@
         compiler_params=params,
     )(late_shifts, late_filters)
     first_tiles = min(time_tiles, far_tiles) if lax.axis_size("tm") > 1 else 0
-    *arrived, (step, first, last) = exchanged(main, max(first_tiles, time_tiles // 2 + 1))
-    columns, taps, last = lax.optimization_barrier((columns, taps, last))
-    arrived.append((step, first, last))
+    arrived = exchanged(main, max(first_tiles, time_tiles // 2 + 1))
+    step, first, block = arrived[2]
+    columns, taps, block = lax.optimization_barrier((columns, taps, block))
+    arrived[2] = (step, first, block)
     pieces = [(step, first) for step, first, _ in arrived]
     main = [block for _, _, block in arrived]
 

time: 22.6 us -> 22.7 us (level)
    ppermute x3, waiting for transfers between devices: 1.24 us -> 1.61 us  [from_ahead(): lax.ppermute(value, 'tm', [((block + steps) % count, block) for block in...]
    ppermute x4, waiting for transfers between devices: 0.92 us -> 0.66 us  [exchanged(): lax.ppermute(blocks[step][first:end], ('freq', 'sub'), route)]
  transfers between devices with their start and end apart: 8 -> 8, of which waited for: 4 -> 3; matrix products, arithmetic and copies ran while one was open for 0% -> 0% of each run, Pallas kernels for 20% -> 20%
where the time goes in v13:
time: 22.7 us; the launch traced here: 22.5 us
  starting transfers between devices  12.1 us (53%)
  Pallas kernels  6.69 us (29%)
  waiting for transfers between devices  2.65 us (12%)
  local copies, waits for them, and re-layouts  0.97 us (4%)
    ppermute x4, starting transfers between devices, exchanged(): lax.ppermute(blocks[step][first:end], ('freq', 'sub'), route)  6.59 us
    ppermute x3, starting transfers between devices, from_ahead(): lax.ppermute(value, 'tm', [((block + steps) % count, block) for block in...  5.09 us
    pallas_call x2, Pallas kernels, within_chip(): pl.pallas_call(functools.partial(chip_kernel, spans, out_tiles, group_cou...  3.38 us
    pallas_call x2, Pallas kernels, between_chips(): pl.pallas_call(functools.partial(trial_kernel, plan, group_count, level_c...  3.05 us
    ppermute x3, waiting for transfers between devices, from_ahead(): lax.ppermute(value, 'tm', [((block + steps) % count, block) for block in...  1.61 us
    unnamed x6, local copies, waits for them, and re-layouts  0.96 us
    ppermute x4, waiting for transfers between devices, exchanged(): lax.ppermute(blocks[step][first:end], ('freq', 'sub'), route)  0.66 us
  transfers between devices with their start and end apart: 8, of which 3 were waited for; matrix products, arithmetic and copies ran while one was open for 0% of the time, Pallas kernels for 20%

profile of v13, /device:TPU:0, one launch (start us, length us, event | category | flops | bytes accessed | tf_op | source)
XLA Modules:
  0.0 22.5 jit_solution(367837184268051725)
XLA Ops:
  0.0 0.5 %collective-permute-start = (bf16[64,2048]{1,0:T(8,128)(2,1)}, bf16[64,2048]{1,0:T(8,128)(2,1)S(1)}, u32[]{:S(2)}, u32[]{:S(2)}) collective-permute-start(bf16[64,2048]{1,0:T(8,128)(2,1)} %whole.1), channel_id=1, source_target_pairs={{0,1},{1,0},{2,3},{3,2},{4,5},{5,4},{6,7},{7,6},{8,9},{9,8},{10,11... | collective-permute-start | bytes 786440 | tf_op jit(solution)/shard_map/ppermute | solution.py:41
  0.5 0.9 %copy-done = bf16[64,2048]{1,0:T(8,128)(2,1)S(1)} copy-done((bf16[64,2048]{1,0:T(8,128)(2,1)S(1)}, bf16[64,2048]{1,0:T(8,128)(2,1)}, u32[]{:S(2)}) %copy-start) | copy-done | bytes 262168
  1.4 0.0 copy-start.1
  1.4 0.4 %collective-permute-done.other.refs_1_ = bf16[64,2048]{1,0:T(8,128)(2,1)S(1)} collective-permute-done((bf16[64,2048]{1,0:T(8,128)(2,1)}, bf16[64,2048]{1,0:T(8,128)(2,1)S(1)}, u32[]{:S(2)}, u32[]{:S(2)}) %collective-permute-start) | collective-permute-done | bytes 262176 | tf_op jit(solution)/shard_map/ppermute | solution.py:41
  1.8 2.9 %collective-permute-start.1 = (bf16[128,128]{1,0:T(8,128)(2,1)S(1)}, bf16[128,128]{1,0:T(8,128)(2,1)S(1)}, u32[]{:S(2)}, u32[]{:S(2)}) collective-permute-start(bf16[128,128]{1,0:T(8,128)(2,1)S(1)} %shard_map.38), channel_id=1, source_target_pairs={{2,0},{0,2},{3,1},{1,3},{6,4},{4,6},{7,5},{5,7},{10,8},{8,10},{11,... | collective-permute-start | bytes 98312 | tf_op jit(solution)/shard_map/ppermute | solution.py:36
  4.8 0.0 copy-done.1
  4.8 2.8 %shard_map.39 = (f32[15,64,128]{2,1,0:T(8,128)S(1)}, f32[128,128]{1,0:T(8,128)S(1)}) custom-call(bf16[64,2048]{1,0:T(8,128)(2,1)S(1)} %shard_map.37.whole.refs_0_, bf16[64,2048]{1,0:T(8,128)(2,1)S(1)} %collective-permute-done.other.refs_1_, s32[9,512]{1,0:T(8,128)S(1)} %copy-done.1), custom_call_target="tpu_custom_call" | custom-call | tf_op jit(solution)/shard_map/pallas_call | solution.py:450
  7.5 0.0 collective-permute-done.1.refs_2_
  7.5 0.6 %shard_map.40 = (bf16[16,16,128]{2,1,0:T(8,128)(2,1)S(1)}, bf16[16,16,128]{2,1,0:T(8,128)(2,1)S(1)}, bf16[16,16,128]{2,1,0:T(8,128)(2,1)S(1)}, bf16[16,16,128]{2,1,0:T(8,128)(2,1)S(1)}) custom-call(bf16[64,2048]{1,0:T(8,128)(2,1)S(1)} %shard_map.37.whole.refs_0_, bf16[64,2048]{1,0:T(8,128)(2,1)S(1)} %collective-permute-done.other.refs_1_, ...), custom_call_target="tpu_custom_call" | custom-call | tf_op jit(solution)/shard_map/pallas_call | solution.py:450
  8.2 3.7 %collective-permute-start.3 = (bf16[16,16,128]{2,1,0:T(8,128)(2,1)S(1)}, bf16[16,16,128]{2,1,0:T(8,128)(2,1)S(1)}, u32[]{:S(2)}, u32[]{:S(2)}) collective-permute-start(bf16[16,16,128]{2,1,0:T(8,128)(2,1)S(1)} %get-tuple-element.32), channel_id=1, source_target_pairs={{0,12},{1,9},{4,8},{5,13},{8,4},{9,1},{12,0},{13,5},{2,14},{3,11},... | collective-permute-start | bytes 196616 | tf_op jit(solution)/shard_map/ppermute | solution.py:64
  11.8 0.0 collective-permute-start.2
  11.8 0.8 %collective-permute-start.4 = (bf16[9,16,128]{2,1,0:T(8,128)(2,1)S(1)}, bf16[9,16,128]{2,1,0:T(8,128)(2,1)S(1)}, u32[]{:S(2)}, u32[]{:S(2)}) collective-permute-start(bf16[9,16,128]{2,1,0:T(8,128)(2,1)S(1)} %slice.6), channel_id=1, source_target_pairs={{0,8},{1,5},{4,12},{5,1},{8,0},{9,13},{12,4},{13,9},{2,10},{3,7},{... | collective-permute-start | bytes 110600 | tf_op jit(solution)/shard_map/ppermute | solution.py:64
  12.6 2.1 %collective-permute-start.5 = (bf16[7,16,128]{2,1,0:T(8,128)(2,1)S(1)}, bf16[7,16,128]{2,1,0:T(8,128)(2,1)S(1)}, u32[]{:S(2)}, u32[]{:S(2)}) collective-permute-start(bf16[7,16,128]{2,1,0:T(8,128)(2,1)S(1)} %slice.7), channel_id=1, source_target_pairs={{0,8},{1,5},{4,12},{5,1},{8,0},{9,13},{12,4},{13,9},{2,10},{3,7},{... | collective-permute-start | bytes 86024 | tf_op jit(solution)/shard_map/ppermute | solution.py:64
  14.8 0.2 shard_map.41
  15.0 0.0 collective-permute-done.3.refs_1_
  15.0 1.2 %collective-permute-start.6 = (bf16[5,32,128]{2,1,0:T(8,128)(2,1)S(1)}, bf16[5,32,128]{2,1,0:T(8,128)(2,1)S(1)}, u32[]{:S(2)}, u32[]{:S(2)}) collective-permute-start(bf16[5,32,128]{2,1,0:T(8,128)(2,1)S(1)} %shard_map.42), channel_id=1, source_target_pairs={{2,0},{0,2},{3,1},{1,3},{6,4},{4,6},{7,5},{5,7},{10,8},{8,10},{11,... | collective-permute-start | bytes 122888 | tf_op jit(solution)/shard_map/ppermute | solution.py:36
  16.2 0.7 %collective-permute-done.2.refs_0_.refs_2_ = bf16[16,16,128]{2,1,0:T(8,128)(2,1)S(1)} collective-permute-done((bf16[16,16,128]{2,1,0:T(8,128)(2,1)S(1)}, bf16[16,16,128]{2,1,0:T(8,128)(2,1)S(1)}, u32[]{:S(2)}, u32[]{:S(2)}) %collective-permute-start.2) | collective-permute-done | bytes 65568 | tf_op jit(solution)/shard_map/ppermute | solution.py:64
  16.9 0.0 collective-permute-done.4.refs_1_.refs_3_
  16.9 1.0 %collective-permute-start.7 = (bf16[5,32,128]{2,1,0:T(8,128)(2,1)S(1)}, bf16[5,32,128]{2,1,0:T(8,128)(2,1)S(1)}, u32[]{:S(2)}, u32[]{:S(2)}) collective-permute-start(bf16[5,32,128]{2,1,0:T(8,128)(2,1)S(1)} %shard_map.43), channel_id=1, source_target_pairs={{2,0},{0,2},{3,1},{1,3},{6,4},{4,6},{7,5},{5,7},{10,8},{8,10},{11,... | collective-permute-start | bytes 122888 | tf_op jit(solution)/shard_map/ppermute | solution.py:36
  17.9 0.0 collective-permute-done.5.refs_4_
  17.9 1.5 %shard_map.44 = (f32[64,1408]{1,0:T(8,128)S(1)}, bf16[2,64,128]{2,1,0:T(8,128)(2,1)S(1)}) custom-call(f32[128,128]{1,0:T(8,128)S(1)} %get-tuple-element.29.columns, bf16[768,384]{1,0:T(8,128)(2,1)S(1)} %get-tuple-element.30.taps, bf16[16,16,128]{2,1,0:T(8,128)(2,1)S(1)} %get-tuple-element.31.refs_0_, ...), custom_call_target="tpu_custom_call" | custom-call | flops 415236096 | bytes 21626880 | tf_op jit(solution)/shard_map/pallas_call | solution.py:475
  19.4 0.0 collective-permute-done.6.refs_5_
  19.4 1.6 %collective-permute-done.7.refs_6_ = bf16[5,32,128]{2,1,0:T(8,128)(2,1)S(1)} collective-permute-done((bf16[5,32,128]{2,1,0:T(8,128)(2,1)S(1)}, bf16[5,32,128]{2,1,0:T(8,128)(2,1)S(1)}, u32[]{:S(2)}, u32[]{:S(2)}) %collective-permute-start.7) | collective-permute-done | bytes 40992 | tf_op jit(solution)/shard_map/ppermute | solution.py:36
  21.0 1.6 %shard_map.45 = f32[64,2048]{1,0:T(8,128)} custom-call(f32[128,128]{1,0:T(8,128)S(1)} %get-tuple-element.29.columns, bf16[768,384]{1,0:T(8,128)(2,1)S(1)} %get-tuple-element.30.taps, bf16[16,16,128]{2,1,0:T(8,128)(2,1)S(1)} %get-tuple-element.31.refs_0_, bf16[16,16,128]{2,1,0:T(8,128)(2,1)S(1)} %collective-permute-done.3.refs_1_, ...), custom_call_target="tpu_custom_call" | custom-call | flops 188743680 | bytes 9830400 | tf_op jit(solution)/shard_map/pallas_call | solution.py:475
  (9 shorter events, 0.0 us)
Async XLA Ops:
  0.0 1.8 %collective-permute-start = (bf16[64,2048]{1,0:T(8,128)(2,1)}, bf16[64,2048]{1,0:T(8,128)(2,1)S(1)}, u32[]{:S(2)}, u32[]{:S(2)}) collective-permute-start(bf16[64,2048]{1,0:T(8,128)(2,1)} %whole.1), channel_id=1, source_target_pairs={{0,1},{1,0},{2,3},{3,2},{4,5},{5,4},{6,7},{7,6},{8,9},{9,8},{10,11... | collective-permute-start | bytes 786440 | tf_op jit(solution)/shard_map/ppermute | solution.py:41
  0.5 0.9 %copy-start = (bf16[64,2048]{1,0:T(8,128)(2,1)S(1)}, bf16[64,2048]{1,0:T(8,128)(2,1)}, u32[]{:S(2)}) copy-start(bf16[64,2048]{1,0:T(8,128)(2,1)} %whole.1) | copy-start | bytes 786436
  1.4 3.3 %copy-start.1 = (s32[9,512]{1,0:T(8,128)S(1)}, s32[9,512]{1,0:T(8,128)}, u32[]{:S(2)}) copy-start(s32[9,512]{1,0:T(8,128)} %shifts) | copy-start | bytes 55300
  1.8 5.7 %collective-permute-start.1 = (bf16[128,128]{1,0:T(8,128)(2,1)S(1)}, bf16[128,128]{1,0:T(8,128)(2,1)S(1)}, u32[]{:S(2)}, u32[]{:S(2)}) collective-permute-start(bf16[128,128]{1,0:T(8,128)(2,1)S(1)} %shard_map.38), channel_id=1, source_target_pairs={{2,0},{0,2},{3,1},{1,3},{6,4},{4,6},{7,5},{5,7},{10,8},{8,10},{11,... | collective-permute-start | bytes 98312 | tf_op jit(solution)/shard_map/ppermute | solution.py:36
  8.2 6.8 %collective-permute-start.3 = (bf16[16,16,128]{2,1,0:T(8,128)(2,1)S(1)}, bf16[16,16,128]{2,1,0:T(8,128)(2,1)S(1)}, u32[]{:S(2)}, u32[]{:S(2)}) collective-permute-start(bf16[16,16,128]{2,1,0:T(8,128)(2,1)S(1)} %get-tuple-element.32), channel_id=1, source_target_pairs={{0,12},{1,9},{4,8},{5,13},{8,4},{9,1},{12,0},{13,5},{2,14},{3,11},... | collective-permute-start | bytes 196616 | tf_op jit(solution)/shard_map/ppermute | solution.py:64
  11.8 5.1 %collective-permute-start.2 = (bf16[16,16,128]{2,1,0:T(8,128)(2,1)S(1)}, bf16[16,16,128]{2,1,0:T(8,128)(2,1)S(1)}, u32[]{:S(2)}, u32[]{:S(2)}) collective-permute-start(bf16[16,16,128]{2,1,0:T(8,128)(2,1)S(1)} %get-tuple-element.28), channel_id=1, source_target_pairs={{0,4},{1,13},{4,0},{5,9},{8,12},{9,5},{12,8},{13,1},{2,6},{3,15},{... | collective-permute-start | bytes 196616 | tf_op jit(solution)/shard_map/ppermute | solution.py:64
  11.8 5.1 %collective-permute-start.4 = (bf16[9,16,128]{2,1,0:T(8,128)(2,1)S(1)}, bf16[9,16,128]{2,1,0:T(8,128)(2,1)S(1)}, u32[]{:S(2)}, u32[]{:S(2)}) collective-permute-start(bf16[9,16,128]{2,1,0:T(8,128)(2,1)S(1)} %slice.6), channel_id=1, source_target_pairs={{0,8},{1,5},{4,12},{5,1},{8,0},{9,13},{12,4},{13,9},{2,10},{3,7},{... | collective-permute-start | bytes 110600 | tf_op jit(solution)/shard_map/ppermute | solution.py:64
  12.6 2.2 %copy-start.2 = (bf16[6,256]{1,0:T(8,128)(2,1)S(1)}, bf16[6,256]{1,0:T(8,128)(2,1)}, u32[]{:S(2)}) copy-start(bf16[6,256]{1,0:T(8,128)(2,1)} %filters) | copy-start | bytes 9220
  12.6 5.2 %collective-permute-start.5 = (bf16[7,16,128]{2,1,0:T(8,128)(2,1)S(1)}, bf16[7,16,128]{2,1,0:T(8,128)(2,1)S(1)}, u32[]{:S(2)}, u32[]{:S(2)}) collective-permute-start(bf16[7,16,128]{2,1,0:T(8,128)(2,1)S(1)} %slice.7), channel_id=1, source_target_pairs={{0,8},{1,5},{4,12},{5,1},{8,0},{9,13},{12,4},{13,9},{2,10},{3,7},{... | collective-permute-start | bytes 86024 | tf_op jit(solution)/shard_map/ppermute | solution.py:64
  15.0 4.3 %collective-permute-start.6 = (bf16[5,32,128]{2,1,0:T(8,128)(2,1)S(1)}, bf16[5,32,128]{2,1,0:T(8,128)(2,1)S(1)}, u32[]{:S(2)}, u32[]{:S(2)}) collective-permute-start(bf16[5,32,128]{2,1,0:T(8,128)(2,1)S(1)} %shard_map.42), channel_id=1, source_target_pairs={{2,0},{0,2},{3,1},{1,3},{6,4},{4,6},{7,5},{5,7},{10,8},{8,10},{11,... | collective-permute-start | bytes 122888 | tf_op jit(solution)/shard_map/ppermute | solution.py:36
  16.9 4.1 %collective-permute-start.7 = (bf16[5,32,128]{2,1,0:T(8,128)(2,1)S(1)}, bf16[5,32,128]{2,1,0:T(8,128)(2,1)S(1)}, u32[]{:S(2)}, u32[]{:S(2)}) collective-permute-start(bf16[5,32,128]{2,1,0:T(8,128)(2,1)S(1)} %shard_map.43), channel_id=1, source_target_pairs={{2,0},{0,2},{3,1},{1,3},{6,4},{4,6},{7,5},{5,7},{10,8},{8,10},{11,... | collective-permute-start | bytes 122888 | tf_op jit(solution)/shard_map/ppermute | solution.py:36

commit v14 on v12

--- a/solution.py
+++ b/solution.py
@@ -43,7 +43,7 @@
 
 def mask_orders(group_count):
     far = list(range(group_count - 1, 1, -1))
-    return [*far[:-1], 1, *far[-1:]], [*far[-1:], *far[:-1], 1]
+    return [1, *far], [*far[-1:], *far[:-1], 1]
 
 
 def step_masks(group_count, core):

time: 22.6 us -> 23.3 us (1.031)
  starting transfers between devices: 12.2 us -> 12.8 us
    ppermute x4, starting transfers between devices: 6.59 us -> 7.04 us  [exchanged(): lax.ppermute(blocks[step][first:end], ('freq', 'sub'), route)]
  transfers between devices with their start and end apart: 8 -> 8, of which waited for: 4 -> 3; matrix products, arithmetic and copies ran while one was open for 0% -> 0% of each run, Pallas kernels for 20% -> 19%
where the time goes in v14:
time: 23.3 us; the launch traced here: 23.2 us
  starting transfers between devices  12.8 us (55%)
  Pallas kernels  6.69 us (29%)
  waiting for transfers between devices  2.62 us (11%)
  local copies, waits for them, and re-layouts  0.97 us (4%)
    ppermute x4, starting transfers between devices, exchanged(): lax.ppermute(blocks[step][first:end], ('freq', 'sub'), route)  7.04 us
    ppermute x3, starting transfers between devices, from_ahead(): lax.ppermute(value, 'tm', [((block + steps) % count, block) for block in...  5.32 us
    pallas_call x2, Pallas kernels, within_chip(): pl.pallas_call(functools.partial(chip_kernel, spans, out_tiles, group_cou...  3.38 us
    pallas_call x2, Pallas kernels, between_chips(): pl.pallas_call(functools.partial(trial_kernel, plan, group_count, level_c...  3.05 us
    ppermute x4, waiting for transfers between devices, exchanged(): lax.ppermute(blocks[step][first:end], ('freq', 'sub'), route)  1.12 us
    ppermute x3, waiting for transfers between devices, from_ahead(): lax.ppermute(value, 'tm', [((block + steps) % count, block) for block in...  1.11 us
    unnamed x6, local copies, waits for them, and re-layouts  0.96 us
  transfers between devices with their start and end apart: 8, of which 3 were waited for; matrix products, arithmetic and copies ran while one was open for 0% of the time, Pallas kernels for 19%

profile of v14, /device:TPU:0, one launch (start us, length us, event | category | flops | bytes accessed | tf_op | source)
XLA Modules:
  0.0 23.2 jit_solution(14023394374977007894)
XLA Ops:
  0.0 0.5 %collective-permute-start = (bf16[64,2048]{1,0:T(8,128)(2,1)}, bf16[64,2048]{1,0:T(8,128)(2,1)S(1)}, u32[]{:S(2)}, u32[]{:S(2)}) collective-permute-start(bf16[64,2048]{1,0:T(8,128)(2,1)} %whole.1), channel_id=1, source_target_pairs={{0,1},{1,0},{2,3},{3,2},{4,5},{5,4},{6,7},{7,6},{8,9},{9,8},{10,11... | collective-permute-start | bytes 786440 | tf_op jit(solution)/shard_map/ppermute | solution.py:41
  0.5 0.9 %copy-done = bf16[64,2048]{1,0:T(8,128)(2,1)S(1)} copy-done((bf16[64,2048]{1,0:T(8,128)(2,1)S(1)}, bf16[64,2048]{1,0:T(8,128)(2,1)}, u32[]{:S(2)}) %copy-start) | copy-done | bytes 262168
  1.4 0.0 copy-start.1
  1.4 0.4 %collective-permute-done.other.refs_1_ = bf16[64,2048]{1,0:T(8,128)(2,1)S(1)} collective-permute-done((bf16[64,2048]{1,0:T(8,128)(2,1)}, bf16[64,2048]{1,0:T(8,128)(2,1)S(1)}, u32[]{:S(2)}, u32[]{:S(2)}) %collective-permute-start) | collective-permute-done | bytes 262176 | tf_op jit(solution)/shard_map/ppermute | solution.py:41
  1.8 2.9 %collective-permute-start.1 = (bf16[128,128]{1,0:T(8,128)(2,1)S(1)}, bf16[128,128]{1,0:T(8,128)(2,1)S(1)}, u32[]{:S(2)}, u32[]{:S(2)}) collective-permute-start(bf16[128,128]{1,0:T(8,128)(2,1)S(1)} %shard_map.38), channel_id=1, source_target_pairs={{2,0},{0,2},{3,1},{1,3},{6,4},{4,6},{7,5},{5,7},{10,8},{8,10},{11,... | collective-permute-start | bytes 98312 | tf_op jit(solution)/shard_map/ppermute | solution.py:36
  4.8 0.0 copy-done.1
  4.8 2.8 %shard_map.39 = (f32[15,64,128]{2,1,0:T(8,128)S(1)}, f32[128,128]{1,0:T(8,128)S(1)}) custom-call(bf16[64,2048]{1,0:T(8,128)(2,1)S(1)} %shard_map.37.whole.refs_0_, bf16[64,2048]{1,0:T(8,128)(2,1)S(1)} %collective-permute-done.other.refs_1_, s32[9,512]{1,0:T(8,128)S(1)} %copy-done.1), custom_call_target="tpu_custom_call" | custom-call | tf_op jit(solution)/shard_map/pallas_call | solution.py:450
  7.5 0.0 collective-permute-done.1.refs_2_
  7.5 0.6 %shard_map.40 = (bf16[16,16,128]{2,1,0:T(8,128)(2,1)S(1)}, bf16[16,16,128]{2,1,0:T(8,128)(2,1)S(1)}, bf16[16,16,128]{2,1,0:T(8,128)(2,1)S(1)}, bf16[16,16,128]{2,1,0:T(8,128)(2,1)S(1)}) custom-call(bf16[64,2048]{1,0:T(8,128)(2,1)S(1)} %shard_map.37.whole.refs_0_, bf16[64,2048]{1,0:T(8,128)(2,1)S(1)} %collective-permute-done.other.refs_1_, ...), custom_call_target="tpu_custom_call" | custom-call | tf_op jit(solution)/shard_map/pallas_call | solution.py:450
  8.2 1.6 %collective-permute-start.3 = (bf16[16,16,128]{2,1,0:T(8,128)(2,1)S(1)}, bf16[16,16,128]{2,1,0:T(8,128)(2,1)S(1)}, u32[]{:S(2)}, u32[]{:S(2)}) collective-permute-start(bf16[16,16,128]{2,1,0:T(8,128)(2,1)S(1)} %get-tuple-element.32), channel_id=1, source_target_pairs={{0,4},{1,9},{4,0},{5,13},{8,12},{9,1},{12,8},{13,5},{2,6},{3,11},{... | collective-permute-start | bytes 196616 | tf_op jit(solution)/shard_map/ppermute | solution.py:64
  9.8 2.5 %collective-permute-start.4 = (bf16[16,16,128]{2,1,0:T(8,128)(2,1)S(1)}, bf16[16,16,128]{2,1,0:T(8,128)(2,1)S(1)}, u32[]{:S(2)}, u32[]{:S(2)}) collective-permute-start(bf16[16,16,128]{2,1,0:T(8,128)(2,1)S(1)} %get-tuple-element.33), channel_id=1, source_target_pairs={{0,12},{1,13},{4,8},{5,9},{8,4},{9,5},{12,0},{13,1},{2,14},{3,15},... | collective-permute-start | bytes 196616 | tf_op jit(solution)/shard_map/ppermute | solution.py:64
  12.3 0.1 collective-permute-start.5
  12.4 2.8 %collective-permute-start.2 = (bf16[7,16,128]{2,1,0:T(8,128)(2,1)S(1)}, bf16[7,16,128]{2,1,0:T(8,128)(2,1)S(1)}, u32[]{:S(2)}, u32[]{:S(2)}) collective-permute-start(bf16[7,16,128]{2,1,0:T(8,128)(2,1)S(1)} %slice.6), channel_id=1, source_target_pairs={{0,8},{1,5},{4,12},{5,1},{8,0},{9,13},{12,4},{13,9},{2,10},{3,7},{... | collective-permute-start | bytes 86024 | tf_op jit(solution)/shard_map/ppermute | solution.py:64
  15.2 0.0 collective-permute-done.3.refs_1_
  15.2 1.2 %collective-permute-start.6 = (bf16[5,32,128]{2,1,0:T(8,128)(2,1)S(1)}, bf16[5,32,128]{2,1,0:T(8,128)(2,1)S(1)}, u32[]{:S(2)}, u32[]{:S(2)}) collective-permute-start(bf16[5,32,128]{2,1,0:T(8,128)(2,1)S(1)} %shard_map.42), channel_id=1, source_target_pairs={{2,0},{0,2},{3,1},{1,3},{6,4},{4,6},{7,5},{5,7},{10,8},{8,10},{11,... | collective-permute-start | bytes 122888 | tf_op jit(solution)/shard_map/ppermute | solution.py:36
  16.4 1.1 %collective-permute-done.5.refs_1_.refs_3_ = bf16[9,16,128]{2,1,0:T(8,128)(2,1)S(1)} collective-permute-done((bf16[9,16,128]{2,1,0:T(8,128)(2,1)S(1)}, bf16[9,16,128]{2,1,0:T(8,128)(2,1)S(1)}, u32[]{:S(2)}, u32[]{:S(2)}) %collective-permute-start.5) | collective-permute-done | bytes 36896 | tf_op jit(solution)/shard_map/ppermute | solution.py:64
  17.5 0.0 collective-permute-done.4.refs_0_.refs_2_
  17.6 1.2 %collective-permute-start.7 = (bf16[5,32,128]{2,1,0:T(8,128)(2,1)S(1)}, bf16[5,32,128]{2,1,0:T(8,128)(2,1)S(1)}, u32[]{:S(2)}, u32[]{:S(2)}) collective-permute-start(bf16[5,32,128]{2,1,0:T(8,128)(2,1)S(1)} %shard_map.43), channel_id=1, source_target_pairs={{2,0},{0,2},{3,1},{1,3},{6,4},{4,6},{7,5},{5,7},{10,8},{8,10},{11,... | collective-permute-start | bytes 122888 | tf_op jit(solution)/shard_map/ppermute | solution.py:36
  18.7 0.2 shard_map.41
  19.0 0.0 collective-permute-done.2.refs_4_
  19.0 1.5 %shard_map.44 = (f32[64,1408]{1,0:T(8,128)S(1)}, bf16[2,64,128]{2,1,0:T(8,128)(2,1)S(1)}) custom-call(f32[128,128]{1,0:T(8,128)S(1)} %get-tuple-element.29.columns, bf16[768,384]{1,0:T(8,128)(2,1)S(1)} %get-tuple-element.30.taps, bf16[16,16,128]{2,1,0:T(8,128)(2,1)S(1)} %get-tuple-element.31.refs_0_, ...), custom_call_target="tpu_custom_call" | custom-call | flops 415236096 | bytes 21626880 | tf_op jit(solution)/shard_map/pallas_call | solution.py:475
  20.5 0.0 collective-permute-done.6.refs_5_
  20.5 1.1 %collective-permute-done.7.refs_6_ = bf16[5,32,128]{2,1,0:T(8,128)(2,1)S(1)} collective-permute-done((bf16[5,32,128]{2,1,0:T(8,128)(2,1)S(1)}, bf16[5,32,128]{2,1,0:T(8,128)(2,1)S(1)}, u32[]{:S(2)}, u32[]{:S(2)}) %collective-permute-start.7) | collective-permute-done | bytes 40992 | tf_op jit(solution)/shard_map/ppermute | solution.py:36
  21.6 1.6 %shard_map.45 = f32[64,2048]{1,0:T(8,128)} custom-call(f32[128,128]{1,0:T(8,128)S(1)} %get-tuple-element.29.columns, bf16[768,384]{1,0:T(8,128)(2,1)S(1)} %get-tuple-element.30.taps, bf16[16,16,128]{2,1,0:T(8,128)(2,1)S(1)} %get-tuple-element.31.refs_0_, bf16[16,16,128]{2,1,0:T(8,128)(2,1)S(1)} %collective-permute-done.3.refs_1_, ...), custom_call_target="tpu_custom_call" | custom-call | flops 188743680 | bytes 9830400 | tf_op jit(solution)/shard_map/pallas_call | solution.py:475
  (9 shorter events, 0.0 us)
Async XLA Ops:
  0.0 1.8 %collective-permute-start = (bf16[64,2048]{1,0:T(8,128)(2,1)}, bf16[64,2048]{1,0:T(8,128)(2,1)S(1)}, u32[]{:S(2)}, u32[]{:S(2)}) collective-permute-start(bf16[64,2048]{1,0:T(8,128)(2,1)} %whole.1), channel_id=1, source_target_pairs={{0,1},{1,0},{2,3},{3,2},{4,5},{5,4},{6,7},{7,6},{8,9},{9,8},{10,11... | collective-permute-start | bytes 786440 | tf_op jit(solution)/shard_map/ppermute | solution.py:41
  0.5 0.9 %copy-start = (bf16[64,2048]{1,0:T(8,128)(2,1)S(1)}, bf16[64,2048]{1,0:T(8,128)(2,1)}, u32[]{:S(2)}) copy-start(bf16[64,2048]{1,0:T(8,128)(2,1)} %whole.1) | copy-start | bytes 786436
  1.4 3.3 %copy-start.1 = (s32[9,512]{1,0:T(8,128)S(1)}, s32[9,512]{1,0:T(8,128)}, u32[]{:S(2)}) copy-start(s32[9,512]{1,0:T(8,128)} %shifts) | copy-start | bytes 55300
  1.8 5.7 %collective-permute-start.1 = (bf16[128,128]{1,0:T(8,128)(2,1)S(1)}, bf16[128,128]{1,0:T(8,128)(2,1)S(1)}, u32[]{:S(2)}, u32[]{:S(2)}) collective-permute-start(bf16[128,128]{1,0:T(8,128)(2,1)S(1)} %shard_map.38), channel_id=1, source_target_pairs={{2,0},{0,2},{3,1},{1,3},{6,4},{4,6},{7,5},{5,7},{10,8},{8,10},{11,... | collective-permute-start | bytes 98312 | tf_op jit(solution)/shard_map/ppermute | solution.py:36
  8.2 7.1 %collective-permute-start.3 = (bf16[16,16,128]{2,1,0:T(8,128)(2,1)S(1)}, bf16[16,16,128]{2,1,0:T(8,128)(2,1)S(1)}, u32[]{:S(2)}, u32[]{:S(2)}) collective-permute-start(bf16[16,16,128]{2,1,0:T(8,128)(2,1)S(1)} %get-tuple-element.32), channel_id=1, source_target_pairs={{0,4},{1,9},{4,0},{5,13},{8,12},{9,1},{12,8},{13,5},{2,6},{3,11},{... | collective-permute-start | bytes 196616 | tf_op jit(solution)/shard_map/ppermute | solution.py:64
  9.8 7.7 %collective-permute-start.4 = (bf16[16,16,128]{2,1,0:T(8,128)(2,1)S(1)}, bf16[16,16,128]{2,1,0:T(8,128)(2,1)S(1)}, u32[]{:S(2)}, u32[]{:S(2)}) collective-permute-start(bf16[16,16,128]{2,1,0:T(8,128)(2,1)S(1)} %get-tuple-element.33), channel_id=1, source_target_pairs={{0,12},{1,13},{4,8},{5,9},{8,4},{9,5},{12,0},{13,1},{2,14},{3,15},... | collective-permute-start | bytes 196616 | tf_op jit(solution)/shard_map/ppermute | solution.py:64
  12.3 5.3 %collective-permute-start.5 = (bf16[9,16,128]{2,1,0:T(8,128)(2,1)S(1)}, bf16[9,16,128]{2,1,0:T(8,128)(2,1)S(1)}, u32[]{:S(2)}, u32[]{:S(2)}) collective-permute-start(bf16[9,16,128]{2,1,0:T(8,128)(2,1)S(1)} %slice.7), channel_id=1, source_target_pairs={{0,8},{1,5},{4,12},{5,1},{8,0},{9,13},{12,4},{13,9},{2,10},{3,7},{... | collective-permute-start | bytes 110600 | tf_op jit(solution)/shard_map/ppermute | solution.py:64
  12.4 6.6 %collective-permute-start.2 = (bf16[7,16,128]{2,1,0:T(8,128)(2,1)S(1)}, bf16[7,16,128]{2,1,0:T(8,128)(2,1)S(1)}, u32[]{:S(2)}, u32[]{:S(2)}) collective-permute-start(bf16[7,16,128]{2,1,0:T(8,128)(2,1)S(1)} %slice.6), channel_id=1, source_target_pairs={{0,8},{1,5},{4,12},{5,1},{8,0},{9,13},{12,4},{13,9},{2,10},{3,7},{... | collective-permute-start | bytes 86024 | tf_op jit(solution)/shard_map/ppermute | solution.py:64
  15.2 3.5 %copy-start.2 = (bf16[6,256]{1,0:T(8,128)(2,1)S(1)}, bf16[6,256]{1,0:T(8,128)(2,1)}, u32[]{:S(2)}) copy-start(bf16[6,256]{1,0:T(8,128)(2,1)} %filters) | copy-start | bytes 9220
  15.2 5.3 %collective-permute-start.6 = (bf16[5,32,128]{2,1,0:T(8,128)(2,1)S(1)}, bf16[5,32,128]{2,1,0:T(8,128)(2,1)S(1)}, u32[]{:S(2)}, u32[]{:S(2)}) collective-permute-start(bf16[5,32,128]{2,1,0:T(8,128)(2,1)S(1)} %shard_map.42), channel_id=1, source_target_pairs={{2,0},{0,2},{3,1},{1,3},{6,4},{4,6},{7,5},{5,7},{10,8},{8,10},{11,... | collective-permute-start | bytes 122888 | tf_op jit(solution)/shard_map/ppermute | solution.py:36
  17.6 4.1 %collective-permute-start.7 = (bf16[5,32,128]{2,1,0:T(8,128)(2,1)S(1)}, bf16[5,32,128]{2,1,0:T(8,128)(2,1)S(1)}, u32[]{:S(2)}, u32[]{:S(2)}) collective-permute-start(bf16[5,32,128]{2,1,0:T(8,128)(2,1)S(1)} %shard_map.43), channel_id=1, source_target_pairs={{2,0},{0,2},{3,1},{1,3},{6,4},{4,6},{7,5},{5,7},{10,8},{8,10},{11,... | collective-permute-start | bytes 122888 | tf_op jit(solution)/shard_map/ppermute | solution.py:36
